TPU v7x, 256 devices: a whole 4x4x8 slice. The times are simulated.
256 devices in a mesh: samp: 64 (over x, y, z_lo), strip: 4 (over z_hi, core).
Axes of the slice: x: 4, y: 4, z: 8 (z_hi: 2, z_lo: 4; z = z_hi * 4 + z_lo), core: 2. Of those that a mesh axis runs over, the one named last changes fastest.
Arguments:
- initial_state: float32 [256, 4096], P('strip'), may hold values from -6 to 6
- target: float32 [256, 4096], P('strip'), may hold values from -6 to 6
- control: float32 [256, 4096], P('strip'), may hold values from -6 to 6
- point_index: int32 [64], P('samp'), may hold values from 0 to 65535
- generator: int32 [32, 32], replicated, may hold values from 1 to 65535
Outputs:
- new_control: float32 [256, 4096], P('strip')
- final_state: float32 [64, 256, 4096], P('samp', 'strip')
All inputs are finite; a program needn't handle non-finite values.
Results may differ from a plain program's by a relative error of at most 0.0003.
Values sent between devices are 32-bit elements; how exact they have to be, the bound alone decides.
No kernel may reach another device: no remote copies, remote signals or barrier semaphores. Data moves between devices by JAX's collectives and lax.ppermute only.
A program may use at most 64 MiB of HBM per device.

v0:
```python
import jax
import jax.numpy as jnp
from jax import lax
from jax.sharding import PartitionSpec as P

STEPS = 3


TWO_PI = 6.283185307179586
DT = 0.12
REG = 0.1
RATE = 1.0


def with_halo(value, sides, width):
    for axis, dim in sides:
        peers, length = (lax.axis_size(axis), value.shape[dim])
        up = [(i, (i + 1) % peers) for i in range(peers)]
        down = [(j, i) for i, j in up]
        last = lax.slice_in_dim(value, length - width, length, axis=dim)
        first = lax.slice_in_dim(value, 0, width, axis=dim)
        before = lax.ppermute(last, axis, up)
        after = lax.ppermute(first, axis, down)
        value = jnp.concatenate([before, value, after], axis=dim)
    return value


def mode_weights(modes):
    ranks = jnp.arange(1, modes + 1, dtype=jnp.float32)
    harmonic = jnp.sum(1.0 / ranks)
    return 4.0 / harmonic / jnp.sqrt(ranks[:, None] * ranks[None, :])


def sine_table(places, modes, period):
    freq = jnp.arange(1, modes + 1, dtype=jnp.int32)
    turns = freq[:, None] * places[None, :] % period
    return jnp.sin(TWO_PI * turns.astype(jnp.float32) / period)


def diffuse(coef, field):
    middle = field[..., 1:-1, :]
    center = coef[..., 1:-1, :]
    total = 0.5 * (center + coef[..., :-2, :]) * (field[..., :-2, :] - middle)
    total = total + 0.5 * (center + coef[..., 2:, :]) * (field[..., 2:, :] - middle)
    total = total + 0.5 * (center + jnp.roll(center, 1, -1)) * (jnp.roll(middle, 1, -1) - middle)
    total = total + 0.5 * (center + jnp.roll(center, -1, -1)) * (jnp.roll(middle, -1, -1) - middle)
    return total


def on_device(initial_state, target, control, point_index, generator):
    rows = initial_state.shape[0]
    width = initial_state.shape[1]
    modes = generator.shape[0]
    samples_dev = point_index.shape[0]
    grid_rows = rows * lax.axis_size("strip")
    count = samples_dev * lax.axis_size("samp")
    first_row = lax.axis_index("strip") * rows
    cells = point_index[:, None, None] * generator[None, :, :] % 65536
    coeff = (cells.astype(jnp.float32) / 65536.0 - 0.5) * mode_weights(modes)[None]
    col_table = sine_table(jnp.arange(width, dtype=jnp.int32), modes, width)
    inner = jnp.einsum(
        "smn,nj->smj",
        coeff,
        col_table,
        precision=lax.Precision.HIGHEST,
        preferred_element_type=jnp.float32,
    )
    places = (first_row - 1 + jnp.arange(rows + 2 * 1, dtype=jnp.int32)) % grid_rows
    table = sine_table(places, modes, grid_rows)
    field_log = jnp.einsum(
        "mi,smj->sij",
        table,
        inner,
        precision=lax.Precision.HIGHEST,
        preferred_element_type=jnp.float32,
    )
    coef = 1.0 + 0.8 * jnp.tanh(field_log)
    state = initial_state[None]
    for step in range(STEPS):
        outer = with_halo(state, (("strip", 1),), 1)
        state = state + DT * (diffuse(coef, outer) + control[None])
    lam = state - target[None]
    summed = lam
    for step in range(STEPS - 1):
        outer = with_halo(lam, (("strip", 1),), 1)
        lam = lam + DT * diffuse(coef, outer)
        summed = summed + lam
    partial_grad = jnp.sum(DT * summed, axis=0)
    summed_all = lax.psum(partial_grad, "samp")
    new_control = control - RATE * (summed_all / count + REG * control)
    return (new_control, state)


def solution(mesh):
    placed = (P("strip", None), P("strip", None), P("strip", None), P("samp"), P())
    return jax.shard_map(
        on_device,
        mesh=mesh,
        in_specs=placed,
        out_specs=(P("strip", None), P("samp", "strip", None)),
        check_vma=False,
    )
```

profile of v0, /device:TPU:8, one launch (start us, length us, event | category | flops | bytes accessed | tf_op | source)
XLA Modules:
  0.0 784.0 jit_solution(1363104328624644954)
XLA Ops:
  7.2 0.0 all-reduce.2.cloned.1.call-start
  7.2 1.0 fusion.153
  8.2 0.1 collective-permute-start
  8.3 6.7 collective-permute-start.1
  15.0 0.6 divide_reduce_fusion
  15.6 0.8 slice_bitcast_fusion.2
  16.5 0.0 copy-start.3
  16.5 1.9 slice_bitcast_fusion
  19.7 0.0 copy-done.3
  19.8 2.6 fusion.74
  22.3 1.3 fusion.2
  23.6 0.0 copy-start
  23.6 0.0 copy-start.1
  23.7 0.4 fusion.140
  24.0 0.1 fusion.139
  24.1 0.0 collective-permute-done
  24.1 0.0 collective-permute-done.1
  24.1 0.7 copy-done
  24.9 0.3 copy-done.1
  25.2 1.9 fusion.51
  27.1 0.3 fusion.150
  27.4 0.7 collective-permute-start.2
  28.1 5.1 collective-permute-start.3
  33.2 0.1 fusion.151
  33.2 1.4 collective-permute-done.2
  34.6 0.0 collective-permute-done.3
  34.6 1.0 fusion.41
  35.6 0.0 copy-start.2
  35.6 0.3 fusion.149
  36.0 6.3 collective-permute-start.4
  42.2 0.0 collective-permute-start.5
  42.3 0.1 fusion.148
  42.3 1.1 collective-permute-done.4
  43.4 0.2 collective-permute-done.5
  43.7 0.0 copy-done.2
  43.7 2.0 bitcast_subtract_fusion
  45.7 0.3 fusion.144
  46.1 6.0 collective-permute-start.6
  52.0 0.0 collective-permute-start.7
  52.0 0.1 fusion.145
  52.1 1.1 collective-permute-done.6
  53.3 0.2 collective-permute-done.7
  53.5 0.9 fusion.21
  54.4 0.3 fusion.141
  54.7 5.8 collective-permute-start.8
  60.5 0.0 collective-permute-start.9
  60.5 0.1 fusion.142
  60.6 1.3 collective-permute-done.8
  61.9 0.1 collective-permute-done.9
  62.0 2.0 fusion.12
  64.0 0.0 all-reduce.2.cloned.1.call-update
  64.0 710.8 %all-reduce.2.cloned.1.call-done = f32[64,4096]{1,0:T(8,128)} async-done(((f32[64,4096]{1,0:T(8,128)}), f32[64,4096]{1,0:T(8,128)}) %all-reduce.2.cloned.1.call-update) | async-done | bytes 1048592 | tf_op jit(solution)/shard_map/psum | solution.py:89
  774.8 2.3 add_subtract_fusion
  (7 shorter events, 0.1 us)
Async XLA Ops:
  7.2 767.7 %all-reduce.2.cloned.1.call-start = ((), (), s32[]{:S(2)}) async-start(), calls=%async_computation | async-start | bytes 2097152 | tf_op jit(solution)/shard_map/psum | solution.py:89
  8.2 15.9 %collective-permute-start = (f32[1,1,4096]{2,1,0:T(1,128)S(1)}, f32[1,1,4096]{2,1,0:T(1,128)S(1)}, u32[]{:S(2)}, u32[]{:S(2)}) collective-permute-start(f32[1,1,4096]{2,1,0:T(1,128)S(1)} %get-tuple-element.41), channel_id=1, source_target_pairs={{0,1},{1,2},{2,3},{3,0},{4,5},{5,6},{6,7},{7,4},{8,9},{9,10},{10,1... | collective-permute-start | bytes 49160 | tf_op jit(solution)/shard_map/ppermute | solution.py:22
  8.3 15.8 %collective-permute-start.1 = (f32[1,1,4096]{2,1,0:T(1,128)S(1)}, f32[1,1,4096]{2,1,0:T(1,128)S(1)}, u32[]{:S(2)}, u32[]{:S(2)}) collective-permute-start(f32[1,1,4096]{2,1,0:T(1,128)S(1)} %get-tuple-element.42), channel_id=1, source_target_pairs={{1,0},{2,1},{3,2},{0,3},{5,4},{6,5},{7,6},{4,7},{9,8},{10,9},{11,1... | collective-permute-start | bytes 49160 | tf_op jit(solution)/shard_map/ppermute | solution.py:23
  16.5 3.3 copy-start.3
  23.6 1.2 copy-start
  23.6 1.5 copy-start.1
  27.4 7.2 collective-permute-start.2
  28.1 6.5 collective-permute-start.3
  35.6 8.1 %copy-start.2 = (f32[64,4096]{1,0:T(8,128)S(1)}, f32[64,4096]{1,0:T(8,128)}, u32[]{:S(2)}) copy-start(f32[64,4096]{1,0:T(8,128)} %param.6) | copy-start | bytes 3145732
  36.0 7.5 collective-permute-start.4
  42.2 1.4 collective-permute-start.5
  46.1 7.2 collective-permute-start.6
  52.0 1.4 collective-permute-start.7
  54.7 7.1 collective-permute-start.8
  60.5 1.4 collective-permute-start.9
Sparse Core Ops, SparseCore 0:
  64.1 710.6 all-reduce.1
where the time goes:
time: 787 us; the launch traced here: 784 us
  waiting for transfers between devices  716 us (91%)
  starting transfers between devices  30.6 us (4%)
  between operations  15.5 us (2%)
  other arithmetic  10.6 us (1%)
    psum x1, waiting for transfers between devices, on_device(): summed_all = lax.psum(partial_grad, 'samp')  711 us
    ppermute x5, starting transfers between devices, with_halo(): before = lax.ppermute(last, axis, up)  18.8 us
  transfers between devices with their start and end apart: 11, of which 8 were waited for; matrix products, arithmetic and copies ran while one was open for 1% of the time, Pallas kernels for 0%

commit v1 on v0

v1 whole, which is shorter than its diff:
```python
import jax
import jax.numpy as jnp
import numpy as np
from jax import lax
from jax.sharding import PartitionSpec as P

STEPS = 3
TWO_PI = 6.283185307179586
DT = 0.12
REG = 0.1
RATE = 1.0
HALO = 2 * STEPS - 1

SAMP = np.arange(64).reshape(4, 4, 4)
ALONG_Z = SAMP.reshape(16, 4).tolist()
ALONG_XY = SAMP.transpose(2, 0, 1).reshape(4, 16).tolist()


def mode_weights(modes):
    ranks = jnp.arange(1, modes + 1, dtype=jnp.float32)
    harmonic = jnp.sum(1.0 / ranks)
    return 4.0 / harmonic / jnp.sqrt(ranks[:, None] * ranks[None, :])


def sine_table(places, modes, period):
    freq = jnp.arange(1, modes + 1, dtype=jnp.int32)
    turns = freq[:, None] * places[None, :] % period
    return jnp.sin(TWO_PI * turns.astype(jnp.float32) / period)


def diffuse(coef, field):
    middle = field[1:-1]
    center = coef[1:-1]
    total = 0.5 * (center + coef[:-2]) * (field[:-2] - middle)
    total = total + 0.5 * (center + coef[2:]) * (field[2:] - middle)
    total = total + 0.5 * (center + jnp.roll(center, 1, -1)) * (jnp.roll(middle, 1, -1) - middle)
    total = total + 0.5 * (center + jnp.roll(center, -1, -1)) * (jnp.roll(middle, -1, -1) - middle)
    return total


def strip_shift(step):
    pairs = []
    for samp in range(64):
        for strip in range(4):
            to = (strip + step) % 4
            other = samp if to // 2 == strip // 2 else samp ^ 2
            pairs.append((samp * 4 + strip, other * 4 + to))
    return pairs


def on_device(initial_state, target, control, point_index, generator):
    rows, width = initial_state.shape
    modes = generator.shape[0]
    grid_rows = rows * lax.axis_size("strip")
    count = lax.axis_size("samp")
    h = HALO
    tail = jnp.concatenate([initial_state[-h:], control[-(h - 1):], target[-2:]], axis=0)
    head = jnp.concatenate([initial_state[:h], control[: h - 1], target[:2]], axis=0)
    before = lax.ppermute(tail, ("samp", "strip"), strip_shift(1))
    after = lax.ppermute(head, ("samp", "strip"), strip_shift(-1))

    first_row = lax.axis_index("strip") * rows
    cells = point_index[:, None] * generator % 65536
    coeff = (cells.astype(jnp.float32) / 65536.0 - 0.5) * mode_weights(modes)
    col_table = sine_table(jnp.arange(width, dtype=jnp.int32), modes, width)
    inner = jnp.dot(coeff, col_table, precision=lax.Precision.HIGHEST)
    places = (first_row - h + jnp.arange(rows + 2 * h, dtype=jnp.int32)) % grid_rows
    table = sine_table(places, modes, grid_rows)
    field_log = jnp.dot(table.T, inner, precision=lax.Precision.HIGHEST)
    coef = 1.0 + 0.8 * jnp.tanh(field_log)

    state = jnp.concatenate([before[:h], initial_state, after[:h]], axis=0)
    source = jnp.concatenate([before[h : 2 * h - 1], control, after[h : 2 * h - 1]], axis=0)
    wanted = jnp.concatenate([before[2 * h - 1 :], target, after[2 * h - 1 :]], axis=0)
    for step in range(STEPS):
        state = state[1:-1] + DT * (diffuse(coef, state) + source)
        coef, source = coef[1:-1], source[1:-1]
    lam = state - wanted
    state = state[2:-2]
    summed = lam[2:-2]
    for step in range(STEPS - 1):
        lam = lam[1:-1] + DT * diffuse(coef, lam)
        coef = coef[1:-1]
        trim = STEPS - 2 - step
        summed = summed + lam[trim : lam.shape[0] - trim]
    partial = DT * summed
    blocks = partial.reshape(8, 8, 8, 512).transpose(0, 2, 1, 3).reshape(16, 4, 8, 512)
    blocks = jnp.sum(lax.all_to_all(blocks, "samp", 0, 0, axis_index_groups=ALONG_XY, tiled=True), axis=0)
    blocks = jnp.sum(lax.all_to_all(blocks, "samp", 0, 0, axis_index_groups=ALONG_Z, tiled=True), axis=0)
    blocks = jnp.broadcast_to(blocks[None], (4, 8, 512))
    blocks = lax.all_to_all(blocks, "samp", 0, 0, axis_index_groups=ALONG_Z, tiled=True)
    blocks = jnp.broadcast_to(blocks[None], (16, 4, 8, 512))
    blocks = lax.all_to_all(blocks, "samp", 0, 0, axis_index_groups=ALONG_XY, tiled=True)
    total = blocks.reshape(8, 8, 8, 512).transpose(0, 2, 1, 3).reshape(rows, width)
    new_control = control - RATE * (total / count + REG * control)
    return (new_control, state[None])


def solution(mesh):
    placed = (P("strip", None), P("strip", None), P("strip", None), P("samp"), P())
    return jax.shard_map(
        on_device,
        mesh=mesh,
        in_specs=placed,
        out_specs=(P("strip", None), P("samp", "strip", None)),
        check_vma=False,
    )
```

time: 787 us -> 95.8 us (0.12)
  waiting for transfers between devices: 716 us -> 15.5 us
  blocking collectives: 0 us -> 39.5 us
  starting transfers between devices: 30.6 us -> 10.8 us
  between operations: 15.5 us -> 2.27 us
    psum x1 -> x0, waiting for transfers between devices: 711 us -> none  [on_device(): summed_all = lax.psum(partial_grad, 'samp')]
    all_to_all x0 -> x3, blocking collectives: none -> 39.5 us  [the longest x1 22.7 us: on_device(): lax.all_to_all(blocks, 'samp', 0, 0, axis_index_groups=ALONG_XY, tiled=True)]
    ppermute x10 -> x2, starting transfers between devices: 30.6 us -> 5.9 us  [the longest x1 5.82 us: on_device(): after = lax.ppermute(head, ('samp', 'strip'), strip_shift(-1))]
    all_to_all x0 -> x1, waiting for transfers between devices: none -> 11.8 us  [on_device(): lax.all_to_all(blocks, 'samp', 0, 0, axis_index_groups=ALONG_XY, tiled=True)]
  transfers between devices with their start and end apart: 11 -> 3, of which waited for: 8 -> 2; matrix products, arithmetic and copies ran while one was open for 1% -> 9% of each run, Pallas kernels for 0% -> 0%
where the time goes in v1:
time: 95.8 us; the launch traced here: 95.3 us
  blocking collectives  39.5 us (41%)
  waiting for transfers between devices  15.5 us (16%)
  other arithmetic  11.9 us (12%)
  local copies, waits for them, and re-layouts  11.4 us (12%)
  starting transfers between devices  10.8 us (11%)
  matrix products  3.97 us (4%)
  between operations  2.27 us (2%)
    all_to_all x1, blocking collectives, on_device(): lax.all_to_all(blocks, 'samp', 0, 0, axis_index_groups=ALONG_XY, tiled=True)  22.7 us
    all_to_all x2, blocking collectives, on_device(): lax.all_to_all(blocks, 'samp', 0, 0, axis_index_groups=ALONG_Z, tiled=True)  16.9 us
    all_to_all x1, waiting for transfers between devices, on_device(): lax.all_to_all(blocks, 'samp', 0, 0, axis_index_groups=ALONG_XY, tiled=True)  11.8 us
    ppermute x1, starting transfers between devices, on_device(): after = lax.ppermute(head, ('samp', 'strip'), strip_shift(-1))  5.82 us
    all_to_all x1, starting transfers between devices, on_device(): lax.all_to_all(blocks, 'samp', 0, 0, axis_index_groups=ALONG_XY, tiled=True)  4.9 us
    add x2, other arithmetic, on_device(): state = state[1:-1] + DT * (diffuse(coef, state) + source)  4.54 us
    ppermute x1, waiting for transfers between devices, on_device(): after = lax.ppermute(head, ('samp', 'strip'), strip_shift(-1))  3.68 us
    dot_general x1, matrix products, on_device(): inner = jnp.dot(coeff, col_table, precision=lax.Precision.HIGHEST)  2.56 us
  transfers between devices with their start and end apart: 3, of which 2 were waited for; matrix products, arithmetic and copies ran while one was open for 9% of the time, Pallas kernels for 0%

profile of v1, /device:TPU:8, one launch (start us, length us, event | category | flops | bytes accessed | tf_op | source)
XLA Modules:
  0.0 95.3 jit_solution(9686426838707045633)
XLA Ops:
  0.6 0.0 copy-start.3
  0.6 1.0 %fusion.158 = (f32[5,4096]{1,0:T(8,128)S(1)}, f32[5,4096]{1,0:T(8,128)S(1)}) fusion(f32[64,4096]{1,0:T(8,128)} %param.5), kind=kLoop, calls=%fused_computation.223 | loop fusion | bytes 327680 | tf_op jit(solution)/shard_map/slice | solution.py:57
  1.6 1.0 %fusion.159 = (f32[4,4096]{1,0:T(4,128)S(1)}, f32[4,4096]{1,0:T(4,128)S(1)}) fusion(f32[64,4096]{1,0:T(8,128)} %param.7), kind=kLoop, calls=%fused_computation.224 | loop fusion | bytes 262144 | tf_op jit(solution)/shard_map/slice | solution.py:57
  2.6 1.0 %fusion.160 = (f32[2,4096]{1,0:T(2,128)S(1)}, f32[2,4096]{1,0:T(2,128)S(1)}) fusion(f32[64,4096]{1,0:T(8,128)} %param.6), kind=kLoop, calls=%fused_computation.225 | loop fusion | bytes 131072 | tf_op jit(solution)/shard_map/slice | solution.py:57
  3.6 0.1 pad_maximum_fusion.6
  3.7 0.1 collective-permute-start
  3.8 0.1 pad_maximum_fusion.7
  3.8 5.8 %collective-permute-start.1 = (f32[11,4096]{1,0:T(8,128)S(1)}, f32[11,4096]{1,0:T(8,128)S(1)}, u32[]{:S(2)}, u32[]{:S(2)}) collective-permute-start(f32[11,4096]{1,0:T(8,128)S(1)} %pad_maximum_fusion.7), channel_id=1, source_target_pairs={{0,11},{1,0},{2,9},{3,2},{4,15},{5,4},{6,13},{7,6},{8,3},{9,8},{10... | collective-permute-start | bytes 540680 | tf_op jit(solution)/shard_map/ppermute | solution.py:60
  9.7 0.6 divide_reduce_fusion
  11.6 0.0 copy-done.3
  11.7 2.6 %fusion.78 = f32[32,4096]{1,0:T(8,128)S(1)} fusion(s32[32]{0:T(128)S(1)} %iota_add_fusion.1, s32[32,32]{1,0:T(8,128)S(1)} %copy-done.3, f32[32]{0:T(128)S(1)} %iota_add_fusion, f32[]{:T(128)S(6)} %div.47, s32[]{:T(128)} %bitcast.14), kind=kOutput, calls=%fused_computation.132 | convolution fusion | flops 52185088 | bytes 528648 | tf_op jit(solution)/shard_map/dot_general | solution.py:66
  14.2 1.4 %fusion.1 = f32[74,4096]{1,0:T(8,128)S(1)} fusion(f32[32,4096]{1,0:T(8,128)S(1)} %fusion.78, s32[74]{0:T(128)S(1)} %and_select_fusion, s32[32]{0:T(128)S(1)} %iota_add_fusion.1), kind=kOutput, calls=%fused_computation.2 | convolution fusion | flops 117031296 | bytes 1737128 | tf_op jit(solution)/shard_map/dot_general | solution.py:69
  15.6 0.4 fusion.148
  16.1 0.1 fusion.149
  16.1 0.4 fusion.145
  16.6 0.1 fusion.146
  16.6 0.4 fusion.144
  17.1 0.1 fusion.143
  17.1 0.4 fusion.141
  17.6 0.1 fusion.142
  17.6 0.0 copy-start.1
  17.7 0.4 fusion.139
  18.0 0.1 fusion.140
  18.1 0.0 collective-permute-done
  18.1 3.7 %collective-permute-done.1 = f32[11,4096]{1,0:T(8,128)S(1)} collective-permute-done((f32[11,4096]{1,0:T(8,128)S(1)}, f32[11,4096]{1,0:T(8,128)S(1)}, u32[]{:S(2)}, u32[]{:S(2)}) %collective-permute-start.1) | collective-permute-done | bytes 180256 | tf_op jit(solution)/shard_map/ppermute | solution.py:60
  21.8 0.0 copy-done.1
  21.8 0.1 pad_maximum_fusion
  22.0 0.0 copy-start
  22.0 0.4 fusion.147
  22.4 0.7 copy-done
  23.2 2.4 %fusion.35 = f32[72,4096]{1,0:T(8,128)S(1)} fusion(f32[5,4096]{1,0:T(8,128)S(1)} %slice.428, f32[64,4096]{1,0:T(8,128)S(1)} %copy-done.1, f32[5,4096]{1,0:T(8,128)S(1)} %slice.427, f32[74,4096]{1,0:T(8,128)S(1)} %pad_maximum_fusion, f32[74,4096]{1,0:T(8,128)S(1)} %fusion.1, f32[72,4095]{1,0:T(8,128)S(1)} %get-tuple-element.23, ...), kind=kLoop, calls=%fused_computation.52 | loop fusion | flops 9437184 | bytes 15367616 | tf_op jit(solution)/shard_map/add | solution.py:76
  25.6 0.4 fusion.156
  26.1 0.1 fusion.157
  26.1 0.1 pad_maximum_fusion.5
  26.3 2.1 %fusion.21 = f32[70,4096]{1,0:T(8,128)S(1)} fusion(f32[72,4096]{1,0:T(8,128)S(1)} %pad_maximum_fusion.5, f32[72,4096]{1,0:T(8,128)S(1)} %fusion.35, f32[74,4096]{1,0:T(8,128)S(1)} %fusion.1, f32[70,4095]{1,0:T(8,128)S(1)} %get-tuple-element.17, f32[70,1]{1,0:T(8,128)S(1)} %get-tuple-element.19, f32[70,4095]{1,0:T(8,128)S(1)} %get-tuple-element.39, ...), kind=kLoop, calls=%fused_computation.33 | loop fusion | flops 7454720 | bytes 13762560 | tf_op jit(solution)/shard_map/add | solution.py:76
  28.4 0.0 copy-start.2
  28.4 0.4 fusion.155
  28.8 0.1 fusion.154
  28.9 0.7 copy-done.2
  29.6 2.5 %maximum_subtract_fusion.4 = (f32[68,4096]{1,0:T(8,128)S(1)}, f32[68,4096]{1,0:T(8,128)S(1)}) fusion(f32[2,4096]{1,0:T(2,128)S(1)} %slice.474, f32[64,4096]{1,0:T(8,128)S(1)} %copy-done.2, f32[2,4096]{1,0:T(2,128)S(1)} %slice.473, f32[72,4096]{1,0:T(8,128)S(1)} %pad_maximum_fusion.5, f32[68,1]{1,0:T(8,128)S(1)} %get-tuple-element.35, ...), kind=kLoop, calls=%fused_computation.90 | loop fusion | flops 8077312 | bytes 15597568 | tf_op jit(solution)/shard_map/sub | solution.py:78
  32.1 0.4 fusion.152
  32.5 0.1 fusion.153
  32.6 1.3 %fusion.7 = f32[66,4096]{1,0:T(8,128)S(1)} fusion(f32[68,4096]{1,0:T(8,128)S(1)} %get-tuple-element.2, f32[74,4096]{1,0:T(8,128)S(1)} %fusion.1, f32[66,4095]{1,0:T(8,128)S(1)} %get-tuple-element.9, f32[66,1]{1,0:T(8,128)S(1)} %get-tuple-element.11, f32[66,4095]{1,0:T(8,128)S(1)} %get-tuple-element.31, f32[66,1]{1,0:T(8,128)S(1)} %get-tuple-element.33, ...), kind=kLoop, calls=%fused_computation.10 | loop fusion | flops 6758400 | bytes 11894784 | tf_op jit(solution)/shard_map/add | solution.py:82
  33.9 0.4 fusion.150
  34.3 0.1 fusion.151
  34.3 1.3 %fusion.66 = f32[64,4096]{1,0:T(8,128)S(1)} fusion(f32[66,4096]{1,0:T(8,128)S(1)} %fusion.7, f32[74,4096]{1,0:T(8,128)S(1)} %fusion.1, f32[68,4096]{1,0:T(8,128)S(1)} %get-tuple-element.2, f32[64,4095]{1,0:T(8,128)S(1)} %get-tuple-element.5, f32[64,1]{1,0:T(8,128)S(1)} %get-tuple-element.7, f32[64,4095]{1,0:T(8,128)S(1)} %get-tuple-element.27, ...), kind=kLoop, calls=%fused_computation.108 | loop fusion | flops 7340032 | bytes 12582912 | tf_op jit(solution)/shard_map/mul | solution.py:86
  35.7 22.7 %all_to_all.20 = f32[16,4,8,512]{3,2,1,0:T(8,128)S(1)} all-to-all(f32[16,4,8,512]{3,2,1,0:T(8,128)S(1)} %bitcast.15), channel_id=1, replica_groups={{0,16,32,48,64,80,96,112,128,144,160,176,192,208,224,240},{4,20,36,52,6..., dimensions={0} | all-to-all | bytes 2097152 | tf_op jit(solution)/shard_map/all_to_all | solution.py:88
  58.3 0.1 reduce_sum.28
  58.4 8.8 %all_to_all.21 = f32[4,8,512]{2,1,0:T(8,128)S(1)} all-to-all(f32[4,8,512]{2,1,0:T(8,128)S(1)} %reduce_sum.28), channel_id=1, replica_groups={{0,4,8,12},{16,20,24,28},{32,36,40,44},{48,52,56,60},{64,68,72,76},{80,..., dimensions={0} | all-to-all | bytes 131072 | tf_op jit(solution)/shard_map/all_to_all | solution.py:89
  67.2 8.1 %all_to_all.22 = f32[4,8,512]{2,1,0:T(8,128)S(1)} all-to-all(f32[4,8,512]{2,1,0:T(8,128)S(1)} %broadcast_in_dim.6), channel_id=1, replica_groups={{0,4,8,12},{16,20,24,28},{32,36,40,44},{48,52,56,60},{64,68,72,76},{80,..., dimensions={0} | all-to-all | bytes 131072 | tf_op jit(solution)/shard_map/all_to_all | solution.py:91
  75.3 1.1 %broadcast_in_dim.7 = f32[16,4,8,512]{3,2,1,0:T(8,128)} broadcast(f32[4,8,512]{2,1,0:T(8,128)S(1)} %all_to_all.22), dimensions={1,2,3} | broadcast | bytes 1114112 | tf_op jit(solution)/shard_map/broadcast_in_dim | solution.py:92
  76.4 4.9 %all-to-all-start.3 = ((f32[16,4,8,512]{3,2,1,0:T(8,128)}), f32[16,4,8,512]{3,2,1,0:T(8,128)S(1)}, u32[]{:S(2)}, u32[]{:S(2)}) async-start(f32[16,4,8,512]{3,2,1,0:T(8,128)} %broadcast_in_dim.7), calls=%async_computation.3 | async-start | bytes 2097152 | tf_op jit(solution)/shard_map/all_to_all | solution.py:93
  81.3 1.1 %slice_bitcast_fusion = f32[1,64,4096]{2,1,0:T(8,128)} fusion(f32[68,4096]{1,0:T(8,128)S(1)} %get-tuple-element.3), kind=kLoop, calls=%fused_computation.99 | loop fusion | bytes 2097152 | tf_op jit(solution)/shard_map/broadcast_in_dim | solution.py:96
  82.4 11.8 %all-to-all-done.3 = f32[16,4,8,512]{3,2,1,0:T(8,128)S(1)} async-done(((f32[16,4,8,512]{3,2,1,0:T(8,128)}), f32[16,4,8,512]{3,2,1,0:T(8,128)S(1)}, u32[]{:S(2)}, u32[]{:S(2)}) %all-to-all-start.3) | async-done | bytes 1048608 | tf_op jit(solution)/shard_map/all_to_all | solution.py:93
  94.1 0.1 broadcast_multiply_fusion
  94.2 1.1 %add_subtract_fusion = f32[64,4096]{1,0:T(8,128)} fusion(f32[64,4096]{1,0:T(8,128)S(1)} %copy-done, f32[64,4096]{1,0:T(8,128)S(1)} %bitcast.16), kind=kLoop, calls=%fused_computation.124 | loop fusion | flops 786432 | bytes 3145728 | tf_op jit(solution)/shard_map/sub | solution.py:95
  (11 shorter events, 0.1 us)
Async XLA Ops:
  0.6 11.0 %copy-start.3 = (s32[32,32]{1,0:T(8,128)S(1)}, s32[32,32]{1,0:T(8,128)}, u32[]{:S(2)}) copy-start(s32[32,32]{1,0:T(8,128)} %param.9) | copy-start | bytes 12292
  3.7 14.4 %collective-permute-start = (f32[11,4096]{1,0:T(8,128)S(1)}, f32[11,4096]{1,0:T(8,128)S(1)}, u32[]{:S(2)}, u32[]{:S(2)}) collective-permute-start(f32[11,4096]{1,0:T(8,128)S(1)} %pad_maximum_fusion.6), channel_id=1, source_target_pairs={{0,1},{1,10},{2,3},{3,8},{4,5},{5,14},{6,7},{7,12},{8,9},{9,2},{10... | collective-permute-start | bytes 540680 | tf_op jit(solution)/shard_map/ppermute | solution.py:59
  3.8 18.0 %collective-permute-start.1 = (f32[11,4096]{1,0:T(8,128)S(1)}, f32[11,4096]{1,0:T(8,128)S(1)}, u32[]{:S(2)}, u32[]{:S(2)}) collective-permute-start(f32[11,4096]{1,0:T(8,128)S(1)} %pad_maximum_fusion.7), channel_id=1, source_target_pairs={{0,11},{1,0},{2,9},{3,2},{4,15},{5,4},{6,13},{7,6},{8,3},{9,8},{10... | collective-permute-start | bytes 540680 | tf_op jit(solution)/shard_map/ppermute | solution.py:60
  17.6 4.2 %copy-start.1 = (f32[64,4096]{1,0:T(8,128)S(1)}, f32[64,4096]{1,0:T(8,128)}, u32[]{:S(2)}) copy-start(f32[64,4096]{1,0:T(8,128)} %param.5) | copy-start | bytes 3145732
  22.0 1.2 %copy-start = (f32[64,4096]{1,0:T(8,128)S(1)}, f32[64,4096]{1,0:T(8,128)}, u32[]{:S(2)}) copy-start(f32[64,4096]{1,0:T(8,128)} %param.7) | copy-start | bytes 3145732
  28.4 1.2 %copy-start.2 = (f32[64,4096]{1,0:T(8,128)S(1)}, f32[64,4096]{1,0:T(8,128)}, u32[]{:S(2)}) copy-start(f32[64,4096]{1,0:T(8,128)} %param.6) | copy-start | bytes 3145732
  76.4 17.7 %all-to-all-start.3 = ((f32[16,4,8,512]{3,2,1,0:T(8,128)}), f32[16,4,8,512]{3,2,1,0:T(8,128)S(1)}, u32[]{:S(2)}, u32[]{:S(2)}) async-start(f32[16,4,8,512]{3,2,1,0:T(8,128)} %broadcast_in_dim.7), calls=%async_computation.3 | async-start | bytes 2097152 | tf_op jit(solution)/shard_map/all_to_all | solution.py:93

commit v2 on v1

v2 whole, which is shorter than its diff:
```python
import jax
import jax.numpy as jnp
import numpy as np
from jax import lax
from jax.experimental import pallas as pl
from jax.experimental.pallas import tpu as pltpu
from jax.sharding import PartitionSpec as P

STEPS = 3
TWO_PI = 6.283185307179586
DT = 0.12
REG = 0.1
RATE = 1.0
SAMPLES = 64
MODES = 32
HALO = 2 * STEPS - 1
TILE = 64
HALF = TILE // 2
COLS = HALF + 2 * HALO
TALL = TILE + 16

SAMP = np.arange(64).reshape(4, 4, 4)
ALONG_Z = SAMP.reshape(16, 4).tolist()
ALONG_XY = SAMP.transpose(2, 0, 1).reshape(4, 16).tolist()


def mode_scale(modes):
    ranks = jnp.arange(1, modes + 1, dtype=jnp.float32)
    return 4.0 / jnp.sum(1.0 / ranks), 1.0 / jnp.sqrt(ranks)


def sine_table(places, modes, period):
    freq = jnp.arange(1, modes + 1, dtype=jnp.int32)
    turns = freq[:, None] * places[None, :] % period
    return jnp.sin(TWO_PI * turns.astype(jnp.float32) / period)


def split(value):
    high = value.astype(jnp.bfloat16)
    return high, (value - high.astype(jnp.float32)).astype(jnp.bfloat16)


def window_kernel(where_ref, *refs):
    ins, out = refs[:9], refs[9]
    odd = where_ref[3]
    for f in range(3):
        row = jnp.concatenate([r[...] for r in ins[3 * f : 3 * f + 3]], axis=1)
        even_part = row[:, 128 - HALO : 256 - HALO]
        odd_part = row[:, 192 - HALO : 320 - HALO]
        out[f] = jnp.where(odd == 1, odd_part, even_part)


def own_windows(fields, tile):
    rows, width = fields[0].shape
    blocks = width // 128
    middle = tile // 2
    where = jnp.stack([(middle - 1) % blocks, middle, (middle + 1) % blocks, tile % 2]).astype(jnp.int32)
    specs = [pl.BlockSpec((rows, 128), lambda i, w, n=n: (0, w[n])) for n in range(3)]
    return pl.pallas_call(
        window_kernel,
        out_shape=jax.ShapeDtypeStruct((3, rows, 128), jnp.float32),
        grid_spec=pltpu.PrefetchScalarGridSpec(
            num_scalar_prefetch=1,
            grid=(1,),
            in_specs=specs * 3,
            out_specs=pl.BlockSpec((3, rows, 128), lambda i, w: (0, 0, 0)),
        ),
        name="own_windows",
    )(where, *[f for f in fields for _ in range(3)])


def tile_kernel(points_ref, gen_ref, col_ref, row_ref, x_ref, out_ref, inner_ref, kx_ref, ky_ref, v_ref, g_ref, t_ref, s_ref):
    f32 = jnp.float32
    lane = lax.broadcasted_iota(jnp.int32, (1, 128), 1)
    left = lane < SAMPLES

    for f, ref, scale in ((0, v_ref, 1.0), (1, g_ref, DT), (2, t_ref, 1.0)):
        x = x_ref[f] * scale
        for j in range(COLS):
            ref[j] = jnp.where(left, x[:, j : j + 1], x[:, j + HALF : j + HALF + 1])

    points = points_ref[...]
    for p in range(MODES):
        cells = (points * gen_ref[:, p : p + 1]) & 65535
        coords = cells.astype(f32) * (1.0 / 65536.0) - 0.5
        both = jnp.concatenate([jnp.where(left, coords, 0.0), jnp.where(left, 0.0, coords)], axis=0)
        high, low = split(both)
        inner_ref[48 * p : 48 * p + 48, :] = jnp.dot(
            col_ref[...], jnp.concatenate([high, low, high], axis=0), preferred_element_type=f32
        )

    def fields(j, before):
        high, low = split(inner_ref[pl.ds(j, MODES, stride=48), :])
        log = jnp.dot(row_ref[...], jnp.concatenate([high, low, high], axis=0), preferred_element_type=f32)
        k = 0.5 * DT + (0.5 * DT * 0.8) * jnp.tanh(log)
        kx_ref[j] = before + k
        ky_ref[j] = k + pltpu.roll(k, TALL - 1, 0)
        return k

    lax.fori_loop(0, COLS, fields, jnp.zeros((TALL, 128), f32))

    def divergence(j, carry):
        v, left_flux = carry
        right = v_ref[j + 1]
        right_flux = kx_ref[j + 1] * (right - v)
        down_flux = ky_ref[j] * (pltpu.roll(v, TALL - 1, 0) - v)
        new = v + ((right_flux - left_flux) + (down_flux - pltpu.roll(down_flux, 1, 0)))
        return new, (right, right_flux)

    def sweep(first, body):
        v = v_ref[first]
        start = (v, kx_ref[first] * (v - v_ref[first - 1]))
        return start, first, COLS - first

    def state_step(j, carry):
        new, after = divergence(j, carry)
        v_ref[j] = new + g_ref[j]
        return after

    def last_state_step(j, carry):
        new, after = divergence(j, carry)
        v_ref[j] = new + g_ref[j] - t_ref[j]
        return after

    def first_costate_step(j, carry):
        new, after = divergence(j, carry)
        s_ref[j] = carry[0] + new
        v_ref[j] = new
        return after

    for t, body in enumerate((state_step, state_step, last_state_step, first_costate_step)):
        start, low_j, high_j = sweep(t + 1, body)
        lax.fori_loop(low_j, high_j, body, start)

    source = lax.broadcasted_iota(jnp.int32, (256, 128), 0) % 128 // SAMPLES
    place = lax.broadcasted_iota(jnp.int32, (256, 128), 1) // HALF % 2
    add_samples = (source == place).astype(f32).astype(jnp.bfloat16)

    def last_costate_step(j, carry):
        total, carry = carry
        new, after = divergence(j, carry)
        high, low = split((s_ref[j] + new)[8 : 8 + TILE])
        sums = jnp.dot(jnp.concatenate([high, low], axis=1), add_samples, preferred_element_type=f32)
        return jnp.where(lane % HALF == j - HALO, sums, total), after

    start, low_j, high_j = sweep(HALO, last_costate_step)
    total, _ = lax.fori_loop(low_j, high_j, last_costate_step, (jnp.zeros((TILE, 128), f32), start))

    total = jnp.where(left, total[:HALF], total[HALF:])
    control = x_ref[1]
    top = pltpu.roll(control[8 : 8 + HALF], 128 - HALO, 1)
    bottom = pltpu.roll(control[8 + HALF : 8 + TILE], TILE - HALO, 1)
    control = jnp.where(left, top, bottom)
    out_ref[...] = control - RATE * (total * (DT / SAMPLES) + REG * control)


def tile_gradient(points, gen_t, col_parts, row_parts, x):
    big = pltpu.VMEM((COLS, TALL, 128), jnp.float32)
    return pl.pallas_call(
        tile_kernel,
        out_shape=jax.ShapeDtypeStruct((HALF, 128), jnp.float32),
        in_specs=[pl.BlockSpec(memory_space=pltpu.VMEM)] * 5,
        out_specs=pl.BlockSpec(memory_space=pltpu.VMEM),
        scratch_shapes=[pltpu.VMEM((48 * MODES, 128), jnp.float32)] + [big] * 6,
        compiler_params=pltpu.CompilerParams(vmem_limit_bytes=40 * 2**20),
        cost_estimate=pl.CostEstimate(flops=400_000_000, bytes_accessed=400_000, transcendentals=430_000),
        name="tile_gradient",
    )(points, gen_t, col_parts, row_parts, x)


def assemble_kernel(tiles_ref, out_ref):
    left = lax.broadcasted_iota(jnp.int32, (1, 128), 1) < TILE
    for m in range(SAMPLES // 2):
        a, b = tiles_ref[2 * m], tiles_ref[2 * m + 1]
        out_ref[:HALF, 128 * m : 128 * m + 128] = jnp.where(left, a, pltpu.roll(b, TILE, 1))
        out_ref[HALF:, 128 * m : 128 * m + 128] = jnp.where(left, pltpu.roll(a, TILE, 1), b)


def assemble(tiles):
    return pl.pallas_call(
        assemble_kernel,
        out_shape=jax.ShapeDtypeStruct((TILE, SAMPLES * TILE), jnp.float32),
        in_specs=[pl.BlockSpec(memory_space=pltpu.VMEM)],
        out_specs=pl.BlockSpec(memory_space=pltpu.VMEM),
        compiler_params=pltpu.CompilerParams(vmem_limit_bytes=16 * 2**20),
        name="assemble",
    )(tiles)


def tables_for_tile(tile, first_row, grid_rows, width):
    scale, by_rank = mode_scale(MODES)
    j = jnp.arange(48, dtype=jnp.int32)
    columns = (TILE * tile - HALO + j) % width
    cols = [sine_table((columns + h * HALF) % width, MODES, width).T * by_rank for h in (0, 1)]
    high, low = split(jnp.concatenate(cols, axis=1))
    col_parts = jnp.concatenate([high, high, low], axis=1)
    places = (first_row - 8 + jnp.arange(TALL, dtype=jnp.int32)) % grid_rows
    high, low = split(sine_table(places, MODES, grid_rows).T * (by_rank * scale))
    row_parts = jnp.concatenate([high, high, low], axis=1)
    return col_parts, row_parts


def diffuse(coef, field):
    middle = field[1:-1]
    center = coef[1:-1]
    total = 0.5 * (center + coef[:-2]) * (field[:-2] - middle)
    total = total + 0.5 * (center + coef[2:]) * (field[2:] - middle)
    total = total + 0.5 * (center + jnp.roll(center, 1, -1)) * (jnp.roll(middle, 1, -1) - middle)
    total = total + 0.5 * (center + jnp.roll(center, -1, -1)) * (jnp.roll(middle, -1, -1) - middle)
    return total


def own_final_state(initial_state, control, before, after, point, generator, first_row, grid_rows):
    rows, width = initial_state.shape
    h = STEPS
    cells = point[:, None] * generator % 65536
    scale, by_rank = mode_scale(MODES)
    coeff = (cells.astype(jnp.float32) / 65536.0 - 0.5) * (scale * by_rank[:, None] * by_rank[None, :])
    col_table = sine_table(jnp.arange(width, dtype=jnp.int32), MODES, width)
    inner = jnp.dot(coeff, col_table, precision=lax.Precision.HIGHEST)
    places = (first_row - h + jnp.arange(rows + 2 * h, dtype=jnp.int32)) % grid_rows
    table = sine_table(places, MODES, grid_rows)
    coef = 1.0 + 0.8 * jnp.tanh(jnp.dot(table.T, inner, precision=lax.Precision.HIGHEST))
    state = jnp.concatenate([before[:h], initial_state, after[:h]], axis=0)
    source = jnp.concatenate([before[h:], control, after[h:]], axis=0)
    for step in range(STEPS):
        state = state[1:-1] + DT * (diffuse(coef, state) + source)
        coef, source = coef[1:-1], source[1:-1]
    return state


def strip_shift(step):
    pairs = []
    for samp in range(64):
        for strip in range(4):
            to = (strip + step) % 4
            other = samp if to // 2 == strip // 2 else samp ^ 2
            pairs.append((samp * 4 + strip, other * 4 + to))
    return pairs


RING_UP = [(i, (i + 1) % 4) for i in range(4)]
RING_DOWN = [(j, i) for i, j in RING_UP]


def on_device(initial_state, target, control, point_index, generator):
    rows, width = initial_state.shape
    grid_rows = rows * lax.axis_size("strip")
    tile = lax.axis_index("samp")
    first_row = lax.axis_index("strip") * rows

    own = own_windows((initial_state, control, target), tile)
    above = lax.ppermute(own[:, -8:], "strip", RING_UP)
    below = lax.ppermute(own[:, :8], "strip", RING_DOWN)
    lane = jnp.arange(128, dtype=jnp.int32)[None, :]
    points = lax.psum(jnp.where(lane % SAMPLES == tile, point_index[:, None], 0), "samp")
    col_parts, row_parts = tables_for_tile(tile, first_row, grid_rows, width)
    x = jnp.concatenate([above, own, below], axis=1)
    mine = tile_gradient(points, generator.T, col_parts, row_parts, x)

    tiles = jnp.broadcast_to(mine[None], (4, HALF, 128))
    tiles = lax.all_to_all(tiles, "samp", 0, 0, axis_index_groups=ALONG_Z, tiled=True)
    tiles = jnp.broadcast_to(tiles[None], (16, 4, HALF, 128))
    tiles = lax.all_to_all(tiles, "samp", 0, 0, axis_index_groups=ALONG_XY, tiled=True)
    new_control = assemble(tiles.reshape(SAMPLES, HALF, 128))

    tail = jnp.concatenate([initial_state[-STEPS:], control[1 - STEPS :]], axis=0)
    head = jnp.concatenate([initial_state[:STEPS], control[: STEPS - 1]], axis=0)
    before = lax.ppermute(tail, ("samp", "strip"), strip_shift(1))
    after = lax.ppermute(head, ("samp", "strip"), strip_shift(-1))
    state = own_final_state(initial_state, control, before, after, point_index, generator, first_row, grid_rows)
    return (new_control, state[None])


def solution(mesh):
    placed = (P("strip", None), P("strip", None), P("strip", None), P("samp"), P())
    return jax.shard_map(
        on_device,
        mesh=mesh,
        in_specs=placed,
        out_specs=(P("strip", None), P("samp", "strip", None)),
        check_vma=False,
    )
```

time: 95.8 us -> 106 us (1.11)
  Pallas kernels: 0 us -> 22 us
  blocking collectives: 39.5 us -> 21 us
  starting transfers between devices: 10.8 us -> 20.2 us
  waiting for transfers between devices: 15.5 us -> 6.17 us
  local copies, waits for them, and re-layouts: 11.4 us -> 16.9 us
    all_to_all x3 -> x0, blocking collectives: 39.5 us -> none  [the longest x1 22.7 us: on_device(): lax.all_to_all(blocks, 'samp', 0, 0, axis_index_groups=ALONG_XY, tiled=True)]
    pallas_call x0 -> x3, Pallas kernels: none -> 22 us  [the longest x1 18.2 us: tile_gradient(): pl.pallas_call(tile_kernel, out_shape=jax.ShapeDtypeStruct((HALF, 128), j...]
    psum x0 -> x1, blocking collectives: none -> 21 us  [on_device(): lax.psum(jnp.where(lane % SAMPLES == tile, point_index[:, None], 0), 'samp')]
    ppermute x0 -> x2, starting transfers between devices: none -> 5.65 us  [the longest x1 4.93 us: on_device(): below = lax.ppermute(own[:, :8], 'strip', RING_DOWN)]
    all_to_all x1 -> x2, waiting for transfers between devices: 11.8 us -> 6.16 us  [the longest x1 6.16 us: on_device(): lax.all_to_all(tiles, 'samp', 0, 0, axis_index_groups=ALONG_XY, tiled=True)]
    broadcast_in_dim x0 -> x1, other arithmetic: none -> 5.47 us  [on_device(): return (new_control, state[None])]
    slice x8 -> x6, local copies, waits for them, and re-layouts: 1.91 us -> 5.63 us  [diffuse(): jnp.roll(center, -1, -1)]
    all_to_all x1 -> x2, starting transfers between devices: 4.9 us -> 8.61 us  [the longest x1 5.32 us: on_device(): lax.all_to_all(tiles, 'samp', 0, 0, axis_index_groups=ALONG_XY, tiled=True)]
  transfers between devices with their start and end apart: 3 -> 6, of which waited for: 2 -> 1; matrix products, arithmetic and copies ran while one was open for 9% -> 27% of each run, Pallas kernels for 0% -> 20%
where the time goes in v2:
time: 106 us; the launch traced here: 105 us
  Pallas kernels  22 us (21%)
  blocking collectives  21 us (20%)
  starting transfers between devices  20.2 us (19%)
  local copies, waits for them, and re-layouts  16.9 us (16%)
  other arithmetic  12.4 us (12%)
  waiting for transfers between devices  6.17 us (6%)
  matrix products  3.86 us (4%)
  between operations  2.32 us (2%)
    psum x1, blocking collectives, on_device(): lax.psum(jnp.where(lane % SAMPLES == tile, point_index[:, None], 0), 'samp')  21 us
    pallas_call x1, Pallas kernels, tile_gradient(): pl.pallas_call(tile_kernel, out_shape=jax.ShapeDtypeStruct((HALF, 128), j...  18.2 us
    all_to_all x1, waiting for transfers between devices, on_device(): lax.all_to_all(tiles, 'samp', 0, 0, axis_index_groups=ALONG_XY, tiled=True)  6.16 us
    ppermute x1, starting transfers between devices, on_device(): after = lax.ppermute(head, ('samp', 'strip'), strip_shift(-1))  5.82 us
    slice x6, local copies, waits for them, and re-layouts, diffuse(): jnp.roll(center, -1, -1)  5.63 us
    broadcast_in_dim x1, other arithmetic, on_device(): return (new_control, state[None])  5.47 us
    all_to_all x1, starting transfers between devices, on_device(): lax.all_to_all(tiles, 'samp', 0, 0, axis_index_groups=ALONG_XY, tiled=True)  5.32 us
    ppermute x1, starting transfers between devices, on_device(): below = lax.ppermute(own[:, :8], 'strip', RING_DOWN)  4.93 us
  transfers between devices with their start and end apart: 6, of which 1 were waited for; matrix products, arithmetic and copies ran while one was open for 27% of the time, Pallas kernels for 20%

profile of v2, /device:TPU:8, one launch (start us, length us, event | category | flops | bytes accessed | tf_op | source)
XLA Modules:
  0.0 104.7 jit_solution(3498230288642841158)
XLA Ops:
  0.6 1.0 fusion.139
  1.6 1.0 fusion.140
  2.7 0.1 collective-permute-start.2
  2.8 5.8 %collective-permute-start.3 = (f32[5,4096]{1,0:T(8,128)S(1)}, f32[5,4096]{1,0:T(8,128)S(1)}, u32[]{:S(2)}, u32[]{:S(2)}) collective-permute-start(f32[5,4096]{1,0:T(8,128)S(1)} %pad_maximum_fusion.7), channel_id=1, source_target_pairs={{0,11},{1,0},{2,9},{3,2},{4,15},{5,4},{6,13},{7,6},{8,3},{9,8},{10... | collective-permute-start | bytes 245768 | tf_op jit(solution)/shard_map/ppermute | solution.py:270
  8.6 0.7 pad_add_fusion.where_ref
  9.3 2.5 %own_windows.1 = f32[3,64,128]{2,1,0:T(8,128)} custom-call(s32[4]{0:T(128)} %pad_add_fusion.where_ref, f32[64,4096]{1,0:T(8,128)} %refs_2_.1, f32[64,4096]{1,0:T(8,128)} %refs_2_.1, f32[64,4096]{1,0:T(8,128)} %refs_2_.1, f32[64,4096]{1,0:T(8,128)} %refs_5_.1, f32[64,4096]{1,0:T(8,128)} %refs_5_.1, f32[64,4096]{1,0:T(8,128)} %refs_5_.1, f32[64,4096]{1,0:T(8,128)} %refs_8_.1, ...), custom_call_target="tpu_custom_call" | custom-call | tf_op jit(solution)/shard_map/own_windows/pallas_call | solution.py:59
  11.8 0.7 fusion.141
  12.5 0.7 collective-permute-start
  13.2 4.9 %collective-permute-start.1 = (f32[3,8,128]{2,1,0:T(8,128)S(1)}, f32[3,8,128]{2,1,0:T(8,128)S(1)}, u32[]{:S(2)}, u32[]{:S(2)}) collective-permute-start(f32[3,8,128]{2,1,0:T(8,128)S(1)} %get-tuple-element.29), channel_id=1, source_target_pairs={{1,0},{2,1},{3,2},{0,3},{5,4},{6,5},{7,6},{4,7},{9,8},{10,9},{11,1... | collective-permute-start | bytes 36872 | tf_op jit(solution)/shard_map/ppermute | solution.py:254
  18.2 0.6 divide_reduce_fusion
  20.2 0.0 copy-done.10
  20.2 2.6 %fusion.52 = f32[32,4096]{1,0:T(8,128)S(1)} fusion(s32[32]{0:T(128)S(1)} %iota_add_fusion.1, s32[32,32]{1,0:T(8,128)S(1)} %copy-done.10, f32[32]{0:T(128)S(1)} %get-tuple-element.36, f32[32]{0:T(128)S(1)} %get-tuple-element.37, s32[]{:T(128)} %bitcast.11), kind=kOutput, calls=%fused_computation.85 | convolution fusion | flops 52184064 | bytes 528772 | tf_op jit(solution)/shard_map/dot_general | solution.py:220
  22.7 1.3 %fusion.1 = f32[70,4096]{1,0:T(8,128)S(1)} fusion(f32[32,4096]{1,0:T(8,128)S(1)} %fusion.52, s32[70]{0:T(128)S(1)} %and_select_fusion, s32[32]{0:T(128)S(1)} %iota_add_fusion.1), kind=kOutput, calls=%fused_computation.2 | convolution fusion | flops 110705280 | bytes 1671576 | tf_op jit(solution)/shard_map/dot_general | solution.py:223
  24.0 1.8 %fusion.137 = (f32[68,4095]{1,0:T(8,128)}, f32[68,4095]{1,0:T(8,128)}) fusion(f32[70,4096]{1,0:T(8,128)S(1)} %fusion.1), kind=kLoop, calls=%fused_computation.219 | loop fusion | bytes 4455360 | tf_op jit(solution)/shard_map/jit(_roll_static)/slice | solution.py:209
  25.9 0.1 fusion.138
  26.0 1.9 %fusion.134 = (f32[66,4095]{1,0:T(8,128)}, f32[66,4095]{1,0:T(8,128)}) fusion(f32[70,4096]{1,0:T(8,128)S(1)} %fusion.1), kind=kLoop, calls=%fused_computation.216 | loop fusion | bytes 4324320 | tf_op jit(solution)/shard_map/jit(_roll_static)/slice | solution.py:209
  27.8 0.1 fusion.135
  27.9 1.7 %fusion.130 = (f32[64,4095]{1,0:T(8,128)}, f32[64,4095]{1,0:T(8,128)}) fusion(f32[70,4096]{1,0:T(8,128)S(1)} %fusion.1), kind=kLoop, calls=%fused_computation.212 | loop fusion | bytes 4193280 | tf_op jit(solution)/shard_map/jit(_roll_static)/slice | solution.py:209
  29.6 0.1 fusion.131
  29.7 0.3 fusion.68
  30.0 0.1 fusion.109
  30.1 0.1 subtract_convert_fusion.1
  30.2 0.1 fusion.75
  30.2 0.1 copy.9
  30.3 0.2 fusion.64
  30.5 0.0 copy-start.2
  30.5 0.1 pad_maximum_fusion.10.col_ref
  30.6 0.1 pad_maximum_fusion.11.row_ref
  30.7 0.1 copy.8
  30.8 21.0 %psum.7.points_ref = s32[1,128]{1,0:T(1,128)S(1)} all-reduce(s32[1,128]{1,0:T(1,128)S(1)} %compare_select_fusion.10), channel_id=1, replica_groups=mesh['samp'=64,'strip'=4] {'samp'}, use_global_device_ids=true, to_apply=%region_0.1 | all-reduce | flops 128 | bytes 1024 | tf_op jit(solution)/shard_map/psum | solution.py:256
  51.7 0.0 collective-permute-done
  51.7 0.0 collective-permute-done.1
  51.8 0.0 copy-done.7
  51.8 18.2 %tile_gradient.1 = f32[32,128]{1,0:T(8,128)S(1)} custom-call(s32[1,128]{1,0:T(1,128)S(1)} %psum.7.points_ref, s32[32,32]{1,0:T(8,128)S(1)} %bitcast.13, bf16[48,192]{1,0:T(8,128)(2,1)S(1)} %pad_maximum_fusion.10.col_ref, bf16[80,96]{1,0:T(8,128)(2,1)S(1)} %pad_maximum_fusion.11.row_ref, f32[3,80,128]{2,1,0:T(8,128)S(1)} %pad_maximum_fusion.8.x_ref), custom_call_target="tpu_custom_call" | custom-call | flops 400000000 | bytes 400000 | tf_op jit(solution)/shard_map/tile_gradient/pallas_call | solution.py:159
  69.9 0.6 broadcast_in_dim.20
  70.6 3.3 %all-to-all-start = ((f32[4,32,128]{2,1,0:T(8,128)}), f32[4,32,128]{2,1,0:T(8,128)S(1)}, u32[]{:S(2)}, u32[]{:S(2)}) async-start(f32[4,32,128]{2,1,0:T(8,128)} %broadcast_in_dim.20), calls=%async_computation | async-start | bytes 131072 | tf_op jit(solution)/shard_map/all_to_all | solution.py:262
  73.9 0.0 collective-permute-done.2
  73.9 0.0 copy-start.8
  73.9 0.0 collective-permute-done.3
  73.9 0.0 copy-start.9
  74.0 0.6 copy-done.8
  74.5 0.0 copy-done.9
  74.6 0.0 copy-done.2
  74.6 0.1 pad_maximum_fusion.4
  74.7 0.0 copy-start
  74.7 0.4 fusion.136
  75.1 1.1 %slice.277 = f32[2,4096]{1,0:T(2,128)S(1)} slice(f32[5,4096]{1,0:T(8,128)} %copy-done.8), slice={[3:5], [0:4096]} | slice | bytes 65536 | tf_op jit(solution)/shard_map/slice | solution.py:225
  76.3 0.9 slice.278
  77.3 2.4 %fusion.17 = f32[68,4096]{1,0:T(8,128)S(1)} fusion(f32[3,4096]{1,0:T(4,128)S(1)} %slice.264, f32[64,4096]{1,0:T(8,128)S(1)} %copy-done.2, f32[3,4096]{1,0:T(4,128)S(1)} %slice.263, f32[70,4096]{1,0:T(8,128)S(1)} %pad_maximum_fusion.4, f32[70,4096]{1,0:T(8,128)S(1)} %fusion.1, f32[68,4095]{1,0:T(8,128)S(1)} %copy-done.4, f32[68,1]{1,0:T(8,128)S(1)} %get-tuple-element.23, ...), kind=kLoop, calls=%fused_computation.24 | loop fusion | flops 8912896 | bytes 14515680 | tf_op jit(solution)/shard_map/add | solution.py:227
  79.7 0.4 fusion.132
  80.1 0.1 fusion.133
  80.2 0.1 pad_maximum_fusion.5
  80.3 0.6 copy-done.6
  81.0 0.6 copy-done.5
  81.6 2.0 %fusion.3 = f32[66,4096]{1,0:T(8,128)S(1)} fusion(f32[68,4096]{1,0:T(8,128)S(1)} %pad_maximum_fusion.5, f32[68,4096]{1,0:T(8,128)S(1)} %fusion.17, f32[70,4096]{1,0:T(8,128)S(1)} %fusion.1, f32[66,4095]{1,0:T(8,128)S(1)} %copy-done.6, f32[66,1]{1,0:T(8,128)S(1)} %get-tuple-element.17, f32[66,4095]{1,0:T(8,128)S(1)} %get-tuple-element.11, ...), kind=kLoop, calls=%fused_computation.5 | loop fusion | flops 7028736 | bytes 12976128 | tf_op jit(solution)/shard_map/add | solution.py:227
  83.6 1.7 %fusion.128 = (f32[64,4095]{1,0:T(8,128)}, f32[64,4095]{1,0:T(8,128)}) fusion(f32[66,4096]{1,0:T(8,128)S(1)} %fusion.3), kind=kLoop, calls=%fused_computation.210 | loop fusion | bytes 4193280 | tf_op jit(solution)/shard_map/jit(_roll_static)/slice | solution.py:209
  85.3 0.0 copy-done.1
  85.3 0.1 fusion.129
  85.4 0.0 all-to-all-done
  85.4 1.1 %broadcast_in_dim.21 = f32[16,4,32,128]{3,2,1,0:T(8,128)} broadcast(f32[4,32,128]{2,1,0:T(8,128)S(1)} %all-to-all-done), dimensions={1,2,3} | broadcast | bytes 1114112 | tf_op jit(solution)/shard_map/broadcast_in_dim | solution.py:263
  86.5 5.3 %all-to-all-start.1 = ((f32[16,4,32,128]{3,2,1,0:T(8,128)}), f32[16,4,32,128]{3,2,1,0:T(8,128)S(1)}, u32[]{:S(2)}, u32[]{:S(2)}) async-start(f32[16,4,32,128]{3,2,1,0:T(8,128)} %broadcast_in_dim.21), calls=%async_computation.1 | async-start | bytes 2097152 | tf_op jit(solution)/shard_map/all_to_all | solution.py:264
  91.8 5.5 %fusion.40 = f32[1,64,4096]{2,1,0:T(8,128)} fusion(f32[64,4096]{1,0:T(8,128)S(1)} %copy-done, f32[66,4096]{1,0:T(8,128)} %copy-done.1, f32[70,4096]{1,0:T(8,128)S(1)} %fusion.1, f32[64,4095]{1,0:T(8,128)} %get-tuple-element.7, f32[64,1]{1,0:T(8,128)S(1)} %get-tuple-element.9, f32[64,4095]{1,0:T(8,128)} %get-tuple-element.3, ...), kind=kLoop, calls=%fused_computation.63 | loop fusion | flops 6815744 | bytes 12582912 | tf_op jit(solution)/shard_map/broadcast_in_dim | solution.py:272
  97.3 6.2 %all-to-all-done.1 = f32[16,4,32,128]{3,2,1,0:T(8,128)S(1)} async-done(((f32[16,4,32,128]{3,2,1,0:T(8,128)}), f32[16,4,32,128]{3,2,1,0:T(8,128)S(1)}, u32[]{:S(2)}, u32[]{:S(2)}) %all-to-all-start.1) | async-done | bytes 1048608 | tf_op jit(solution)/shard_map/all_to_all | solution.py:264
  103.4 1.3 %assemble.1 = f32[64,4096]{1,0:T(8,128)} custom-call(f32[64,32,128]{2,1,0:T(8,128)S(1)} %bitcast.12), custom_call_target="tpu_custom_call" | custom-call | tf_op jit(solution)/shard_map/assemble/pallas_call | solution.py:180
  (21 shorter events, 0.2 us)
Async XLA Ops:
  2.7 71.2 %collective-permute-start.2 = (f32[5,4096]{1,0:T(8,128)S(1)}, f32[5,4096]{1,0:T(8,128)S(1)}, u32[]{:S(2)}, u32[]{:S(2)}) collective-permute-start(f32[5,4096]{1,0:T(8,128)S(1)} %pad_maximum_fusion.6), channel_id=1, source_target_pairs={{0,1},{1,10},{2,3},{3,8},{4,5},{5,14},{6,7},{7,12},{8,9},{9,2},{10... | collective-permute-start | bytes 245768 | tf_op jit(solution)/shard_map/ppermute | solution.py:269
  2.8 71.1 %collective-permute-start.3 = (f32[5,4096]{1,0:T(8,128)S(1)}, f32[5,4096]{1,0:T(8,128)S(1)}, u32[]{:S(2)}, u32[]{:S(2)}) collective-permute-start(f32[5,4096]{1,0:T(8,128)S(1)} %pad_maximum_fusion.7), channel_id=1, source_target_pairs={{0,11},{1,0},{2,9},{3,2},{4,15},{5,4},{6,13},{7,6},{8,3},{9,8},{10... | collective-permute-start | bytes 245768 | tf_op jit(solution)/shard_map/ppermute | solution.py:270
  9.3 10.9 %copy-start.10 = (s32[32,32]{1,0:T(8,128)S(1)}, s32[32,32]{1,0:T(8,128)}, u32[]{:S(2)}) copy-start(s32[32,32]{1,0:T(8,128)} %param.9) | copy-start | bytes 12292
  12.5 39.2 %collective-permute-start = (f32[3,8,128]{2,1,0:T(8,128)S(1)}, f32[3,8,128]{2,1,0:T(8,128)S(1)}, u32[]{:S(2)}, u32[]{:S(2)}) collective-permute-start(f32[3,8,128]{2,1,0:T(8,128)S(1)} %get-tuple-element.28), channel_id=1, source_target_pairs={{0,1},{1,2},{2,3},{3,0},{4,5},{5,6},{6,7},{7,4},{8,9},{9,10},{10,1... | collective-permute-start | bytes 36872 | tf_op jit(solution)/shard_map/ppermute | solution.py:253
  13.2 38.5 %collective-permute-start.1 = (f32[3,8,128]{2,1,0:T(8,128)S(1)}, f32[3,8,128]{2,1,0:T(8,128)S(1)}, u32[]{:S(2)}, u32[]{:S(2)}) collective-permute-start(f32[3,8,128]{2,1,0:T(8,128)S(1)} %get-tuple-element.29), channel_id=1, source_target_pairs={{1,0},{2,1},{3,2},{0,3},{5,4},{6,5},{7,6},{4,7},{9,8},{10,9},{11,1... | collective-permute-start | bytes 36872 | tf_op jit(solution)/shard_map/ppermute | solution.py:254
  27.9 23.9 %copy-start.7 = (f32[3,64,128]{2,1,0:T(8,128)S(1)}, f32[3,64,128]{2,1,0:T(8,128)}, u32[]{:S(2)}) copy-start(f32[3,64,128]{2,1,0:T(8,128)} %own_windows.1) | copy-start | bytes 294916
  30.5 44.1 %copy-start.2 = (f32[64,4096]{1,0:T(8,128)S(1)}, f32[64,4096]{1,0:T(8,128)}, u32[]{:S(2)}) copy-start(f32[64,4096]{1,0:T(8,128)} %refs_2_.1) | copy-start | bytes 3145732
  70.6 14.8 %all-to-all-start = ((f32[4,32,128]{2,1,0:T(8,128)}), f32[4,32,128]{2,1,0:T(8,128)S(1)}, u32[]{:S(2)}, u32[]{:S(2)}) async-start(f32[4,32,128]{2,1,0:T(8,128)} %broadcast_in_dim.20), calls=%async_computation | async-start | bytes 131072 | tf_op jit(solution)/shard_map/all_to_all | solution.py:262
  73.9 0.7 copy-start.8
  73.9 0.7 copy-start.9
  74.7 2.5 %copy-start = (f32[64,4096]{1,0:T(8,128)S(1)}, f32[64,4096]{1,0:T(8,128)}, u32[]{:S(2)}) copy-start(f32[64,4096]{1,0:T(8,128)} %refs_5_.1) | copy-start | bytes 3145732
  74.7 2.5 %copy-start.3 = (f32[68,4095]{1,0:T(8,128)S(1)}, f32[68,4095]{1,0:T(8,128)}, u32[]{:S(2)}) copy-start(f32[68,4095]{1,0:T(8,128)} %get-tuple-element.20) | copy-start | bytes 3341524
  74.7 2.5 %copy-start.4 = (f32[68,4095]{1,0:T(8,128)S(1)}, f32[68,4095]{1,0:T(8,128)}, u32[]{:S(2)}) copy-start(f32[68,4095]{1,0:T(8,128)} %get-tuple-element.21) | copy-start | bytes 3341524
  79.7 1.3 %copy-start.6 = (f32[66,4095]{1,0:T(8,128)S(1)}, f32[66,4095]{1,0:T(8,128)}, u32[]{:S(2)}) copy-start(f32[66,4095]{1,0:T(8,128)} %get-tuple-element.15) | copy-start | bytes 3243244
  80.2 1.4 %copy-start.5 = (f32[66,4095]{1,0:T(8,128)S(1)}, f32[66,4095]{1,0:T(8,128)}, u32[]{:S(2)}) copy-start(f32[66,4095]{1,0:T(8,128)} %get-tuple-element.14) | copy-start | bytes 3243244
  83.6 1.7 %copy-start.1 = (f32[66,4096]{1,0:T(8,128)}, f32[66,4096]{1,0:T(8,128)S(1)}, u32[]{:S(2)}) copy-start(f32[66,4096]{1,0:T(8,128)S(1)} %fusion.3) | copy-start | bytes 3244036
  86.5 17.0 %all-to-all-start.1 = ((f32[16,4,32,128]{3,2,1,0:T(8,128)}), f32[16,4,32,128]{3,2,1,0:T(8,128)S(1)}, u32[]{:S(2)}, u32[]{:S(2)}) async-start(f32[16,4,32,128]{3,2,1,0:T(8,128)} %broadcast_in_dim.21), calls=%async_computation.1 | async-start | bytes 2097152 | tf_op jit(solution)/shard_map/all_to_all | solution.py:264

commit v3 on v2

v3 whole, which is shorter than its diff:
```python
import jax
import jax.numpy as jnp
import numpy as np
from jax import lax
from jax.experimental import pallas as pl
from jax.experimental.pallas import tpu as pltpu
from jax.sharding import PartitionSpec as P

STEPS = 3
DT = 0.12
REG = 0.1
RATE = 1.0
SAMPLES = 64
MODES = 32
HALO = 2 * STEPS - 1
TILE = 64
HALF = TILE // 2
COLS = HALF + 2 * HALO
TALL = TILE + 16

SAMP = np.arange(64).reshape(4, 4, 4)
ALONG_Z = SAMP.reshape(16, 4).tolist()
ALONG_XY = SAMP.transpose(2, 0, 1).reshape(4, 16).tolist()


RANKS = np.arange(1, MODES + 1)
BY_RANK = (1.0 / np.sqrt(RANKS)).astype(np.float32)
SCALE = np.float32(4.0 / np.sum(1.0 / RANKS))


def split(value):
    high = value.astype(jnp.bfloat16)
    return high, (value - high.astype(jnp.float32)).astype(jnp.bfloat16)


def both_parts(value):
    high = value.astype(jnp.bfloat16)
    low = (value - high.astype(np.float32)).astype(jnp.bfloat16)
    return np.concatenate([high, high, low], axis=1)


def row_tables(grid_rows):
    places = np.arange(-8, grid_rows + 8)[:, None]
    sines = np.sin(2.0 * np.pi * (places * RANKS[None, :] % grid_rows) / grid_rows)
    return both_parts((sines * BY_RANK * SCALE).astype(np.float32))


def rows_of_strip(row_ref):
    first = pl.multiple_of(lax.axis_index("strip") * TILE, TILE)
    return row_ref[pl.ds(first, TALL), :]


def tile_col_tables(width):
    ranks = np.tile(RANKS, 4)[None, :]
    turn = 2.0 * np.pi / width
    coarse = turn * (TILE * np.arange(width // TILE)[:, None] * ranks % width)
    half = np.repeat([0, HALF, 0, HALF], MODES)[None, :]
    fine = turn * ((np.arange(48)[:, None] - HALO + half) * ranks % width)
    scaled = np.tile(BY_RANK, 4)[None, :]
    coarse = np.stack([np.sin(coarse), np.cos(coarse)])
    fine = np.stack([np.sin(fine) * scaled, np.cos(fine) * scaled])
    return coarse.astype(np.float32), fine.astype(np.float32)


def edges_kernel(*refs):
    fields, (own, tail, head), near, wide, sems, wide_sems = refs[:3], refs[3:6], *refs[6:]
    rows, width = fields[0].shape
    blocks = width // 128
    tile = lax.axis_index("samp")
    copies = []
    for f in range(2):
        for n, first in enumerate((rows - 8, 0)):
            copies.append(pltpu.make_async_copy(fields[f].at[first : first + 8, :], wide.at[f, n], wide_sems.at[f, n]))
    for f in range(3):
        for n in range(3):
            block = lax.rem(tile // 2 + (blocks - 1 + n), blocks)
            columns = pl.ds(pl.multiple_of(block * 128, 128), 128)
            copies.append(pltpu.make_async_copy(fields[f].at[:, columns], near.at[f, n], sems.at[f, n]))
    for copy in copies:
        copy.start()
    for copy in copies:
        copy.wait()
    row = lax.broadcasted_iota(jnp.int32, (8, 128), 0)
    for b in range(blocks):
        columns = slice(128 * b, 128 * b + 128)
        tail[b] = jnp.where(row >= 8 - STEPS, wide[0, 0, :, columns], pltpu.roll(wide[1, 0, :, columns], 5, 0))
        head[b] = jnp.where(row < STEPS, wide[0, 1, :, columns], pltpu.roll(wide[1, 1, :, columns], 3, 0))
    odd = lax.rem(tile, 2) == 1
    for f in range(3):
        line = jnp.concatenate([near[f, n] for n in range(3)], axis=1)
        even_part = line[:, 128 - HALO : 256 - HALO]
        odd_part = line[:, 192 - HALO : 320 - HALO]
        part = jnp.where(odd, odd_part, even_part)
        own[f] = part
        tail[blocks + f] = part[-8:]
        head[blocks + f] = part[:8]


def own_edges(fields):
    rows, width = fields[0].shape
    vmem = pl.BlockSpec(memory_space=pltpu.VMEM)
    payload = jax.ShapeDtypeStruct((width // 128 + 3, 8, 128), jnp.float32)
    return pl.pallas_call(
        edges_kernel,
        out_shape=[jax.ShapeDtypeStruct((3, rows, 128), jnp.float32), payload, payload],
        in_specs=[pl.BlockSpec(memory_space=pl.ANY)] * 3,
        out_specs=[vmem] * 3,
        scratch_shapes=[
            pltpu.VMEM((3, 3, rows, 128), jnp.float32),
            pltpu.VMEM((2, 2, 8, width), jnp.float32),
            pltpu.SemaphoreType.DMA((3, 3)),
            pltpu.SemaphoreType.DMA((2, 2)),
        ],
        compiler_params=pltpu.CompilerParams(vmem_limit_bytes=56 * 2**20),
        name="own_edges",
    )(*fields)


def tile_kernel(points_ref, gen_ref, coarse_ref, fine_ref, row_ref, above_ref, own_ref, below_ref, out_ref, inner_ref, kx_ref, ky_ref, v_ref, g_ref, t_ref, s_ref):
    f32 = jnp.float32
    lane = lax.broadcasted_iota(jnp.int32, (1, 128), 1)
    left = lane < SAMPLES
    edge = above_ref.shape[0] - 3
    tile = lax.axis_index("samp")
    sines = coarse_ref[0, pl.ds(tile, 1), :] * fine_ref[1] + coarse_ref[1, pl.ds(tile, 1), :] * fine_ref[0]
    high, low = split(sines)
    col_parts = jnp.concatenate([high, low[:, : 2 * MODES]], axis=1)
    row_parts = rows_of_strip(row_ref)

    sample = lax.broadcasted_iota(jnp.int32, (SAMPLES, 128), 0)
    points = jnp.sum(jnp.where(sample == lane % SAMPLES, points_ref[...], 0), axis=0, keepdims=True)
    for p in range(MODES):
        cells = (points * gen_ref[:, p : p + 1]) & 65535
        coords = cells.astype(f32) * (1.0 / 65536.0) - 0.5
        both = jnp.concatenate([jnp.where(left, coords, 0.0), jnp.where(left, 0.0, coords)], axis=0)
        high, low = split(both)
        inner_ref[48 * p : 48 * p + 48, :] = jnp.dot(
            col_parts, jnp.concatenate([high, low, high], axis=0), preferred_element_type=f32
        )

    start_fields = []
    for f in range(3):
        x = jnp.concatenate([above_ref[edge + f], own_ref[f], below_ref[edge + f]], axis=0)
        start_fields.append(x * DT if f == 1 else x)
    before = jnp.zeros((TALL, 128), f32)
    for j in range(COLS):
        high, low = split(inner_ref[pl.ds(j, MODES, stride=48), :])
        log = jnp.dot(row_parts, jnp.concatenate([high, low, high], axis=0), preferred_element_type=f32)
        k = 0.5 * DT + (0.5 * DT * 0.8) * jnp.tanh(log)
        kx_ref[j] = before + k
        ky_ref[j] = k + pltpu.roll(k, TALL - 1, 0)
        before = k
        for x, ref in zip(start_fields, (v_ref, g_ref, t_ref)):
            ref[j] = jnp.where(left, x[:, j : j + 1], x[:, j + HALF : j + HALF + 1])

    def divergence(j, carry):
        v, left_flux = carry
        right = v_ref[j + 1]
        right_flux = kx_ref[j + 1] * (right - v)
        down_flux = ky_ref[j] * (pltpu.roll(v, TALL - 1, 0) - v)
        new = v + ((right_flux - left_flux) + (down_flux - pltpu.roll(down_flux, 1, 0)))
        return new, (right, right_flux)

    def sweep(first, body):
        v = v_ref[first]
        start = (v, kx_ref[first] * (v - v_ref[first - 1]))
        return start, first, COLS - first

    def state_step(j, carry):
        new, after = divergence(j, carry)
        v_ref[j] = new + g_ref[j]
        return after

    def last_state_step(j, carry):
        new, after = divergence(j, carry)
        v_ref[j] = new + g_ref[j] - t_ref[j]
        return after

    def first_costate_step(j, carry):
        new, after = divergence(j, carry)
        s_ref[j] = carry[0] + new
        v_ref[j] = new
        return after

    for t, body in enumerate((state_step, state_step, last_state_step, first_costate_step)):
        start, low_j, high_j = sweep(t + 1, body)
        lax.fori_loop(low_j, high_j, body, start, unroll=2)

    source = lax.broadcasted_iota(jnp.int32, (256, 128), 0) % 128 // SAMPLES
    place = lax.broadcasted_iota(jnp.int32, (256, 128), 1) // HALF % 2
    add_samples = (source == place).astype(f32).astype(jnp.bfloat16)

    def last_costate_step(j, carry):
        total, carry = carry
        new, after = divergence(j, carry)
        high, low = split((s_ref[j] + new)[8 : 8 + TILE])
        sums = jnp.dot(jnp.concatenate([high, low], axis=1), add_samples, preferred_element_type=f32)
        return jnp.where(lane % HALF == j - HALO, sums, total), after

    start, low_j, high_j = sweep(HALO, last_costate_step)
    total, _ = lax.fori_loop(low_j, high_j, last_costate_step, (jnp.zeros((TILE, 128), f32), start), unroll=16)

    total = jnp.where(left, total[:HALF], total[HALF:])
    control = own_ref[1]
    top = pltpu.roll(control[:HALF], 128 - HALO, 1)
    bottom = pltpu.roll(control[HALF:], TILE - HALO, 1)
    control = jnp.where(left, top, bottom)
    out_ref[...] = control - RATE * (total * (DT / SAMPLES) + REG * control)


def tile_gradient(*args):
    big = pltpu.VMEM((COLS, TALL, 128), jnp.float32)
    return pl.pallas_call(
        tile_kernel,
        out_shape=jax.ShapeDtypeStruct((HALF, 128), jnp.float32),
        in_specs=[pl.BlockSpec(memory_space=pltpu.VMEM)] * len(args),
        out_specs=pl.BlockSpec(memory_space=pltpu.VMEM),
        scratch_shapes=[pltpu.VMEM((48 * MODES, 128), jnp.float32)] + [big] * 6,
        compiler_params=pltpu.CompilerParams(vmem_limit_bytes=40 * 2**20),
        cost_estimate=pl.CostEstimate(flops=400_000_000, bytes_accessed=400_000, transcendentals=430_000),
        name="tile_gradient",
    )(*args)


def assemble_kernel(tiles_ref, out_ref):
    left = lax.broadcasted_iota(jnp.int32, (1, 128), 1) < TILE
    z = lax.rem(lax.axis_index("samp"), 4)
    for m in range(SAMPLES // 2):
        near = 4 * (m // 2)
        a = tiles_ref[near + lax.rem(z + (4 - 2 * m % 4), 4)]
        b = tiles_ref[near + lax.rem(z + (3 - 2 * m % 4), 4)]
        out_ref[:HALF, 128 * m : 128 * m + 128] = jnp.where(left, a, pltpu.roll(b, TILE, 1))
        out_ref[HALF:, 128 * m : 128 * m + 128] = jnp.where(left, pltpu.roll(a, TILE, 1), b)


def assemble(tiles):
    return pl.pallas_call(
        assemble_kernel,
        out_shape=jax.ShapeDtypeStruct((TILE, SAMPLES * TILE), jnp.float32),
        in_specs=[pl.BlockSpec(memory_space=pltpu.VMEM)],
        out_specs=pl.BlockSpec(memory_space=pltpu.VMEM),
        compiler_params=pltpu.CompilerParams(vmem_limit_bytes=16 * 2**20),
        name="assemble",
    )(tiles)


def state_kernel(point_ref, gen_ref, row_ref, coarse_ref, fine_ref, init_ref, control_ref, before_ref, after_ref, out_ref, kx_ref, ky_ref, g_ref, v_ref, w_ref):
    f32 = jnp.float32
    blocks = v_ref.shape[0]
    lane = lax.broadcasted_iota(jnp.int32, (1, 128), 1)
    first, last = lane == 0, lane == 127

    cells = (point_ref[0] * gen_ref[...]) & 65535
    high, low = split(cells.astype(f32) * (1.0 / 65536.0) - 0.5)
    coords = jnp.concatenate([high, high, low], axis=1)

    rows, above = out_ref.shape[0], 8
    row_parts = rows_of_strip(row_ref)

    def to_left(value):
        return pltpu.roll(value, 127, 1)

    def up(value):
        return pltpu.roll(value, value.shape[0] - 1, 0)

    before_k, before_shifted, first_shifted = None, None, None
    for b in range(blocks):
        sine = coarse_ref[0][:, b : b + 1] * fine_ref[1] + coarse_ref[1][:, b : b + 1] * fine_ref[0]
        high, low = split(sine)
        inner = jnp.dot(coords, jnp.concatenate([high, low, high], axis=0), preferred_element_type=f32)
        high, low = split(inner)
        log = jnp.dot(row_parts, jnp.concatenate([high, low, high], axis=0), preferred_element_type=f32)
        k = 0.5 * DT + (0.5 * DT * 0.8) * jnp.tanh(log)
        ky_ref[b] = k + up(k)
        shifted = to_left(k)
        if b == 0:
            first_shifted = shifted
        else:
            kx_ref[b - 1] = before_k + jnp.where(last, shifted, before_shifted)
        before_k, before_shifted = k, shifted
        columns = slice(128 * b, 128 * b + 128)
        lead, trail = before_ref[b], after_ref[b]
        v_ref[b] = jnp.concatenate([lead, init_ref[:, columns], trail], axis=0)
        g_ref[b] = DT * jnp.concatenate([pltpu.roll(lead, 3, 0), control_ref[:, columns], pltpu.roll(trail, 5, 0)], axis=0)
    kx_ref[blocks - 1] = before_k + jnp.where(last, first_shifted, before_shifted)

    def sweep(source, write):
        v = source[blocks - 1]
        flux = kx_ref[blocks - 1] * (jnp.where(last, to_left(source[0]), to_left(v)) - v)
        start = (source[0], to_left(source[0]), pltpu.roll(flux, 1, 1))

        def step(b, carry):
            v, shifted, flux_before = carry
            following = source[lax.rem(b + 1, blocks)]
            following_shifted = to_left(following)
            flux = kx_ref[b] * (jnp.where(last, following_shifted, shifted) - v)
            flux_shifted = pltpu.roll(flux, 1, 1)
            down = ky_ref[b] * (up(v) - v)
            new = v + ((flux - jnp.where(first, flux_before, flux_shifted)) + (down - pltpu.roll(down, 1, 0)))
            write(b, new + g_ref[b])
            return following, following_shifted, flux_shifted

        lax.fori_loop(0, blocks, step, start, unroll=2)

    def keep(ref):
        def write(b, value):
            ref[b] = value
        return write

    def finish(b, value):
        out_ref[:, pl.ds(pl.multiple_of(b * 128, 128), 128)] = value[above : above + rows]

    sweep(v_ref, keep(w_ref))
    sweep(w_ref, keep(v_ref))
    sweep(v_ref, finish)


def own_final_state(point_index, generator, row_table, initial_state, control, before, after):
    rows, width = initial_state.shape
    blocks = width // 128
    turns = 2.0 * np.pi / width * RANKS[:, None]
    coarse = turns * (128 * np.arange(blocks))[None, :]
    fine = turns * np.arange(128)[None, :]
    scaled = BY_RANK[:, None]
    coarse = np.stack([np.sin(coarse), np.cos(coarse)]).astype(np.float32)
    fine = np.stack([np.sin(fine) * scaled, np.cos(fine) * scaled]).astype(np.float32)
    big = pltpu.VMEM((blocks, rows + 16, 128), jnp.float32)
    return pl.pallas_call(
        state_kernel,
        out_shape=jax.ShapeDtypeStruct((rows, width), jnp.float32),
        in_specs=[pl.BlockSpec(memory_space=pltpu.SMEM)] + [pl.BlockSpec(memory_space=pltpu.VMEM)] * 8,
        out_specs=pl.BlockSpec(memory_space=pltpu.VMEM),
        scratch_shapes=[big] * 5,
        compiler_params=pltpu.CompilerParams(vmem_limit_bytes=40 * 2**20),
        cost_estimate=pl.CostEstimate(flops=2_000_000_000, bytes_accessed=3_500_000, transcendentals=330_000),
        name="own_final_state",
    )(point_index, generator, row_table, coarse, fine, initial_state, control, before, after)


RING_UP = [(i, (i + 1) % 4) for i in range(4)]
RING_DOWN = [(j, i) for i, j in RING_UP]


def z_shift(step):
    return [(i, i // 4 * 4 + (i + step) % 4) for i in range(64)]


def on_device(initial_state, target, control, point_index, generator):
    rows, width = initial_state.shape
    row_table = row_tables(rows * lax.axis_size("strip"))

    own, tail, head = own_edges((initial_state, control, target))
    point_index, tail, head = lax.optimization_barrier((point_index, tail, head))
    above = lax.ppermute(tail, "strip", RING_UP)
    below = lax.ppermute(head, "strip", RING_DOWN)
    points = jnp.broadcast_to(point_index[:, None, None], (SAMPLES, 1, 128))
    points = lax.all_to_all(points, "samp", 0, 0, tiled=True).reshape(SAMPLES, 128)
    mine = tile_gradient(points, generator.T, *tile_col_tables(width), row_table, above, own, below)

    tiles = jnp.stack([mine] + [lax.ppermute(mine, "samp", z_shift(k)) for k in (1, 2, 3)])
    tiles = jnp.broadcast_to(tiles[None], (16, 4, HALF, 128))
    tiles, generator = lax.optimization_barrier((tiles, generator))
    tiles = lax.all_to_all(tiles, "samp", 0, 0, axis_index_groups=ALONG_XY, tiled=True)
    new_control = assemble(tiles.reshape(SAMPLES, HALF, 128))

    state = own_final_state(point_index, generator, row_table, initial_state, control, above, below)
    return (new_control, state[None])


def solution(mesh):
    placed = (P("strip", None), P("strip", None), P("strip", None), P("samp"), P())
    return jax.shard_map(
        on_device,
        mesh=mesh,
        in_specs=placed,
        out_specs=(P("strip", None), P("samp", "strip", None)),
        check_vma=False,
    )
```

time: 106 us -> 67.7 us (0.64)
  blocking collectives: 21 us -> 0 us
  local copies, waits for them, and re-layouts: 16.9 us -> 3.48 us
  other arithmetic: 12.4 us -> 0.01 us
  waiting for transfers between devices: 6.17 us -> 13.8 us
  starting transfers between devices: 20.2 us -> 25.5 us
  matrix products: 3.86 us -> 0 us
    psum x1 -> x0, blocking collectives: 21 us -> none  [on_device(): lax.psum(jnp.where(lane % SAMPLES == tile, point_index[:, None], 0), 'samp')]
    slice x18 -> x0, local copies, waits for them, and re-layouts: 13.1 us -> none  [the longest x6 5.63 us: diffuse(): jnp.roll(center, -1, -1)]
    pallas_call x1 -> x2, Pallas kernels: 2.51 us -> 14.6 us  [the longest x1 12.3 us: own_final_state(): pl.pallas_call(state_kernel, out_shape=jax.ShapeDtypeStruct((rows, width)...]
    pallas_call x1, Pallas kernels: 18.2 us -> 7.05 us  [tile_gradient(): pl.pallas_call(tile_kernel, out_shape=jax.ShapeDtypeStruct((HALF, 128), j...]
    all_to_all x1, waiting for transfers between devices: 0.01 us -> 8.75 us  [on_device(): lax.all_to_all(points, 'samp', 0, 0, tiled=True).reshape(SAMPLES, 128)]
    all_to_all x1, starting transfers between devices: 3.28 us -> 11.1 us  [on_device(): lax.all_to_all(points, 'samp', 0, 0, tiled=True).reshape(SAMPLES, 128)]
    all_to_all x1, waiting for transfers between devices: 6.16 us -> 0.01 us  [on_device(): lax.all_to_all(tiles, 'samp', 0, 0, axis_index_groups=ALONG_XY, tiled=True)]
    broadcast_in_dim x1 -> x0, other arithmetic: 5.47 us -> none  [on_device(): return (new_control, state[None])]
  transfers between devices with their start and end apart: 6 -> 7, of which waited for: 1 -> 4; matrix products, arithmetic and copies ran while one was open for 27% -> 1% of each run, Pallas kernels for 20% -> 18%
where the time goes in v3:
time: 67.7 us; the launch traced here: 67.2 us
  starting transfers between devices  25.5 us (38%)
  Pallas kernels  23 us (34%)
  waiting for transfers between devices  13.8 us (20%)
  local copies, waits for them, and re-layouts  3.48 us (5%)
  between operations  1.41 us (2%)
    pallas_call x1, Pallas kernels, own_final_state(): pl.pallas_call(state_kernel, out_shape=jax.ShapeDtypeStruct((rows, width)...  12.3 us
    all_to_all x1, starting transfers between devices, on_device(): lax.all_to_all(points, 'samp', 0, 0, tiled=True).reshape(SAMPLES, 128)  11.1 us
    all_to_all x1, waiting for transfers between devices, on_device(): lax.all_to_all(points, 'samp', 0, 0, tiled=True).reshape(SAMPLES, 128)  8.75 us
    pallas_call x1, Pallas kernels, tile_gradient(): pl.pallas_call(tile_kernel, out_shape=jax.ShapeDtypeStruct((HALF, 128), j...  7.05 us
    ppermute x1, starting transfers between devices, on_device(): below = lax.ppermute(head, 'strip', RING_DOWN)  6.71 us
    ppermute x3, waiting for transfers between devices, on_device(): lax.ppermute(mine, 'samp', z_shift(k))  5.04 us
    all_to_all x1, starting transfers between devices, on_device(): lax.all_to_all(tiles, 'samp', 0, 0, axis_index_groups=ALONG_XY, tiled=True)  4.99 us
    ppermute x3, starting transfers between devices, on_device(): lax.ppermute(mine, 'samp', z_shift(k))  2.64 us
  transfers between devices with their start and end apart: 7, of which 4 were waited for; matrix products, arithmetic and copies ran while one was open for 1% of the time, Pallas kernels for 18%

profile of v3, /device:TPU:8, one launch (start us, length us, event | category | flops | bytes accessed | tf_op | source)
XLA Modules:
  0.0 67.2 jit_solution(7217062492767459574)
XLA Ops:
  0.6 0.0 copy-start.5
  0.6 2.3 %own_edges.1 = (f32[3,64,128]{2,1,0:T(8,128)}, f32[35,8,128]{2,1,0:T(8,128)}, f32[35,8,128]{2,1,0:T(8,128)}) custom-call(f32[64,4096]{1,0:T(8,128)} %init_ref.1, f32[64,4096]{1,0:T(8,128)} %control_ref.1, f32[64,4096]{1,0:T(8,128)} %refs_2_.1), custom_call_target="tpu_custom_call" | custom-call | tf_op jit(solution)/shard_map/own_edges/pallas_call | solution.py:103
  3.0 0.1 collective-permute-start
  3.0 6.7 %collective-permute-start.1 = (f32[35,8,128]{2,1,0:T(8,128)}, f32[35,8,128]{2,1,0:T(8,128)S(1)}, u32[]{:S(2)}, u32[]{:S(2)}) collective-permute-start(f32[35,8,128]{2,1,0:T(8,128)} %get-tuple-element.15), channel_id=1, source_target_pairs={{1,0},{2,1},{3,2},{0,3},{5,4},{6,5},{7,6},{4,7},{9,8},{10,9},{11,1... | collective-permute-start | bytes 430088 | tf_op jit(solution)/shard_map/ppermute | solution.py:355
  10.4 0.0 copy-start.4
  10.4 0.6 broadcast_in_dim.18
  11.1 0.0 copy-start.2
  11.1 0.0 copy-start.6
  11.1 11.1 %all-to-all-start = ((s32[64,1,128]{2,1,0:T(1,128)}), s32[64,1,128]{2,1,0:T(1,128)S(1)}, u32[]{:S(2)}, u32[]{:S(2)}) async-start(s32[64,1,128]{2,1,0:T(1,128)} %broadcast_in_dim.18), calls=%async_computation | async-start | bytes 65536 | tf_op jit(solution)/shard_map/all_to_all | solution.py:357
  22.1 0.0 copy-done.2
  22.1 0.1 copy.13
  22.2 8.7 %all-to-all-done = s32[64,1,128]{2,1,0:T(1,128)S(1)} async-done(((s32[64,1,128]{2,1,0:T(1,128)}), s32[64,1,128]{2,1,0:T(1,128)S(1)}, u32[]{:S(2)}, u32[]{:S(2)}) %all-to-all-start) | async-done | bytes 32800 | tf_op jit(solution)/shard_map/all_to_all | solution.py:357
  31.0 0.0 collective-permute-done.above_ref.before_ref
  31.0 0.0 collective-permute-done.1.below_ref.after_ref
  31.0 0.0 copy-done.5
  31.0 0.0 copy-done.4
  31.0 0.0 copy-done.6
  31.0 0.0 copy-start.3
  31.0 0.9 %copy-done.3 = f32[3,64,128]{2,1,0:T(8,128)S(1)} copy-done((f32[3,64,128]{2,1,0:T(8,128)S(1)}, f32[3,64,128]{2,1,0:T(8,128)}, u32[]{:S(2)}) %copy-start.3) | copy-done | bytes 98328
  31.9 7.1 %tile_gradient.1 = f32[32,128]{1,0:T(8,128)S(1)} custom-call(s32[64,128]{1,0:T(8,128)S(1)} %bitcast.11, s32[32,32]{1,0:T(8,128)S(1)} %bitcast.12, f32[2,64,128]{2,1,0:T(8,128)S(1)} %copy-done.5, f32[2,48,128]{2,1,0:T(8,128)S(1)} %copy-done.6, bf16[272,96]{1,0:T(8,128)(2,1)S(1)} %copy-done.4, f32[35,8,128]{2,1,0:T(8,128)S(1)} %collective-permute-done.above_ref.before_ref, ...), custom_call_target="tpu_custom_call" | custom-call | flops 400000000 | bytes 400000 | tf_op jit(solution)/shard_map/tile_gradient/pallas_call | solution.py:213
  38.9 0.7 %collective-permute-start.4 = (f32[32,128]{1,0:T(8,128)S(1)}, f32[32,128]{1,0:T(8,128)S(1)}, u32[]{:S(2)}, u32[]{:S(2)}) collective-permute-start(f32[32,128]{1,0:T(8,128)S(1)} %tile_gradient.1), channel_id=1, source_target_pairs={{0,12},{4,0},{8,4},{12,8},{16,28},{20,16},{24,20},{28,24},{32,44},... | collective-permute-start | bytes 49160 | tf_op jit(solution)/shard_map/ppermute | solution.py:360
  39.7 1.4 %collective-permute-start.3 = (f32[32,128]{1,0:T(8,128)S(1)}, f32[32,128]{1,0:T(8,128)S(1)}, u32[]{:S(2)}, u32[]{:S(2)}) collective-permute-start(f32[32,128]{1,0:T(8,128)S(1)} %tile_gradient.1), channel_id=1, source_target_pairs={{0,8},{4,12},{8,0},{12,4},{16,24},{20,28},{24,16},{28,20},{32,40},... | collective-permute-start | bytes 49160 | tf_op jit(solution)/shard_map/ppermute | solution.py:360
  41.1 0.5 collective-permute-start.2
  41.6 1.2 %collective-permute-done.4 = f32[32,128]{1,0:T(8,128)S(1)} collective-permute-done((f32[32,128]{1,0:T(8,128)S(1)}, f32[32,128]{1,0:T(8,128)S(1)}, u32[]{:S(2)}, u32[]{:S(2)}) %collective-permute-start.4) | collective-permute-done | bytes 16416 | tf_op jit(solution)/shard_map/ppermute | solution.py:360
  42.8 1.5 %collective-permute-done.3 = f32[32,128]{1,0:T(8,128)S(1)} collective-permute-done((f32[32,128]{1,0:T(8,128)S(1)}, f32[32,128]{1,0:T(8,128)S(1)}, u32[]{:S(2)}, u32[]{:S(2)}) %collective-permute-start.3) | collective-permute-done | bytes 16416 | tf_op jit(solution)/shard_map/ppermute | solution.py:360
  44.3 2.3 %collective-permute-done.2 = f32[32,128]{1,0:T(8,128)S(1)} collective-permute-done((f32[32,128]{1,0:T(8,128)S(1)}, f32[32,128]{1,0:T(8,128)S(1)}, u32[]{:S(2)}, u32[]{:S(2)}) %collective-permute-start.2) | collective-permute-done | bytes 16416 | tf_op jit(solution)/shard_map/ppermute | solution.py:360
  46.6 0.0 copy-start.7
  46.6 1.1 %broadcast_in_dim.19 = f32[16,4,32,128]{3,2,1,0:T(8,128)} broadcast(f32[4,32,128]{2,1,0:T(8,128)S(1)} %pad_maximum_fusion), dimensions={1,2,3} | broadcast | bytes 1114112 | tf_op jit(solution)/shard_map/broadcast_in_dim | solution.py:361
  47.7 0.0 copy-start
  47.7 0.0 copy-start.1
  47.7 5.0 %all-to-all-start.1 = ((f32[16,4,32,128]{3,2,1,0:T(8,128)}), f32[16,4,32,128]{3,2,1,0:T(8,128)S(1)}, u32[]{:S(2)}, u32[]{:S(2)}) async-start(f32[16,4,32,128]{3,2,1,0:T(8,128)} %broadcast_in_dim.19), calls=%async_computation.1 | async-start | bytes 2097152 | tf_op jit(solution)/shard_map/all_to_all | solution.py:363
  52.7 0.0 copy-done.7
  52.7 0.0 copy-done
  52.8 0.0 copy-done.1
  52.8 0.0 copy-start.8
  52.8 0.7 %copy-done.8 = f32[2,32,32]{2,1,0:T(8,128)S(1)} copy-done((f32[2,32,32]{2,1,0:T(8,128)S(1)}, f32[2,32,32]{2,1,0:T(8,128)}, u32[]{:S(2)}) %copy-start.8) | copy-done | bytes 8216
  53.5 12.3 %own_final_state.1 = f32[64,4096]{1,0:T(8,128)} custom-call(s32[1]{0:T(128)} %copy.14.point_ref, s32[32,32]{1,0:T(8,128)S(1)} %copy-done.2, bf16[272,96]{1,0:T(8,128)(2,1)S(1)} %copy-done.4, f32[2,32,32]{2,1,0:T(8,128)S(1)} %copy-done.8, f32[2,32,128]{2,1,0:T(8,128)S(1)} %copy-done.7, f32[64,4096]{1,0:T(8,128)S(1)} %copy-done, f32[64,4096]{1,0:T(8,128)S(1)} %copy-done.1, ...), custom_call_target="tpu_custom_call" | custom-call | flops 2000000000 | bytes 3500000 | tf_op jit(solution)/shard_map/own_final_state/pallas_call | solution.py:328
  65.9 0.0 all-to-all-done.1
  65.9 1.3 %assemble.1 = f32[64,4096]{1,0:T(8,128)} custom-call(f32[64,32,128]{2,1,0:T(8,128)S(1)} %bitcast.10), custom_call_target="tpu_custom_call" | custom-call | tf_op jit(solution)/shard_map/assemble/pallas_call | solution.py:237
  (1 shorter events, 0.0 us)
Async XLA Ops:
  0.6 30.3 %copy-start.5 = (f32[2,64,128]{2,1,0:T(8,128)S(1)}, f32[2,64,128]{2,1,0:T(8,128)}, u32[]{:S(2)}) copy-start(f32[2,64,128]{2,1,0:T(8,128)} %constant.10.clone.coarse_ref) | copy-start | bytes 196612
  3.0 28.0 %collective-permute-start = (f32[35,8,128]{2,1,0:T(8,128)}, f32[35,8,128]{2,1,0:T(8,128)S(1)}, u32[]{:S(2)}, u32[]{:S(2)}) collective-permute-start(f32[35,8,128]{2,1,0:T(8,128)} %get-tuple-element.13), channel_id=1, source_target_pairs={{0,1},{1,2},{2,3},{3,0},{4,5},{5,6},{6,7},{7,4},{8,9},{9,10},{10,1... | collective-permute-start | bytes 430088 | tf_op jit(solution)/shard_map/ppermute | solution.py:354
  3.0 27.9 %collective-permute-start.1 = (f32[35,8,128]{2,1,0:T(8,128)}, f32[35,8,128]{2,1,0:T(8,128)S(1)}, u32[]{:S(2)}, u32[]{:S(2)}) collective-permute-start(f32[35,8,128]{2,1,0:T(8,128)} %get-tuple-element.15), channel_id=1, source_target_pairs={{1,0},{2,1},{3,2},{0,3},{5,4},{6,5},{7,6},{4,7},{9,8},{10,9},{11,1... | collective-permute-start | bytes 430088 | tf_op jit(solution)/shard_map/ppermute | solution.py:355
  10.4 20.6 %copy-start.4 = (bf16[272,96]{1,0:T(8,128)(2,1)S(1)}, bf16[272,96]{1,0:T(8,128)(2,1)}, u32[]{:S(2)}) copy-start(bf16[272,96]{1,0:T(8,128)(2,1)} %constant.12.clone.row_ref) | copy-start | bytes 156676
  11.1 11.1 %copy-start.2 = (s32[32,32]{1,0:T(8,128)S(1)}, s32[32,32]{1,0:T(8,128)}, u32[]{:S(2)}) copy-start(s32[32,32]{1,0:T(8,128)} %gen_ref) | copy-start | bytes 12292
  11.1 19.9 %copy-start.6 = (f32[2,48,128]{2,1,0:T(8,128)S(1)}, f32[2,48,128]{2,1,0:T(8,128)}, u32[]{:S(2)}) copy-start(f32[2,48,128]{2,1,0:T(8,128)} %constant.11.clone.fine_ref) | copy-start | bytes 147460
  11.1 19.9 %all-to-all-start = ((s32[64,1,128]{2,1,0:T(1,128)}), s32[64,1,128]{2,1,0:T(1,128)S(1)}, u32[]{:S(2)}, u32[]{:S(2)}) async-start(s32[64,1,128]{2,1,0:T(1,128)} %broadcast_in_dim.18), calls=%async_computation | async-start | bytes 65536 | tf_op jit(solution)/shard_map/all_to_all | solution.py:357
  31.0 0.9 %copy-start.3 = (f32[3,64,128]{2,1,0:T(8,128)S(1)}, f32[3,64,128]{2,1,0:T(8,128)}, u32[]{:S(2)}) copy-start(f32[3,64,128]{2,1,0:T(8,128)} %get-tuple-element.14.own_ref) | copy-start | bytes 294916
  38.9 3.9 %collective-permute-start.4 = (f32[32,128]{1,0:T(8,128)S(1)}, f32[32,128]{1,0:T(8,128)S(1)}, u32[]{:S(2)}, u32[]{:S(2)}) collective-permute-start(f32[32,128]{1,0:T(8,128)S(1)} %tile_gradient.1), channel_id=1, source_target_pairs={{0,12},{4,0},{8,4},{12,8},{16,28},{20,16},{24,20},{28,24},{32,44},... | collective-permute-start | bytes 49160 | tf_op jit(solution)/shard_map/ppermute | solution.py:360
  39.7 4.6 %collective-permute-start.3 = (f32[32,128]{1,0:T(8,128)S(1)}, f32[32,128]{1,0:T(8,128)S(1)}, u32[]{:S(2)}, u32[]{:S(2)}) collective-permute-start(f32[32,128]{1,0:T(8,128)S(1)} %tile_gradient.1), channel_id=1, source_target_pairs={{0,8},{4,12},{8,0},{12,4},{16,24},{20,28},{24,16},{28,20},{32,40},... | collective-permute-start | bytes 49160 | tf_op jit(solution)/shard_map/ppermute | solution.py:360
  41.1 5.5 %collective-permute-start.2 = (f32[32,128]{1,0:T(8,128)S(1)}, f32[32,128]{1,0:T(8,128)S(1)}, u32[]{:S(2)}, u32[]{:S(2)}) collective-permute-start(f32[32,128]{1,0:T(8,128)S(1)} %tile_gradient.1), channel_id=1, source_target_pairs={{0,4},{4,8},{8,12},{12,0},{16,20},{20,24},{24,28},{28,16},{32,36},... | collective-permute-start | bytes 49160 | tf_op jit(solution)/shard_map/ppermute | solution.py:360
  46.6 6.1 %copy-start.7 = (f32[2,32,128]{2,1,0:T(8,128)S(1)}, f32[2,32,128]{2,1,0:T(8,128)}, u32[]{:S(2)}) copy-start(f32[2,32,128]{2,1,0:T(8,128)} %constant.14.clone.fine_ref) | copy-start | bytes 98308
  47.7 5.0 %copy-start = (f32[64,4096]{1,0:T(8,128)S(1)}, f32[64,4096]{1,0:T(8,128)}, u32[]{:S(2)}) copy-start(f32[64,4096]{1,0:T(8,128)} %init_ref.1) | copy-start | bytes 3145732
  47.7 5.0 %copy-start.1 = (f32[64,4096]{1,0:T(8,128)S(1)}, f32[64,4096]{1,0:T(8,128)}, u32[]{:S(2)}) copy-start(f32[64,4096]{1,0:T(8,128)} %control_ref.1) | copy-start | bytes 3145732
  47.7 18.1 %all-to-all-start.1 = ((f32[16,4,32,128]{3,2,1,0:T(8,128)}), f32[16,4,32,128]{3,2,1,0:T(8,128)S(1)}, u32[]{:S(2)}, u32[]{:S(2)}) async-start(f32[16,4,32,128]{3,2,1,0:T(8,128)} %broadcast_in_dim.19), calls=%async_computation.1 | async-start | bytes 2097152 | tf_op jit(solution)/shard_map/all_to_all | solution.py:363
  52.8 0.8 %copy-start.8 = (f32[2,32,32]{2,1,0:T(8,128)S(1)}, f32[2,32,32]{2,1,0:T(8,128)}, u32[]{:S(2)}) copy-start(f32[2,32,32]{2,1,0:T(8,128)} %constant.13.clone.coarse_ref) | copy-start | bytes 24580

commit v4 on v3

--- a/solution.py
+++ b/solution.py
@@ -62,65 +62,82 @@
     return coarse.astype(np.float32), fine.astype(np.float32)
 
 
+def window_of(parts, tile):
+    line = jnp.concatenate(parts, axis=1)
+    even_part = line[:, 128 - HALO : 256 - HALO]
+    odd_part = line[:, 192 - HALO : 320 - HALO]
+    return jnp.where(lax.rem(tile, 2) == 1, odd_part, even_part)
+
+
+def edge_rows(rows):
+    odd = lax.rem(lax.axis_index("strip"), 2)
+    return pl.multiple_of((1 - odd) * (rows - 8), 8), pl.multiple_of(odd * (rows - 8), 8)
+
+
 def edges_kernel(*refs):
-    fields, (own, tail, head), near, wide, sems, wide_sems = refs[:3], refs[3:6], *refs[6:]
+    fields, (own, to_core, to_z, wide_to_core, wide_to_z), near, edge, sems, edge_sems = refs[:3], refs[3:8], *refs[8:]
     rows, width = fields[0].shape
     blocks = width // 128
     tile = lax.axis_index("samp")
+    firsts = edge_rows(rows)
+
+    def column_block(t, n):
+        block = lax.rem(t // 2 + (blocks - 1 + n), blocks)
+        return pl.ds(pl.multiple_of(block * 128, 128), 128)
+
     copies = []
-    for f in range(2):
-        for n, first in enumerate((rows - 8, 0)):
-            copies.append(pltpu.make_async_copy(fields[f].at[first : first + 8, :], wide.at[f, n], wide_sems.at[f, n]))
+    for n in range(2):
+        for f in range(3):
+            copies.append(pltpu.make_async_copy(fields[f].at[pl.ds(firsts[n], 8), :], edge.at[f, n], edge_sems.at[f, n]))
     for f in range(3):
         for n in range(3):
-            block = lax.rem(tile // 2 + (blocks - 1 + n), blocks)
-            columns = pl.ds(pl.multiple_of(block * 128, 128), 128)
-            copies.append(pltpu.make_async_copy(fields[f].at[:, columns], near.at[f, n], sems.at[f, n]))
+            copies.append(pltpu.make_async_copy(fields[f].at[:, column_block(tile, n)], near.at[f, n], sems.at[f, n]))
     for copy in copies:
         copy.start()
     for copy in copies:
         copy.wait()
+
+    odd = lax.rem(lax.axis_index("strip"), 2)
+    for f in range(3):
+        own[f] = window_of([near[f, n] for n in range(3)], tile)
+        for n, (out, partner) in enumerate(((to_core, tile), (to_z, tile ^ 2))):
+            out[f] = window_of([edge[f, n, :, column_block(partner, m)] for m in range(3)], tile)
     row = lax.broadcasted_iota(jnp.int32, (8, 128), 0)
-    for b in range(blocks):
-        columns = slice(128 * b, 128 * b + 128)
-        tail[b] = jnp.where(row >= 8 - STEPS, wide[0, 0, :, columns], pltpu.roll(wide[1, 0, :, columns], 5, 0))
-        head[b] = jnp.where(row < STEPS, wide[0, 1, :, columns], pltpu.roll(wide[1, 1, :, columns], 3, 0))
-    odd = lax.rem(tile, 2) == 1
-    for f in range(3):
-        line = jnp.concatenate([near[f, n] for n in range(3)], axis=1)
-        even_part = line[:, 128 - HALO : 256 - HALO]
-        odd_part = line[:, 192 - HALO : 320 - HALO]
-        part = jnp.where(odd, odd_part, even_part)
-        own[f] = part
-        tail[blocks + f] = part[-8:]
-        head[blocks + f] = part[:8]
-
-
-def own_edges(fields):
+    for n, out in enumerate((wide_to_core, wide_to_z)):
+        is_tail = odd == n
+        is_state = jnp.where(is_tail, row, 7 - row) >= 8 - STEPS
+        for b in range(blocks):
+            columns = slice(128 * b, 128 * b + 128)
+            source = edge[1, n, :, columns]
+            moved = jnp.where(is_tail, pltpu.roll(source, 5, 0), pltpu.roll(source, 3, 0))
+            out[b] = jnp.where(is_state, edge[0, n, :, columns], moved)
+
+
+def strip_edges(fields):
     rows, width = fields[0].shape
     vmem = pl.BlockSpec(memory_space=pltpu.VMEM)
-    payload = jax.ShapeDtypeStruct((width // 128 + 3, 8, 128), jnp.float32)
+    shapes = [(3, rows, 128), (3, 8, 128), (3, 8, 128), (width // 128, 8, 128), (width // 128, 8, 128)]
     return pl.pallas_call(
         edges_kernel,
-        out_shape=[jax.ShapeDtypeStruct((3, rows, 128), jnp.float32), payload, payload],
+        out_shape=[jax.ShapeDtypeStruct(shape, jnp.float32) for shape in shapes],
         in_specs=[pl.BlockSpec(memory_space=pl.ANY)] * 3,
-        out_specs=[vmem] * 3,
+        out_specs=[vmem] * 5,
         scratch_shapes=[
             pltpu.VMEM((3, 3, rows, 128), jnp.float32),
-            pltpu.VMEM((2, 2, 8, width), jnp.float32),
+            pltpu.VMEM((3, 2, 8, width), jnp.float32),
             pltpu.SemaphoreType.DMA((3, 3)),
-            pltpu.SemaphoreType.DMA((2, 2)),
+            pltpu.SemaphoreType.DMA((3, 2)),
         ],
         compiler_params=pltpu.CompilerParams(vmem_limit_bytes=56 * 2**20),
-        name="own_edges",
+        name="strip_edges",
     )(*fields)
 
 
-def tile_kernel(points_ref, gen_ref, coarse_ref, fine_ref, row_ref, above_ref, own_ref, below_ref, out_ref, inner_ref, kx_ref, ky_ref, v_ref, g_ref, t_ref, s_ref):
+def tile_kernel(points_ref, gen_ref, coarse_ref, fine_ref, row_ref, core_ref, own_ref, z_ref, out_ref, inner_ref, kx_ref, ky_ref, v_ref, g_ref, t_ref, s_ref):
     f32 = jnp.float32
     lane = lax.broadcasted_iota(jnp.int32, (1, 128), 1)
     left = lane < SAMPLES
-    edge = above_ref.shape[0] - 3
+    odd = lax.rem(lax.axis_index("strip"), 2) == 1
     tile = lax.axis_index("samp")
     sines = coarse_ref[0, pl.ds(tile, 1), :] * fine_ref[1] + coarse_ref[1, pl.ds(tile, 1), :] * fine_ref[0]
     high, low = split(sines)
@@ -140,7 +157,8 @@
 
     start_fields = []
     for f in range(3):
-        x = jnp.concatenate([above_ref[edge + f], own_ref[f], below_ref[edge + f]], axis=0)
+        core, far = core_ref[f], z_ref[f]
+        x = jnp.concatenate([jnp.where(odd, core, far), own_ref[f], jnp.where(odd, far, core)], axis=0)
         start_fields.append(x * DT if f == 1 else x)
     before = jnp.zeros((TALL, 128), f32)
     for j in range(COLS):
@@ -184,7 +202,7 @@
 
     for t, body in enumerate((state_step, state_step, last_state_step, first_costate_step)):
         start, low_j, high_j = sweep(t + 1, body)
-        lax.fori_loop(low_j, high_j, body, start, unroll=2)
+        lax.fori_loop(low_j, high_j, body, start, unroll=8)
 
     source = lax.broadcasted_iota(jnp.int32, (256, 128), 0) % 128 // SAMPLES
     place = lax.broadcasted_iota(jnp.int32, (256, 128), 1) // HALF % 2
@@ -198,7 +216,7 @@
         return jnp.where(lane % HALF == j - HALO, sums, total), after
 
     start, low_j, high_j = sweep(HALO, last_costate_step)
-    total, _ = lax.fori_loop(low_j, high_j, last_costate_step, (jnp.zeros((TILE, 128), f32), start), unroll=16)
+    total, _ = lax.fori_loop(low_j, high_j, last_costate_step, (jnp.zeros((TILE, 128), f32), start), unroll=32)
 
     total = jnp.where(left, total[:HALF], total[HALF:])
     control = own_ref[1]
@@ -217,7 +235,7 @@
         out_specs=pl.BlockSpec(memory_space=pltpu.VMEM),
         scratch_shapes=[pltpu.VMEM((48 * MODES, 128), jnp.float32)] + [big] * 6,
         compiler_params=pltpu.CompilerParams(vmem_limit_bytes=40 * 2**20),
-        cost_estimate=pl.CostEstimate(flops=400_000_000, bytes_accessed=400_000, transcendentals=430_000),
+        cost_estimate=pl.CostEstimate(flops=4_000_000_000, bytes_accessed=20_000_000, transcendentals=430_000),
         name="tile_gradient",
     )(*args)
 
@@ -227,8 +245,8 @@
     z = lax.rem(lax.axis_index("samp"), 4)
     for m in range(SAMPLES // 2):
         near = 4 * (m // 2)
-        a = tiles_ref[near + lax.rem(z + (4 - 2 * m % 4), 4)]
-        b = tiles_ref[near + lax.rem(z + (3 - 2 * m % 4), 4)]
+        a = tiles_ref[near + (z ^ (2 * m % 4))]
+        b = tiles_ref[near + (z ^ (2 * m % 4 + 1))]
         out_ref[:HALF, 128 * m : 128 * m + 128] = jnp.where(left, a, pltpu.roll(b, TILE, 1))
         out_ref[HALF:, 128 * m : 128 * m + 128] = jnp.where(left, pltpu.roll(a, TILE, 1), b)
 
@@ -244,7 +262,7 @@
     )(tiles)
 
 
-def state_kernel(point_ref, gen_ref, row_ref, coarse_ref, fine_ref, init_ref, control_ref, before_ref, after_ref, out_ref, kx_ref, ky_ref, g_ref, v_ref, w_ref):
+def state_kernel(point_ref, gen_ref, row_ref, coarse_ref, fine_ref, init_ref, control_ref, core_ref, z_ref, out_ref, kx_ref, ky_ref, g_ref, v_ref, w_ref):
     f32 = jnp.float32
     blocks = v_ref.shape[0]
     lane = lax.broadcasted_iota(jnp.int32, (1, 128), 1)
@@ -256,6 +274,7 @@
 
     rows, above = out_ref.shape[0], 8
     row_parts = rows_of_strip(row_ref)
+    odd = lax.rem(lax.axis_index("strip"), 2) == 1
 
     def to_left(value):
         return pltpu.roll(value, 127, 1)
@@ -279,7 +298,8 @@
             kx_ref[b - 1] = before_k + jnp.where(last, shifted, before_shifted)
         before_k, before_shifted = k, shifted
         columns = slice(128 * b, 128 * b + 128)
-        lead, trail = before_ref[b], after_ref[b]
+        core, far = core_ref[b], z_ref[b]
+        lead, trail = jnp.where(odd, core, far), jnp.where(odd, far, core)
         v_ref[b] = jnp.concatenate([lead, init_ref[:, columns], trail], axis=0)
         g_ref[b] = DT * jnp.concatenate([pltpu.roll(lead, 3, 0), control_ref[:, columns], pltpu.roll(trail, 5, 0)], axis=0)
     kx_ref[blocks - 1] = before_k + jnp.where(last, first_shifted, before_shifted)
@@ -300,7 +320,7 @@
             write(b, new + g_ref[b])
             return following, following_shifted, flux_shifted
 
-        lax.fori_loop(0, blocks, step, start, unroll=2)
+        lax.fori_loop(0, blocks, step, start, unroll=8)
 
     def keep(ref):
         def write(b, value):
@@ -315,7 +335,7 @@
     sweep(v_ref, finish)
 
 
-def own_final_state(point_index, generator, row_table, initial_state, control, before, after):
+def own_final_state(point_index, generator, row_table, initial_state, control, from_core, from_z):
     rows, width = initial_state.shape
     blocks = width // 128
     turns = 2.0 * np.pi / width * RANKS[:, None]
@@ -334,36 +354,37 @@
         compiler_params=pltpu.CompilerParams(vmem_limit_bytes=40 * 2**20),
         cost_estimate=pl.CostEstimate(flops=2_000_000_000, bytes_accessed=3_500_000, transcendentals=330_000),
         name="own_final_state",
-    )(point_index, generator, row_table, coarse, fine, initial_state, control, before, after)
-
-
-RING_UP = [(i, (i + 1) % 4) for i in range(4)]
-RING_DOWN = [(j, i) for i, j in RING_UP]
-
-
-def z_shift(step):
-    return [(i, i // 4 * 4 + (i + step) % 4) for i in range(64)]
+    )(point_index, generator, row_table, coarse, fine, initial_state, control, from_core, from_z)
+
+
+CORES = [(s * 4 + k, s * 4 + (k ^ 1)) for s in range(64) for k in range(4)]
+ACROSS = [(s * 4 + k, (s ^ 2) * 4 + 3 - k) for s in range(64) for k in range(4)]
+
+
+def z_partner(other):
+    return [(i, i ^ other) for i in range(64)]
 
 
 def on_device(initial_state, target, control, point_index, generator):
     rows, width = initial_state.shape
     row_table = row_tables(rows * lax.axis_size("strip"))
 
-    own, tail, head = own_edges((initial_state, control, target))
-    point_index, tail, head = lax.optimization_barrier((point_index, tail, head))
-    above = lax.ppermute(tail, "strip", RING_UP)
-    below = lax.ppermute(head, "strip", RING_DOWN)
+    both = ("samp", "strip")
+    own, to_core, to_z, wide_to_core, wide_to_z = strip_edges((initial_state, control, target))
+    core, far = lax.ppermute(to_core, both, CORES), lax.ppermute(to_z, both, ACROSS)
+    core_wide, far_wide = lax.ppermute(wide_to_core, both, CORES), lax.ppermute(wide_to_z, both, ACROSS)
     points = jnp.broadcast_to(point_index[:, None, None], (SAMPLES, 1, 128))
     points = lax.all_to_all(points, "samp", 0, 0, tiled=True).reshape(SAMPLES, 128)
-    mine = tile_gradient(points, generator.T, *tile_col_tables(width), row_table, above, own, below)
-
-    tiles = jnp.stack([mine] + [lax.ppermute(mine, "samp", z_shift(k)) for k in (1, 2, 3)])
+    mine = tile_gradient(points, generator.T, *tile_col_tables(width), row_table, core, own, far)
+
+    mine, core_wide, far_wide = lax.optimization_barrier((mine, core_wide, far_wide))
+    tiles = jnp.stack([mine] + [lax.ppermute(mine, "samp", z_partner(k)) for k in (1, 2, 3)])
     tiles = jnp.broadcast_to(tiles[None], (16, 4, HALF, 128))
     tiles, generator = lax.optimization_barrier((tiles, generator))
     tiles = lax.all_to_all(tiles, "samp", 0, 0, axis_index_groups=ALONG_XY, tiled=True)
     new_control = assemble(tiles.reshape(SAMPLES, HALF, 128))
 
-    state = own_final_state(point_index, generator, row_table, initial_state, control, above, below)
+    state = own_final_state(point_index, generator, row_table, initial_state, control, core_wide, far_wide)
     return (new_control, state[None])
 
 

time: 67.7 us -> 63.3 us (0.935)
  Pallas kernels: 23 us -> 18.5 us
  starting transfers between devices: 25.5 us -> 29 us
  waiting for transfers between devices: 13.8 us -> 10.6 us
    all_to_all x1, waiting for transfers between devices: 8.75 us -> 0.04 us  [on_device(): lax.all_to_all(points, 'samp', 0, 0, tiled=True).reshape(SAMPLES, 128)]
    all_to_all x1, waiting for transfers between devices: 0.01 us -> 5.42 us  [on_device(): lax.all_to_all(tiles, 'samp', 0, 0, axis_index_groups=ALONG_XY, tiled=True)]
    pallas_call x1, Pallas kernels: 12.3 us -> 8.14 us  [own_final_state(): pl.pallas_call(state_kernel, out_shape=jax.ShapeDtypeStruct((rows, width)...]
    all_to_all x1, starting transfers between devices: 4.99 us -> 7.52 us  [on_device(): lax.all_to_all(tiles, 'samp', 0, 0, axis_index_groups=ALONG_XY, tiled=True)]
    all_to_all x1, starting transfers between devices: 11.1 us -> 12 us  [on_device(): lax.all_to_all(points, 'samp', 0, 0, tiled=True).reshape(SAMPLES, 128)]
    ppermute x5 -> x7, starting transfers between devices: 9.42 us -> 9.5 us  [the longest x3 4.61 us: on_device(): lax.ppermute(mine, 'samp', z_partner(k))]
    ppermute x5 -> x7, waiting for transfers between devices: 5.05 us -> 5.1 us  [the longest x3 3.73 us: on_device(): lax.ppermute(mine, 'samp', z_partner(k))]
  transfers between devices with their start and end apart: 7 -> 9, of which waited for: 4 -> 5; matrix products, arithmetic and copies ran while one was open for 1% -> 0% of each run, Pallas kernels for 18% -> 27%
where the time goes in v4:
time: 63.3 us; the launch traced here: 63 us
  starting transfers between devices  29 us (46%)
  Pallas kernels  18.5 us (29%)
  waiting for transfers between devices  10.6 us (17%)
  local copies, waits for them, and re-layouts  3.48 us (5%)
  between operations  1.41 us (2%)
    all_to_all x1, starting transfers between devices, on_device(): lax.all_to_all(points, 'samp', 0, 0, tiled=True).reshape(SAMPLES, 128)  12 us
    pallas_call x1, Pallas kernels, own_final_state(): pl.pallas_call(state_kernel, out_shape=jax.ShapeDtypeStruct((rows, width)...  8.14 us
    all_to_all x1, starting transfers between devices, on_device(): lax.all_to_all(tiles, 'samp', 0, 0, axis_index_groups=ALONG_XY, tiled=True)  7.52 us
    pallas_call x1, Pallas kernels, tile_gradient(): pl.pallas_call(tile_kernel, out_shape=jax.ShapeDtypeStruct((HALF, 128), j...  6.68 us
    all_to_all x1, waiting for transfers between devices, on_device(): lax.all_to_all(tiles, 'samp', 0, 0, axis_index_groups=ALONG_XY, tiled=True)  5.42 us
    ppermute x3, starting transfers between devices, on_device(): lax.ppermute(mine, 'samp', z_partner(k))  4.61 us
    ppermute x1, starting transfers between devices, on_device(): lax.ppermute(to_z, both, ACROSS)  4.61 us
    ppermute x3, waiting for transfers between devices, on_device(): lax.ppermute(mine, 'samp', z_partner(k))  3.73 us
  transfers between devices with their start and end apart: 9, of which 5 were waited for; matrix products, arithmetic and copies ran while one was open for 0% of the time, Pallas kernels for 27%

profile of v4, /device:TPU:8, one launch (start us, length us, event | category | flops | bytes accessed | tf_op | source)
XLA Modules:
  0.0 63.0 jit_solution(12696762328712671377)
XLA Ops:
  1.3 0.6 %broadcast_in_dim.18 = s32[64,1,128]{2,1,0:T(1,128)} broadcast(s32[]{:T(128)} %bitcast.9), dimensions={} | broadcast | bytes 32772 | tf_op jit(solution)/shard_map/broadcast_in_dim | solution.py:376
  1.9 12.0 %all-to-all-start = ((s32[64,1,128]{2,1,0:T(1,128)}), s32[64,1,128]{2,1,0:T(1,128)S(1)}, u32[]{:S(2)}, u32[]{:S(2)}) async-start(s32[64,1,128]{2,1,0:T(1,128)} %broadcast_in_dim.18), calls=%async_computation | async-start | bytes 65536 | tf_op jit(solution)/shard_map/all_to_all | solution.py:377
  13.9 0.0 copy-start.2
  13.9 0.0 copy-start.4
  13.9 0.0 copy-start.5
  13.9 0.0 copy-start.6
  14.0 2.4 %strip_edges.1 = (f32[3,64,128]{2,1,0:T(8,128)}, f32[3,8,128]{2,1,0:T(8,128)}, f32[3,8,128]{2,1,0:T(8,128)}, f32[32,8,128]{2,1,0:T(8,128)}, f32[32,8,128]{2,1,0:T(8,128)}) custom-call(f32[64,4096]{1,0:T(8,128)} %init_ref.1, f32[64,4096]{1,0:T(8,128)} %control_ref.1, f32[64,4096]{1,0:T(8,128)} %refs_2_.1), custom_call_target="tpu_custom_call" | custom-call | tf_op jit(solution)/shard_map/strip_edges/pallas_call | solution.py:120
  16.4 0.1 collective-permute-start
  16.5 4.6 %collective-permute-start.1 = (f32[3,8,128]{2,1,0:T(8,128)}, f32[3,8,128]{2,1,0:T(8,128)S(1)}, u32[]{:S(2)}, u32[]{:S(2)}) collective-permute-start(f32[3,8,128]{2,1,0:T(8,128)} %get-tuple-element.14), channel_id=1, source_target_pairs={{0,11},{1,10},{2,9},{3,8},{4,15},{5,14},{6,13},{7,12},{8,3},{9,2},... | collective-permute-start | bytes 36872 | tf_op jit(solution)/shard_map/ppermute | solution.py:374
  21.1 0.1 collective-permute-start.2
  21.2 0.1 collective-permute-start.3
  21.3 0.0 copy-done.2
  21.3 0.1 copy.13
  21.3 0.0 collective-permute-done.core_ref
  21.3 1.4 %collective-permute-done.1.z_ref = f32[3,8,128]{2,1,0:T(8,128)S(1)} collective-permute-done((f32[3,8,128]{2,1,0:T(8,128)}, f32[3,8,128]{2,1,0:T(8,128)S(1)}, u32[]{:S(2)}, u32[]{:S(2)}) %collective-permute-start.1) | collective-permute-done | bytes 12320 | tf_op jit(solution)/shard_map/ppermute | solution.py:374
  22.7 0.0 all-to-all-done
  22.7 0.0 copy-done.4
  22.7 0.0 copy-done.5
  22.8 0.0 copy-done.6
  22.8 0.0 copy-start.3
  22.8 0.9 %copy-done.3 = f32[3,64,128]{2,1,0:T(8,128)S(1)} copy-done((f32[3,64,128]{2,1,0:T(8,128)S(1)}, f32[3,64,128]{2,1,0:T(8,128)}, u32[]{:S(2)}) %copy-start.3) | copy-done | bytes 98328
  23.6 6.7 %tile_gradient.1 = f32[32,128]{1,0:T(8,128)S(1)} custom-call(s32[64,128]{1,0:T(8,128)S(1)} %bitcast.11, s32[32,32]{1,0:T(8,128)S(1)} %bitcast.12, f32[2,64,128]{2,1,0:T(8,128)S(1)} %copy-done.5, f32[2,48,128]{2,1,0:T(8,128)S(1)} %copy-done.6, bf16[272,96]{1,0:T(8,128)(2,1)S(1)} %copy-done.4, f32[3,8,128]{2,1,0:T(8,128)S(1)} %collective-permute-done.core_ref, ...), custom_call_target="tpu_custom_call" | custom-call | flops 4000000000 | bytes 20000000 | tf_op jit(solution)/shard_map/tile_gradient/pallas_call | solution.py:231
  30.3 0.0 collective-permute-done.2.core_ref
  30.3 0.0 collective-permute-done.3.z_ref
  30.4 2.6 %collective-permute-start.6 = (f32[32,128]{1,0:T(8,128)S(1)}, f32[32,128]{1,0:T(8,128)S(1)}, u32[]{:S(2)}, u32[]{:S(2)}) collective-permute-start(f32[32,128]{1,0:T(8,128)S(1)} %tile_gradient.1), channel_id=1, source_target_pairs={{0,12},{4,8},{8,4},{12,0},{16,28},{20,24},{24,20},{28,16},{32,44},... | collective-permute-start | bytes 49160 | tf_op jit(solution)/shard_map/ppermute | solution.py:381
  33.0 2.0 %collective-permute-start.5 = (f32[32,128]{1,0:T(8,128)S(1)}, f32[32,128]{1,0:T(8,128)S(1)}, u32[]{:S(2)}, u32[]{:S(2)}) collective-permute-start(f32[32,128]{1,0:T(8,128)S(1)} %tile_gradient.1), channel_id=1, source_target_pairs={{0,8},{4,12},{8,0},{12,4},{16,24},{20,28},{24,16},{28,20},{32,40},... | collective-permute-start | bytes 49160 | tf_op jit(solution)/shard_map/ppermute | solution.py:381
  35.0 0.0 collective-permute-start.4
  35.0 1.0 %collective-permute-done.6 = f32[32,128]{1,0:T(8,128)S(1)} collective-permute-done((f32[32,128]{1,0:T(8,128)S(1)}, f32[32,128]{1,0:T(8,128)S(1)}, u32[]{:S(2)}, u32[]{:S(2)}) %collective-permute-start.6) | collective-permute-done | bytes 16416 | tf_op jit(solution)/shard_map/ppermute | solution.py:381
  36.0 1.8 %collective-permute-done.5 = f32[32,128]{1,0:T(8,128)S(1)} collective-permute-done((f32[32,128]{1,0:T(8,128)S(1)}, f32[32,128]{1,0:T(8,128)S(1)}, u32[]{:S(2)}, u32[]{:S(2)}) %collective-permute-start.5) | collective-permute-done | bytes 16416 | tf_op jit(solution)/shard_map/ppermute | solution.py:381
  37.8 0.9 %collective-permute-done.4 = f32[32,128]{1,0:T(8,128)S(1)} collective-permute-done((f32[32,128]{1,0:T(8,128)S(1)}, f32[32,128]{1,0:T(8,128)S(1)}, u32[]{:S(2)}, u32[]{:S(2)}) %collective-permute-start.4) | collective-permute-done | bytes 16416 | tf_op jit(solution)/shard_map/ppermute | solution.py:381
  38.7 0.0 copy-start.7
  38.7 1.1 %broadcast_in_dim.19 = f32[16,4,32,128]{3,2,1,0:T(8,128)} broadcast(f32[4,32,128]{2,1,0:T(8,128)S(1)} %pad_maximum_fusion), dimensions={1,2,3} | broadcast | bytes 1114112 | tf_op jit(solution)/shard_map/broadcast_in_dim | solution.py:382
  39.8 0.0 copy-start
  39.8 0.0 copy-start.1
  39.8 7.5 %all-to-all-start.1 = ((f32[16,4,32,128]{3,2,1,0:T(8,128)}), f32[16,4,32,128]{3,2,1,0:T(8,128)S(1)}, u32[]{:S(2)}, u32[]{:S(2)}) async-start(f32[16,4,32,128]{3,2,1,0:T(8,128)} %broadcast_in_dim.19), calls=%async_computation.1 | async-start | bytes 2097152 | tf_op jit(solution)/shard_map/all_to_all | solution.py:384
  47.3 0.0 copy-done.7
  47.3 0.0 copy-done
  47.4 0.0 copy-done.1
  47.4 0.0 copy-start.8
  47.4 0.7 %copy-done.8 = f32[2,32,32]{2,1,0:T(8,128)S(1)} copy-done((f32[2,32,32]{2,1,0:T(8,128)S(1)}, f32[2,32,32]{2,1,0:T(8,128)}, u32[]{:S(2)}) %copy-start.8) | copy-done | bytes 8216
  48.1 8.1 %own_final_state.1 = f32[64,4096]{1,0:T(8,128)} custom-call(s32[1]{0:T(128)} %copy.14.point_ref, s32[32,32]{1,0:T(8,128)S(1)} %copy-done.2, bf16[272,96]{1,0:T(8,128)(2,1)S(1)} %copy-done.4, f32[2,32,32]{2,1,0:T(8,128)S(1)} %copy-done.8, f32[2,32,128]{2,1,0:T(8,128)S(1)} %copy-done.7, f32[64,4096]{1,0:T(8,128)S(1)} %copy-done, f32[64,4096]{1,0:T(8,128)S(1)} %copy-done.1, ...), custom_call_target="tpu_custom_call" | custom-call | flops 2000000000 | bytes 3500000 | tf_op jit(solution)/shard_map/own_final_state/pallas_call | solution.py:348
  56.3 5.4 %all-to-all-done.1 = f32[16,4,32,128]{3,2,1,0:T(8,128)S(1)} async-done(((f32[16,4,32,128]{3,2,1,0:T(8,128)}), f32[16,4,32,128]{3,2,1,0:T(8,128)S(1)}, u32[]{:S(2)}, u32[]{:S(2)}) %all-to-all-start.1) | async-done | bytes 1048608 | tf_op jit(solution)/shard_map/all_to_all | solution.py:384
  61.7 1.3 %assemble.1 = f32[64,4096]{1,0:T(8,128)} custom-call(f32[64,32,128]{2,1,0:T(8,128)S(1)} %bitcast.10), custom_call_target="tpu_custom_call" | custom-call | tf_op jit(solution)/shard_map/assemble/pallas_call | solution.py:255
  (1 shorter events, 0.0 us)
Async XLA Ops:
  1.9 20.8 %all-to-all-start = ((s32[64,1,128]{2,1,0:T(1,128)}), s32[64,1,128]{2,1,0:T(1,128)S(1)}, u32[]{:S(2)}, u32[]{:S(2)}) async-start(s32[64,1,128]{2,1,0:T(1,128)} %broadcast_in_dim.18), calls=%async_computation | async-start | bytes 65536 | tf_op jit(solution)/shard_map/all_to_all | solution.py:377
  13.9 7.4 %copy-start.2 = (s32[32,32]{1,0:T(8,128)S(1)}, s32[32,32]{1,0:T(8,128)}, u32[]{:S(2)}) copy-start(s32[32,32]{1,0:T(8,128)} %gen_ref) | copy-start | bytes 12292
  13.9 8.8 %copy-start.4 = (bf16[272,96]{1,0:T(8,128)(2,1)S(1)}, bf16[272,96]{1,0:T(8,128)(2,1)}, u32[]{:S(2)}) copy-start(bf16[272,96]{1,0:T(8,128)(2,1)} %constant.12.clone.row_ref) | copy-start | bytes 156676
  13.9 8.8 %copy-start.5 = (f32[2,64,128]{2,1,0:T(8,128)S(1)}, f32[2,64,128]{2,1,0:T(8,128)}, u32[]{:S(2)}) copy-start(f32[2,64,128]{2,1,0:T(8,128)} %constant.10.clone.coarse_ref) | copy-start | bytes 196612
  13.9 8.8 %copy-start.6 = (f32[2,48,128]{2,1,0:T(8,128)S(1)}, f32[2,48,128]{2,1,0:T(8,128)}, u32[]{:S(2)}) copy-start(f32[2,48,128]{2,1,0:T(8,128)} %constant.11.clone.fine_ref) | copy-start | bytes 147460
  16.4 5.0 %collective-permute-start = (f32[3,8,128]{2,1,0:T(8,128)}, f32[3,8,128]{2,1,0:T(8,128)S(1)}, u32[]{:S(2)}, u32[]{:S(2)}) collective-permute-start(f32[3,8,128]{2,1,0:T(8,128)} %get-tuple-element.12), channel_id=1, source_target_pairs={{0,1},{1,0},{2,3},{3,2},{4,5},{5,4},{6,7},{7,6},{8,9},{9,8},{10,11... | collective-permute-start | bytes 36872 | tf_op jit(solution)/shard_map/ppermute | solution.py:374
  16.5 6.2 %collective-permute-start.1 = (f32[3,8,128]{2,1,0:T(8,128)}, f32[3,8,128]{2,1,0:T(8,128)S(1)}, u32[]{:S(2)}, u32[]{:S(2)}) collective-permute-start(f32[3,8,128]{2,1,0:T(8,128)} %get-tuple-element.14), channel_id=1, source_target_pairs={{0,11},{1,10},{2,9},{3,8},{4,15},{5,14},{6,13},{7,12},{8,3},{9,2},... | collective-permute-start | bytes 36872 | tf_op jit(solution)/shard_map/ppermute | solution.py:374
  21.1 9.2 %collective-permute-start.2 = (f32[32,8,128]{2,1,0:T(8,128)}, f32[32,8,128]{2,1,0:T(8,128)S(1)}, u32[]{:S(2)}, u32[]{:S(2)}) collective-permute-start(f32[32,8,128]{2,1,0:T(8,128)} %get-tuple-element.15), channel_id=1, source_target_pairs={{0,1},{1,0},{2,3},{3,2},{4,5},{5,4},{6,7},{7,6},{8,9},{9,8},{10,11... | collective-permute-start | bytes 393224 | tf_op jit(solution)/shard_map/ppermute | solution.py:375
  21.2 9.2 %collective-permute-start.3 = (f32[32,8,128]{2,1,0:T(8,128)}, f32[32,8,128]{2,1,0:T(8,128)S(1)}, u32[]{:S(2)}, u32[]{:S(2)}) collective-permute-start(f32[32,8,128]{2,1,0:T(8,128)} %get-tuple-element.16), channel_id=1, source_target_pairs={{0,11},{1,10},{2,9},{3,8},{4,15},{5,14},{6,13},{7,12},{8,3},{9,2},... | collective-permute-start | bytes 393224 | tf_op jit(solution)/shard_map/ppermute | solution.py:375
  22.8 0.9 %copy-start.3 = (f32[3,64,128]{2,1,0:T(8,128)S(1)}, f32[3,64,128]{2,1,0:T(8,128)}, u32[]{:S(2)}) copy-start(f32[3,64,128]{2,1,0:T(8,128)} %get-tuple-element.13.own_ref) | copy-start | bytes 294916
  30.4 5.6 %collective-permute-start.6 = (f32[32,128]{1,0:T(8,128)S(1)}, f32[32,128]{1,0:T(8,128)S(1)}, u32[]{:S(2)}, u32[]{:S(2)}) collective-permute-start(f32[32,128]{1,0:T(8,128)S(1)} %tile_gradient.1), channel_id=1, source_target_pairs={{0,12},{4,8},{8,4},{12,0},{16,28},{20,24},{24,20},{28,16},{32,44},... | collective-permute-start | bytes 49160 | tf_op jit(solution)/shard_map/ppermute | solution.py:381
  33.0 4.8 %collective-permute-start.5 = (f32[32,128]{1,0:T(8,128)S(1)}, f32[32,128]{1,0:T(8,128)S(1)}, u32[]{:S(2)}, u32[]{:S(2)}) collective-permute-start(f32[32,128]{1,0:T(8,128)S(1)} %tile_gradient.1), channel_id=1, source_target_pairs={{0,8},{4,12},{8,0},{12,4},{16,24},{20,28},{24,16},{28,20},{32,40},... | collective-permute-start | bytes 49160 | tf_op jit(solution)/shard_map/ppermute | solution.py:381
  35.0 3.7 %collective-permute-start.4 = (f32[32,128]{1,0:T(8,128)S(1)}, f32[32,128]{1,0:T(8,128)S(1)}, u32[]{:S(2)}, u32[]{:S(2)}) collective-permute-start(f32[32,128]{1,0:T(8,128)S(1)} %tile_gradient.1), channel_id=1, source_target_pairs={{0,4},{4,0},{8,12},{12,8},{16,20},{20,16},{24,28},{28,24},{32,36},... | collective-permute-start | bytes 49160 | tf_op jit(solution)/shard_map/ppermute | solution.py:381
  38.7 8.6 %copy-start.7 = (f32[2,32,128]{2,1,0:T(8,128)S(1)}, f32[2,32,128]{2,1,0:T(8,128)}, u32[]{:S(2)}) copy-start(f32[2,32,128]{2,1,0:T(8,128)} %constant.14.clone.fine_ref) | copy-start | bytes 98308
  39.8 7.5 %copy-start = (f32[64,4096]{1,0:T(8,128)S(1)}, f32[64,4096]{1,0:T(8,128)}, u32[]{:S(2)}) copy-start(f32[64,4096]{1,0:T(8,128)} %init_ref.1) | copy-start | bytes 3145732
  39.8 7.5 %copy-start.1 = (f32[64,4096]{1,0:T(8,128)S(1)}, f32[64,4096]{1,0:T(8,128)}, u32[]{:S(2)}) copy-start(f32[64,4096]{1,0:T(8,128)} %control_ref.1) | copy-start | bytes 3145732
  39.8 21.9 %all-to-all-start.1 = ((f32[16,4,32,128]{3,2,1,0:T(8,128)}), f32[16,4,32,128]{3,2,1,0:T(8,128)S(1)}, u32[]{:S(2)}, u32[]{:S(2)}) async-start(f32[16,4,32,128]{3,2,1,0:T(8,128)} %broadcast_in_dim.19), calls=%async_computation.1 | async-start | bytes 2097152 | tf_op jit(solution)/shard_map/all_to_all | solution.py:384
  47.4 0.8 %copy-start.8 = (f32[2,32,32]{2,1,0:T(8,128)S(1)}, f32[2,32,32]{2,1,0:T(8,128)}, u32[]{:S(2)}) copy-start(f32[2,32,32]{2,1,0:T(8,128)} %constant.13.clone.coarse_ref) | copy-start | bytes 24580

commit v5 on v4

--- a/solution.py
+++ b/solution.py
@@ -17,11 +17,6 @@
 HALF = TILE // 2
 COLS = HALF + 2 * HALO
 TALL = TILE + 16
-
-SAMP = np.arange(64).reshape(4, 4, 4)
-ALONG_Z = SAMP.reshape(16, 4).tolist()
-ALONG_XY = SAMP.transpose(2, 0, 1).reshape(4, 16).tolist()
-
 
 RANKS = np.arange(1, MODES + 1)
 BY_RANK = (1.0 / np.sqrt(RANKS)).astype(np.float32)
@@ -240,26 +235,30 @@
     )(*args)
 
 
-def assemble_kernel(tiles_ref, out_ref):
+def assemble_kernel(*refs):
+    parts, out_ref = refs[:4], refs[4]
     left = lax.broadcasted_iota(jnp.int32, (1, 128), 1) < TILE
-    z = lax.rem(lax.axis_index("samp"), 4)
-    for m in range(SAMPLES // 2):
-        near = 4 * (m // 2)
-        a = tiles_ref[near + (z ^ (2 * m % 4))]
-        b = tiles_ref[near + (z ^ (2 * m % 4 + 1))]
-        out_ref[:HALF, 128 * m : 128 * m + 128] = jnp.where(left, a, pltpu.roll(b, TILE, 1))
-        out_ref[HALF:, 128 * m : 128 * m + 128] = jnp.where(left, pltpu.roll(a, TILE, 1), b)
-
-
-def assemble(tiles):
+    tile = lax.axis_index("samp")
+    x, y, z = tile // 16, lax.rem(tile // 4, 4), lax.rem(tile, 4)
+    for kx in range(4):
+        for pair in range(8):
+            to_y, to_z = pair // 2, pair % 2 * 2
+            a = parts[kx][y ^ to_y, z ^ to_z]
+            b = parts[kx][y ^ to_y, z ^ (to_z + 1)]
+            first = pl.multiple_of(((x ^ kx) * 8 + pair) * 128, 128)
+            out_ref[:HALF, pl.ds(first, 128)] = jnp.where(left, a, pltpu.roll(b, TILE, 1))
+            out_ref[HALF:, pl.ds(first, 128)] = jnp.where(left, pltpu.roll(a, TILE, 1), b)
+
+
+def assemble(parts):
     return pl.pallas_call(
         assemble_kernel,
         out_shape=jax.ShapeDtypeStruct((TILE, SAMPLES * TILE), jnp.float32),
-        in_specs=[pl.BlockSpec(memory_space=pltpu.VMEM)],
+        in_specs=[pl.BlockSpec(memory_space=pltpu.VMEM)] * 4,
         out_specs=pl.BlockSpec(memory_space=pltpu.VMEM),
         compiler_params=pltpu.CompilerParams(vmem_limit_bytes=16 * 2**20),
         name="assemble",
-    )(tiles)
+    )(*parts)
 
 
 def state_kernel(point_ref, gen_ref, row_ref, coarse_ref, fine_ref, init_ref, control_ref, core_ref, z_ref, out_ref, kx_ref, ky_ref, g_ref, v_ref, w_ref):
@@ -361,8 +360,9 @@
 ACROSS = [(s * 4 + k, (s ^ 2) * 4 + 3 - k) for s in range(64) for k in range(4)]
 
 
-def z_partner(other):
-    return [(i, i ^ other) for i in range(64)]
+def exchange(block, stride):
+    others = [lax.ppermute(block, "samp", [(i, i ^ stride * k) for i in range(64)]) for k in (1, 2, 3)]
+    return [block] + others
 
 
 def on_device(initial_state, target, control, point_index, generator):
@@ -371,6 +371,7 @@
 
     both = ("samp", "strip")
     own, to_core, to_z, wide_to_core, wide_to_z = strip_edges((initial_state, control, target))
+    own = jnp.maximum(own, jnp.finfo(jnp.float32).min)
     core, far = lax.ppermute(to_core, both, CORES), lax.ppermute(to_z, both, ACROSS)
     core_wide, far_wide = lax.ppermute(wide_to_core, both, CORES), lax.ppermute(wide_to_z, both, ACROSS)
     points = jnp.broadcast_to(point_index[:, None, None], (SAMPLES, 1, 128))
@@ -378,11 +379,10 @@
     mine = tile_gradient(points, generator.T, *tile_col_tables(width), row_table, core, own, far)
 
     mine, core_wide, far_wide = lax.optimization_barrier((mine, core_wide, far_wide))
-    tiles = jnp.stack([mine] + [lax.ppermute(mine, "samp", z_partner(k)) for k in (1, 2, 3)])
-    tiles = jnp.broadcast_to(tiles[None], (16, 4, HALF, 128))
+    tiles = jnp.stack(exchange(mine, 1))
+    tiles = jnp.stack(exchange(tiles, 4))
     tiles, generator = lax.optimization_barrier((tiles, generator))
-    tiles = lax.all_to_all(tiles, "samp", 0, 0, axis_index_groups=ALONG_XY, tiled=True)
-    new_control = assemble(tiles.reshape(SAMPLES, HALF, 128))
+    new_control = assemble(exchange(tiles, 16))
 
     state = own_final_state(point_index, generator, row_table, initial_state, control, core_wide, far_wide)
     return (new_control, state[None])

time: 63.3 us -> 62.7 us (level)
  the two profiles are of different devices: /device:TPU:8 before, /device:TPU:6 now
where the time goes in v5:
time: 62.7 us; the launch traced here: 62.5 us
  starting transfers between devices  31.3 us (50%)
  Pallas kernels  18.3 us (29%)
  waiting for transfers between devices  9.86 us (16%)
  between operations  1.39 us (2%)
  other arithmetic  0.97 us (2%)
  local copies, waits for them, and re-layouts  0.73 us (1%)
    ppermute x9, starting transfers between devices, exchange(): lax.ppermute(block, 'samp', [(i, i ^ stride * k) for i in range(64)])  14.2 us
    all_to_all x1, starting transfers between devices, on_device(): lax.all_to_all(points, 'samp', 0, 0, tiled=True).reshape(SAMPLES, 128)  12.2 us
    ppermute x9, waiting for transfers between devices, exchange(): lax.ppermute(block, 'samp', [(i, i ^ stride * k) for i in range(64)])  9.46 us
    pallas_call x1, Pallas kernels, own_final_state(): pl.pallas_call(state_kernel, out_shape=jax.ShapeDtypeStruct((rows, width)...  7.95 us
    pallas_call x1, Pallas kernels, tile_gradient(): pl.pallas_call(tile_kernel, out_shape=jax.ShapeDtypeStruct((HALF, 128), j...  6.65 us
    ppermute x1, starting transfers between devices, on_device(): lax.ppermute(to_z, both, ACROSS)  4.63 us
    pallas_call x1, Pallas kernels, strip_edges(): pl.pallas_call(edges_kernel, out_shape=[jax.ShapeDtypeStruct(shape, jnp.f...  2.38 us
    pallas_call x1, Pallas kernels, assemble(): pl.pallas_call(assemble_kernel, out_shape=jax.ShapeDtypeStruct((TILE, SAM...  1.32 us
  transfers between devices with their start and end apart: 14, of which 9 were waited for; matrix products, arithmetic and copies ran while one was open for 2% of the time, Pallas kernels for 27%

profile of v5, /device:TPU:6, one launch (start us, length us, event | category | flops | bytes accessed | tf_op | source)
XLA Modules:
  0.0 62.5 jit_solution(15054966554931987538)
XLA Ops:
  1.3 0.6 broadcast_in_dim.12
  1.9 12.2 %all-to-all-start = ((s32[64,1,128]{2,1,0:T(1,128)}), s32[64,1,128]{2,1,0:T(1,128)S(1)}, u32[]{:S(2)}, u32[]{:S(2)}) async-start(s32[64,1,128]{2,1,0:T(1,128)} %broadcast_in_dim.12), calls=%async_computation | async-start | bytes 65536 | tf_op jit(solution)/shard_map/all_to_all | solution.py:378
  14.1 2.4 %strip_edges.1 = (f32[3,64,128]{2,1,0:T(8,128)}, f32[3,8,128]{2,1,0:T(8,128)}, f32[3,8,128]{2,1,0:T(8,128)}, f32[32,8,128]{2,1,0:T(8,128)}, f32[32,8,128]{2,1,0:T(8,128)}) custom-call(f32[64,4096]{1,0:T(8,128)} %init_ref.1, f32[64,4096]{1,0:T(8,128)} %control_ref.1, f32[64,4096]{1,0:T(8,128)} %refs_2_.1), custom_call_target="tpu_custom_call" | custom-call | tf_op jit(solution)/shard_map/strip_edges/pallas_call | solution.py:115
  16.5 0.1 collective-permute-start
  16.6 4.6 %collective-permute-start.1 = (f32[3,8,128]{2,1,0:T(8,128)}, f32[3,8,128]{2,1,0:T(8,128)S(1)}, u32[]{:S(2)}, u32[]{:S(2)}) collective-permute-start(f32[3,8,128]{2,1,0:T(8,128)} %get-tuple-element.14), channel_id=1, source_target_pairs={{0,11},{1,10},{2,9},{3,8},{4,15},{5,14},{6,13},{7,12},{8,3},{9,2},... | collective-permute-start | bytes 36872 | tf_op jit(solution)/shard_map/ppermute | solution.py:375
  21.3 0.1 collective-permute-start.2
  21.3 0.1 collective-permute-start.3
  21.4 0.0 copy-start.2
  21.4 0.0 copy-start.3
  21.4 0.0 copy-start.4
  21.4 0.0 copy-start.5
  21.4 0.9 %broadcast_maximum_fusion.own_ref = f32[3,64,128]{2,1,0:T(8,128)S(1)} fusion(f32[3,64,128]{2,1,0:T(8,128)} %get-tuple-element.13), kind=kLoop, calls=%fused_computation.2 | loop fusion | flops 24576 | bytes 196608 | tf_op jit(solution)/shard_map/max | solution.py:374
  22.4 0.0 copy-done.2
  22.4 0.1 copy.13
  22.5 0.0 collective-permute-done.core_ref
  22.5 0.4 collective-permute-done.1.z_ref
  22.9 0.0 all-to-all-done
  22.9 0.0 copy-done.3
  22.9 0.0 copy-done.4
  22.9 0.0 copy-done.5
  22.9 0.0 copy-start
  22.9 0.0 copy-start.1
  22.9 6.6 %tile_gradient.1 = f32[32,128]{1,0:T(8,128)S(1)} custom-call(s32[64,128]{1,0:T(8,128)S(1)} %bitcast.14, s32[32,32]{1,0:T(8,128)S(1)} %bitcast.16, f32[2,64,128]{2,1,0:T(8,128)S(1)} %copy-done.4, f32[2,48,128]{2,1,0:T(8,128)S(1)} %copy-done.5, bf16[272,96]{1,0:T(8,128)(2,1)S(1)} %copy-done.3, f32[3,8,128]{2,1,0:T(8,128)S(1)} %collective-permute-done.core_ref, ...), custom_call_target="tpu_custom_call" | custom-call | flops 4000000000 | bytes 20000000 | tf_op jit(solution)/shard_map/tile_gradient/pallas_call | solution.py:226
  29.6 0.0 collective-permute-done.2.core_ref
  29.6 0.0 collective-permute-done.3.z_ref
  29.6 2.7 %collective-permute-start.6 = (f32[32,128]{1,0:T(8,128)S(1)}, f32[32,128]{1,0:T(8,128)S(1)}, u32[]{:S(2)}, u32[]{:S(2)}) collective-permute-start(f32[32,128]{1,0:T(8,128)S(1)} %tile_gradient.1), channel_id=1, source_target_pairs={{0,12},{4,8},{8,4},{12,0},{16,28},{20,24},{24,20},{28,16},{32,44},... | collective-permute-start | bytes 49160 | tf_op jit(solution)/shard_map/ppermute | solution.py:364
  32.2 2.9 %collective-permute-start.5 = (f32[32,128]{1,0:T(8,128)S(1)}, f32[32,128]{1,0:T(8,128)S(1)}, u32[]{:S(2)}, u32[]{:S(2)}) collective-permute-start(f32[32,128]{1,0:T(8,128)S(1)} %tile_gradient.1), channel_id=1, source_target_pairs={{0,8},{4,12},{8,0},{12,4},{16,24},{20,28},{24,16},{28,20},{32,40},... | collective-permute-start | bytes 49160 | tf_op jit(solution)/shard_map/ppermute | solution.py:364
  35.1 0.0 collective-permute-start.4
  35.1 0.1 collective-permute-done.6
  35.2 2.0 %collective-permute-done.5 = f32[32,128]{1,0:T(8,128)S(1)} collective-permute-done((f32[32,128]{1,0:T(8,128)S(1)}, f32[32,128]{1,0:T(8,128)S(1)}, u32[]{:S(2)}, u32[]{:S(2)}) %collective-permute-start.5) | collective-permute-done | bytes 16416 | tf_op jit(solution)/shard_map/ppermute | solution.py:364
  37.2 1.7 %collective-permute-done.4 = f32[32,128]{1,0:T(8,128)S(1)} collective-permute-done((f32[32,128]{1,0:T(8,128)S(1)}, f32[32,128]{1,0:T(8,128)S(1)}, u32[]{:S(2)}, u32[]{:S(2)}) %collective-permute-start.4) | collective-permute-done | bytes 16416 | tf_op jit(solution)/shard_map/ppermute | solution.py:364
  38.9 3.1 %collective-permute-start.8 = (f32[4,32,128]{2,1,0:T(8,128)S(1)}, f32[4,32,128]{2,1,0:T(8,128)S(1)}, u32[]{:S(2)}, u32[]{:S(2)}) collective-permute-start(f32[4,32,128]{2,1,0:T(8,128)S(1)} %get-tuple-element.23), channel_id=1, source_target_pairs={{0,32},{4,36},{8,40},{12,44},{16,48},{20,52},{24,56},{28,60},{32,0... | collective-permute-start | bytes 196616 | tf_op jit(solution)/shard_map/ppermute | solution.py:364
  42.0 0.6 collective-permute-start.7
  42.6 0.6 collective-permute-start.9
  43.1 1.7 %collective-permute-done.8 = f32[4,32,128]{2,1,0:T(8,128)S(1)} collective-permute-done((f32[4,32,128]{2,1,0:T(8,128)S(1)}, f32[4,32,128]{2,1,0:T(8,128)S(1)}, u32[]{:S(2)}, u32[]{:S(2)}) %collective-permute-start.8) | collective-permute-done | bytes 65568 | tf_op jit(solution)/shard_map/ppermute | solution.py:364
  44.8 1.5 %collective-permute-done.7 = f32[4,32,128]{2,1,0:T(8,128)S(1)} collective-permute-done((f32[4,32,128]{2,1,0:T(8,128)S(1)}, f32[4,32,128]{2,1,0:T(8,128)S(1)}, u32[]{:S(2)}, u32[]{:S(2)}) %collective-permute-start.7) | collective-permute-done | bytes 65568 | tf_op jit(solution)/shard_map/ppermute | solution.py:364
  46.3 1.8 %collective-permute-done.9 = f32[4,32,128]{2,1,0:T(8,128)S(1)} collective-permute-done((f32[4,32,128]{2,1,0:T(8,128)S(1)}, f32[4,32,128]{2,1,0:T(8,128)S(1)}, u32[]{:S(2)}, u32[]{:S(2)}) %collective-permute-start.9) | collective-permute-done | bytes 65568 | tf_op jit(solution)/shard_map/ppermute | solution.py:364
  48.1 0.0 copy-start.6
  48.1 0.0 copy-start.7
  48.1 0.5 collective-permute-start.12
  48.6 2.6 %collective-permute-start.11 = (f32[4,4,32,128]{3,2,1,0:T(8,128)S(1)}, f32[4,4,32,128]{3,2,1,0:T(8,128)S(1)}, u32[]{:S(2)}, u32[]{:S(2)}) collective-permute-start(f32[4,4,32,128]{3,2,1,0:T(8,128)S(1)} %pad_maximum_fusion.refs_0_), channel_id=1, source_target_pairs={{0,128},{4,132},{8,136},{12,140},{16,144},{20,148},{24,152},{28,15... | collective-permute-start | bytes 786440 | tf_op jit(solution)/shard_map/ppermute | solution.py:364
  51.2 1.3 %collective-permute-start.10 = (f32[4,4,32,128]{3,2,1,0:T(8,128)S(1)}, f32[4,4,32,128]{3,2,1,0:T(8,128)S(1)}, u32[]{:S(2)}, u32[]{:S(2)}) collective-permute-start(f32[4,4,32,128]{3,2,1,0:T(8,128)S(1)} %pad_maximum_fusion.refs_0_), channel_id=1, source_target_pairs={{0,64},{4,68},{8,72},{12,76},{16,80},{20,84},{24,88},{28,92},{32,9... | collective-permute-start | bytes 786440 | tf_op jit(solution)/shard_map/ppermute | solution.py:364
  52.4 0.0 copy-done
  52.5 0.0 copy-done.1
  52.5 0.0 copy-done.6
  52.5 0.0 copy-done.7
  52.5 8.0 %own_final_state.1 = f32[64,4096]{1,0:T(8,128)} custom-call(s32[1]{0:T(128)} %copy.14.point_ref, s32[32,32]{1,0:T(8,128)S(1)} %copy-done.2, bf16[272,96]{1,0:T(8,128)(2,1)S(1)} %copy-done.3, f32[2,32,32]{2,1,0:T(8,128)S(1)} %copy-done.7, f32[2,32,128]{2,1,0:T(8,128)S(1)} %copy-done.6, f32[64,4096]{1,0:T(8,128)S(1)} %copy-done, f32[64,4096]{1,0:T(8,128)S(1)} %copy-done.1, ...), custom_call_target="tpu_custom_call" | custom-call | flops 2000000000 | bytes 3500000 | tf_op jit(solution)/shard_map/own_final_state/pallas_call | solution.py:347
  60.4 0.2 collective-permute-done.12.refs_3_
  60.6 0.0 collective-permute-done.11.refs_2_
  60.6 0.6 collective-permute-done.10.refs_1_
  61.2 1.3 %assemble.1 = f32[64,4096]{1,0:T(8,128)} custom-call(f32[4,4,32,128]{3,2,1,0:T(8,128)S(1)} %pad_maximum_fusion.refs_0_, f32[4,4,32,128]{3,2,1,0:T(8,128)S(1)} %collective-permute-done.10.refs_1_, f32[4,4,32,128]{3,2,1,0:T(8,128)S(1)} %collective-permute-done.11.refs_2_, f32[4,4,32,128]{3,2,1,0:T(8,128)S(1)} %collective-permute-done.12.refs_3_), custom_call_target="tpu_custom_call" | custom-call | tf_op jit(solution)/shard_map/assemble/pallas_call | solution.py:254
  (2 shorter events, 0.0 us)
Async XLA Ops:
  1.9 21.0 %all-to-all-start = ((s32[64,1,128]{2,1,0:T(1,128)}), s32[64,1,128]{2,1,0:T(1,128)S(1)}, u32[]{:S(2)}, u32[]{:S(2)}) async-start(s32[64,1,128]{2,1,0:T(1,128)} %broadcast_in_dim.12), calls=%async_computation | async-start | bytes 65536 | tf_op jit(solution)/shard_map/all_to_all | solution.py:378
  16.5 5.9 %collective-permute-start = (f32[3,8,128]{2,1,0:T(8,128)}, f32[3,8,128]{2,1,0:T(8,128)S(1)}, u32[]{:S(2)}, u32[]{:S(2)}) collective-permute-start(f32[3,8,128]{2,1,0:T(8,128)} %get-tuple-element.12), channel_id=1, source_target_pairs={{0,1},{1,0},{2,3},{3,2},{4,5},{5,4},{6,7},{7,6},{8,9},{9,8},{10,11... | collective-permute-start | bytes 36872 | tf_op jit(solution)/shard_map/ppermute | solution.py:375
  16.6 6.2 %collective-permute-start.1 = (f32[3,8,128]{2,1,0:T(8,128)}, f32[3,8,128]{2,1,0:T(8,128)S(1)}, u32[]{:S(2)}, u32[]{:S(2)}) collective-permute-start(f32[3,8,128]{2,1,0:T(8,128)} %get-tuple-element.14), channel_id=1, source_target_pairs={{0,11},{1,10},{2,9},{3,8},{4,15},{5,14},{6,13},{7,12},{8,3},{9,2},... | collective-permute-start | bytes 36872 | tf_op jit(solution)/shard_map/ppermute | solution.py:375
  21.3 8.3 %collective-permute-start.2 = (f32[32,8,128]{2,1,0:T(8,128)}, f32[32,8,128]{2,1,0:T(8,128)S(1)}, u32[]{:S(2)}, u32[]{:S(2)}) collective-permute-start(f32[32,8,128]{2,1,0:T(8,128)} %get-tuple-element.15), channel_id=1, source_target_pairs={{0,1},{1,0},{2,3},{3,2},{4,5},{5,4},{6,7},{7,6},{8,9},{9,8},{10,11... | collective-permute-start | bytes 393224 | tf_op jit(solution)/shard_map/ppermute | solution.py:376
  21.3 8.2 %collective-permute-start.3 = (f32[32,8,128]{2,1,0:T(8,128)}, f32[32,8,128]{2,1,0:T(8,128)S(1)}, u32[]{:S(2)}, u32[]{:S(2)}) collective-permute-start(f32[32,8,128]{2,1,0:T(8,128)} %get-tuple-element.16), channel_id=1, source_target_pairs={{0,11},{1,10},{2,9},{3,8},{4,15},{5,14},{6,13},{7,12},{8,3},{9,2},... | collective-permute-start | bytes 393224 | tf_op jit(solution)/shard_map/ppermute | solution.py:376
  21.4 1.0 %copy-start.2 = (s32[32,32]{1,0:T(8,128)S(1)}, s32[32,32]{1,0:T(8,128)}, u32[]{:S(2)}) copy-start(s32[32,32]{1,0:T(8,128)} %gen_ref) | copy-start | bytes 12292
  21.4 1.4 %copy-start.3 = (bf16[272,96]{1,0:T(8,128)(2,1)S(1)}, bf16[272,96]{1,0:T(8,128)(2,1)}, u32[]{:S(2)}) copy-start(bf16[272,96]{1,0:T(8,128)(2,1)} %constant.14.clone.row_ref) | copy-start | bytes 156676
  21.4 1.4 %copy-start.4 = (f32[2,64,128]{2,1,0:T(8,128)S(1)}, f32[2,64,128]{2,1,0:T(8,128)}, u32[]{:S(2)}) copy-start(f32[2,64,128]{2,1,0:T(8,128)} %constant.12.clone.coarse_ref) | copy-start | bytes 196612
  21.4 1.4 %copy-start.5 = (f32[2,48,128]{2,1,0:T(8,128)S(1)}, f32[2,48,128]{2,1,0:T(8,128)}, u32[]{:S(2)}) copy-start(f32[2,48,128]{2,1,0:T(8,128)} %constant.13.clone.fine_ref) | copy-start | bytes 147460
  22.9 29.6 %copy-start = (f32[64,4096]{1,0:T(8,128)S(1)}, f32[64,4096]{1,0:T(8,128)}, u32[]{:S(2)}) copy-start(f32[64,4096]{1,0:T(8,128)} %init_ref.1) | copy-start | bytes 3145732
  22.9 29.6 %copy-start.1 = (f32[64,4096]{1,0:T(8,128)S(1)}, f32[64,4096]{1,0:T(8,128)}, u32[]{:S(2)}) copy-start(f32[64,4096]{1,0:T(8,128)} %control_ref.1) | copy-start | bytes 3145732
  29.6 5.6 %collective-permute-start.6 = (f32[32,128]{1,0:T(8,128)S(1)}, f32[32,128]{1,0:T(8,128)S(1)}, u32[]{:S(2)}, u32[]{:S(2)}) collective-permute-start(f32[32,128]{1,0:T(8,128)S(1)} %tile_gradient.1), channel_id=1, source_target_pairs={{0,12},{4,8},{8,4},{12,0},{16,28},{20,24},{24,20},{28,16},{32,44},... | collective-permute-start | bytes 49160 | tf_op jit(solution)/shard_map/ppermute | solution.py:364
  32.2 4.9 %collective-permute-start.5 = (f32[32,128]{1,0:T(8,128)S(1)}, f32[32,128]{1,0:T(8,128)S(1)}, u32[]{:S(2)}, u32[]{:S(2)}) collective-permute-start(f32[32,128]{1,0:T(8,128)S(1)} %tile_gradient.1), channel_id=1, source_target_pairs={{0,8},{4,12},{8,0},{12,4},{16,24},{20,28},{24,16},{28,20},{32,40},... | collective-permute-start | bytes 49160 | tf_op jit(solution)/shard_map/ppermute | solution.py:364
  35.1 3.7 %collective-permute-start.4 = (f32[32,128]{1,0:T(8,128)S(1)}, f32[32,128]{1,0:T(8,128)S(1)}, u32[]{:S(2)}, u32[]{:S(2)}) collective-permute-start(f32[32,128]{1,0:T(8,128)S(1)} %tile_gradient.1), channel_id=1, source_target_pairs={{0,4},{4,0},{8,12},{12,8},{16,20},{20,16},{24,28},{28,24},{32,36},... | collective-permute-start | bytes 49160 | tf_op jit(solution)/shard_map/ppermute | solution.py:364
  38.9 5.9 %collective-permute-start.8 = (f32[4,32,128]{2,1,0:T(8,128)S(1)}, f32[4,32,128]{2,1,0:T(8,128)S(1)}, u32[]{:S(2)}, u32[]{:S(2)}) collective-permute-start(f32[4,32,128]{2,1,0:T(8,128)S(1)} %get-tuple-element.23), channel_id=1, source_target_pairs={{0,32},{4,36},{8,40},{12,44},{16,48},{20,52},{24,56},{28,60},{32,0... | collective-permute-start | bytes 196616 | tf_op jit(solution)/shard_map/ppermute | solution.py:364
  42.0 4.3 %collective-permute-start.7 = (f32[4,32,128]{2,1,0:T(8,128)S(1)}, f32[4,32,128]{2,1,0:T(8,128)S(1)}, u32[]{:S(2)}, u32[]{:S(2)}) collective-permute-start(f32[4,32,128]{2,1,0:T(8,128)S(1)} %get-tuple-element.23), channel_id=1, source_target_pairs={{0,16},{4,20},{8,24},{12,28},{16,0},{20,4},{24,8},{28,12},{32,48},... | collective-permute-start | bytes 196616 | tf_op jit(solution)/shard_map/ppermute | solution.py:364
  42.6 5.5 %collective-permute-start.9 = (f32[4,32,128]{2,1,0:T(8,128)S(1)}, f32[4,32,128]{2,1,0:T(8,128)S(1)}, u32[]{:S(2)}, u32[]{:S(2)}) collective-permute-start(f32[4,32,128]{2,1,0:T(8,128)S(1)} %get-tuple-element.23), channel_id=1, source_target_pairs={{0,48},{4,52},{8,56},{12,60},{16,32},{20,36},{24,40},{28,44},{32,1... | collective-permute-start | bytes 196616 | tf_op jit(solution)/shard_map/ppermute | solution.py:364
  48.1 4.4 %copy-start.6 = (f32[2,32,128]{2,1,0:T(8,128)S(1)}, f32[2,32,128]{2,1,0:T(8,128)}, u32[]{:S(2)}) copy-start(f32[2,32,128]{2,1,0:T(8,128)} %constant.16.clone.fine_ref) | copy-start | bytes 98308
  48.1 4.4 %copy-start.7 = (f32[2,32,32]{2,1,0:T(8,128)S(1)}, f32[2,32,32]{2,1,0:T(8,128)}, u32[]{:S(2)}) copy-start(f32[2,32,32]{2,1,0:T(8,128)} %constant.15.clone.coarse_ref) | copy-start | bytes 24580
  48.1 12.5 %collective-permute-start.12 = (f32[4,4,32,128]{3,2,1,0:T(8,128)S(1)}, f32[4,4,32,128]{3,2,1,0:T(8,128)S(1)}, u32[]{:S(2)}, u32[]{:S(2)}) collective-permute-start(f32[4,4,32,128]{3,2,1,0:T(8,128)S(1)} %pad_maximum_fusion.refs_0_), channel_id=1, source_target_pairs={{0,192},{4,196},{8,200},{12,204},{16,208},{20,212},{24,216},{28,22... | collective-permute-start | bytes 786440 | tf_op jit(solution)/shard_map/ppermute | solution.py:364
  48.6 12.0 %collective-permute-start.11 = (f32[4,4,32,128]{3,2,1,0:T(8,128)S(1)}, f32[4,4,32,128]{3,2,1,0:T(8,128)S(1)}, u32[]{:S(2)}, u32[]{:S(2)}) collective-permute-start(f32[4,4,32,128]{3,2,1,0:T(8,128)S(1)} %pad_maximum_fusion.refs_0_), channel_id=1, source_target_pairs={{0,128},{4,132},{8,136},{12,140},{16,144},{20,148},{24,152},{28,15... | collective-permute-start | bytes 786440 | tf_op jit(solution)/shard_map/ppermute | solution.py:364
  51.2 10.0 %collective-permute-start.10 = (f32[4,4,32,128]{3,2,1,0:T(8,128)S(1)}, f32[4,4,32,128]{3,2,1,0:T(8,128)S(1)}, u32[]{:S(2)}, u32[]{:S(2)}) collective-permute-start(f32[4,4,32,128]{3,2,1,0:T(8,128)S(1)} %pad_maximum_fusion.refs_0_), channel_id=1, source_target_pairs={{0,64},{4,68},{8,72},{12,76},{16,80},{20,84},{24,88},{28,92},{32,9... | collective-permute-start | bytes 786440 | tf_op jit(solution)/shard_map/ppermute | solution.py:364

commit v6 on v5

--- a/solution.py
+++ b/solution.py
@@ -378,8 +378,8 @@
     points = lax.all_to_all(points, "samp", 0, 0, tiled=True).reshape(SAMPLES, 128)
     mine = tile_gradient(points, generator.T, *tile_col_tables(width), row_table, core, own, far)
 
-    mine, core_wide, far_wide = lax.optimization_barrier((mine, core_wide, far_wide))
     tiles = jnp.stack(exchange(mine, 1))
+    tiles, core_wide, far_wide = lax.optimization_barrier((tiles, core_wide, far_wide))
     tiles = jnp.stack(exchange(tiles, 4))
     tiles, generator = lax.optimization_barrier((tiles, generator))
     new_control = assemble(exchange(tiles, 16))

time: 62.7 us -> 60.6 us (0.967)
  starting transfers between devices: 31.3 us -> 30.1 us
  waiting for transfers between devices: 9.86 us -> 8.92 us
    ppermute x9, starting transfers between devices: 14.2 us -> 13 us  [exchange(): lax.ppermute(block, 'samp', [(i, i ^ stride * k) for i in range(64)])]
    ppermute x9, waiting for transfers between devices: 9.46 us -> 8.52 us  [exchange(): lax.ppermute(block, 'samp', [(i, i ^ stride * k) for i in range(64)])]
  transfers between devices with their start and end apart: 14 -> 14, of which waited for: 9 -> 7; matrix products, arithmetic and copies ran while one was open for 2% -> 2% of each run, Pallas kernels for 27% -> 28%
where the time goes in v6:
time: 60.6 us; the launch traced here: 60.4 us
  starting transfers between devices  30.1 us (50%)
  Pallas kernels  18.3 us (30%)
  waiting for transfers between devices  8.92 us (15%)
  between operations  1.39 us (2%)
  other arithmetic  0.96 us (2%)
  local copies, waits for them, and re-layouts  0.72 us (1%)
    ppermute x9, starting transfers between devices, exchange(): lax.ppermute(block, 'samp', [(i, i ^ stride * k) for i in range(64)])  13 us
    all_to_all x1, starting transfers between devices, on_device(): lax.all_to_all(points, 'samp', 0, 0, tiled=True).reshape(SAMPLES, 128)  12.2 us
    ppermute x9, waiting for transfers between devices, exchange(): lax.ppermute(block, 'samp', [(i, i ^ stride * k) for i in range(64)])  8.52 us
    pallas_call x1, Pallas kernels, own_final_state(): pl.pallas_call(state_kernel, out_shape=jax.ShapeDtypeStruct((rows, width)...  7.95 us
    pallas_call x1, Pallas kernels, tile_gradient(): pl.pallas_call(tile_kernel, out_shape=jax.ShapeDtypeStruct((HALF, 128), j...  6.65 us
    ppermute x1, starting transfers between devices, on_device(): lax.ppermute(to_z, both, ACROSS)  4.63 us
    pallas_call x1, Pallas kernels, strip_edges(): pl.pallas_call(edges_kernel, out_shape=[jax.ShapeDtypeStruct(shape, jnp.f...  2.37 us
    pallas_call x1, Pallas kernels, assemble(): pl.pallas_call(assemble_kernel, out_shape=jax.ShapeDtypeStruct((TILE, SAM...  1.32 us
  transfers between devices with their start and end apart: 14, of which 7 were waited for; matrix products, arithmetic and copies ran while one was open for 2% of the time, Pallas kernels for 28%

profile of v6, /device:TPU:6, one launch (start us, length us, event | category | flops | bytes accessed | tf_op | source)
XLA Modules:
  0.0 60.4 jit_solution(1753740126289493030)
XLA Ops:
  1.3 0.6 %broadcast_in_dim.12 = s32[64,1,128]{2,1,0:T(1,128)} broadcast(s32[]{:T(128)} %bitcast.12), dimensions={} | broadcast | bytes 32772 | tf_op jit(solution)/shard_map/broadcast_in_dim | solution.py:377
  1.9 12.2 %all-to-all-start = ((s32[64,1,128]{2,1,0:T(1,128)}), s32[64,1,128]{2,1,0:T(1,128)S(1)}, u32[]{:S(2)}, u32[]{:S(2)}) async-start(s32[64,1,128]{2,1,0:T(1,128)} %broadcast_in_dim.12), calls=%async_computation | async-start | bytes 65536 | tf_op jit(solution)/shard_map/all_to_all | solution.py:378
  14.1 2.4 %strip_edges.1 = (f32[3,64,128]{2,1,0:T(8,128)}, f32[3,8,128]{2,1,0:T(8,128)}, f32[3,8,128]{2,1,0:T(8,128)}, f32[32,8,128]{2,1,0:T(8,128)}, f32[32,8,128]{2,1,0:T(8,128)}) custom-call(f32[64,4096]{1,0:T(8,128)} %init_ref.1, f32[64,4096]{1,0:T(8,128)} %control_ref.1, f32[64,4096]{1,0:T(8,128)} %refs_2_.1), custom_call_target="tpu_custom_call" | custom-call | tf_op jit(solution)/shard_map/strip_edges/pallas_call | solution.py:115
  16.5 0.1 collective-permute-start
  16.6 4.6 %collective-permute-start.1 = (f32[3,8,128]{2,1,0:T(8,128)}, f32[3,8,128]{2,1,0:T(8,128)S(1)}, u32[]{:S(2)}, u32[]{:S(2)}) collective-permute-start(f32[3,8,128]{2,1,0:T(8,128)} %get-tuple-element.14), channel_id=1, source_target_pairs={{0,11},{1,10},{2,9},{3,8},{4,15},{5,14},{6,13},{7,12},{8,3},{9,2},... | collective-permute-start | bytes 36872 | tf_op jit(solution)/shard_map/ppermute | solution.py:375
  21.2 0.1 collective-permute-start.5
  21.3 0.1 collective-permute-start.6
  21.4 0.0 copy-start.2
  21.4 0.0 copy-start.3
  21.4 0.0 copy-start.4
  21.4 0.0 copy-start.5
  21.4 0.9 %broadcast_maximum_fusion.own_ref = f32[3,64,128]{2,1,0:T(8,128)S(1)} fusion(f32[3,64,128]{2,1,0:T(8,128)} %get-tuple-element.13), kind=kLoop, calls=%fused_computation.2 | loop fusion | flops 24576 | bytes 196608 | tf_op jit(solution)/shard_map/max | solution.py:374
  22.4 0.0 copy-done.2
  22.4 0.1 copy.13
  22.5 0.0 collective-permute-done.core_ref
  22.5 0.4 collective-permute-done.1.z_ref
  22.9 0.0 all-to-all-done
  22.9 0.0 copy-done.3
  22.9 0.0 copy-done.4
  22.9 0.0 copy-done.5
  22.9 0.0 copy-start
  22.9 0.0 copy-start.1
  22.9 6.7 %tile_gradient.1 = f32[32,128]{1,0:T(8,128)S(1)} custom-call(s32[64,128]{1,0:T(8,128)S(1)} %bitcast.13, s32[32,32]{1,0:T(8,128)S(1)} %bitcast.14, f32[2,64,128]{2,1,0:T(8,128)S(1)} %copy-done.4, f32[2,48,128]{2,1,0:T(8,128)S(1)} %copy-done.5, bf16[272,96]{1,0:T(8,128)(2,1)S(1)} %copy-done.3, f32[3,8,128]{2,1,0:T(8,128)S(1)} %collective-permute-done.core_ref, ...), custom_call_target="tpu_custom_call" | custom-call | flops 4000000000 | bytes 20000000 | tf_op jit(solution)/shard_map/tile_gradient/pallas_call | solution.py:226
  29.6 2.7 %collective-permute-start.4 = (f32[32,128]{1,0:T(8,128)S(1)}, f32[32,128]{1,0:T(8,128)S(1)}, u32[]{:S(2)}, u32[]{:S(2)}) collective-permute-start(f32[32,128]{1,0:T(8,128)S(1)} %tile_gradient.1), channel_id=1, source_target_pairs={{0,12},{4,8},{8,4},{12,0},{16,28},{20,24},{24,20},{28,16},{32,44},... | collective-permute-start | bytes 49160 | tf_op jit(solution)/shard_map/ppermute | solution.py:364
  32.2 0.4 collective-permute-start.3
  32.7 1.4 %collective-permute-start.2 = (f32[32,128]{1,0:T(8,128)S(1)}, f32[32,128]{1,0:T(8,128)S(1)}, u32[]{:S(2)}, u32[]{:S(2)}) collective-permute-start(f32[32,128]{1,0:T(8,128)S(1)} %tile_gradient.1), channel_id=1, source_target_pairs={{0,4},{4,0},{8,12},{12,8},{16,20},{20,16},{24,28},{28,24},{32,36},... | collective-permute-start | bytes 49160 | tf_op jit(solution)/shard_map/ppermute | solution.py:364
  34.0 1.3 %collective-permute-done.4 = f32[32,128]{1,0:T(8,128)S(1)} collective-permute-done((f32[32,128]{1,0:T(8,128)S(1)}, f32[32,128]{1,0:T(8,128)S(1)}, u32[]{:S(2)}, u32[]{:S(2)}) %collective-permute-start.4) | collective-permute-done | bytes 16416 | tf_op jit(solution)/shard_map/ppermute | solution.py:364
  35.3 1.5 %collective-permute-done.3 = f32[32,128]{1,0:T(8,128)S(1)} collective-permute-done((f32[32,128]{1,0:T(8,128)S(1)}, f32[32,128]{1,0:T(8,128)S(1)}, u32[]{:S(2)}, u32[]{:S(2)}) %collective-permute-start.3) | collective-permute-done | bytes 16416 | tf_op jit(solution)/shard_map/ppermute | solution.py:364
  36.9 0.0 collective-permute-done.2
  36.9 0.0 collective-permute-done.5.core_ref
  36.9 0.0 collective-permute-done.6.z_ref
  36.9 2.8 %collective-permute-start.9 = (f32[4,32,128]{2,1,0:T(8,128)S(1)}, f32[4,32,128]{2,1,0:T(8,128)S(1)}, u32[]{:S(2)}, u32[]{:S(2)}) collective-permute-start(f32[4,32,128]{2,1,0:T(8,128)S(1)} %pad_maximum_fusion.1), channel_id=1, source_target_pairs={{0,48},{4,52},{8,56},{12,60},{16,32},{20,36},{24,40},{28,44},{32,1... | collective-permute-start | bytes 196616 | tf_op jit(solution)/shard_map/ppermute | solution.py:364
  39.7 0.8 %collective-permute-start.8 = (f32[4,32,128]{2,1,0:T(8,128)S(1)}, f32[4,32,128]{2,1,0:T(8,128)S(1)}, u32[]{:S(2)}, u32[]{:S(2)}) collective-permute-start(f32[4,32,128]{2,1,0:T(8,128)S(1)} %pad_maximum_fusion.1), channel_id=1, source_target_pairs={{0,32},{4,36},{8,40},{12,44},{16,48},{20,52},{24,56},{28,60},{32,0... | collective-permute-start | bytes 196616 | tf_op jit(solution)/shard_map/ppermute | solution.py:364
  40.5 0.5 collective-permute-start.7
  41.1 1.4 %collective-permute-done.9 = f32[4,32,128]{2,1,0:T(8,128)S(1)} collective-permute-done((f32[4,32,128]{2,1,0:T(8,128)S(1)}, f32[4,32,128]{2,1,0:T(8,128)S(1)}, u32[]{:S(2)}, u32[]{:S(2)}) %collective-permute-start.9) | collective-permute-done | bytes 65568 | tf_op jit(solution)/shard_map/ppermute | solution.py:364
  42.4 3.0 %collective-permute-done.8 = f32[4,32,128]{2,1,0:T(8,128)S(1)} collective-permute-done((f32[4,32,128]{2,1,0:T(8,128)S(1)}, f32[4,32,128]{2,1,0:T(8,128)S(1)}, u32[]{:S(2)}, u32[]{:S(2)}) %collective-permute-start.8) | collective-permute-done | bytes 65568 | tf_op jit(solution)/shard_map/ppermute | solution.py:364
  45.5 0.0 collective-permute-done.7
  45.5 0.0 copy-start.6
  45.5 0.0 copy-start.7
  45.5 0.5 collective-permute-start.12
  46.1 2.6 %collective-permute-start.11 = (f32[4,4,32,128]{3,2,1,0:T(8,128)S(1)}, f32[4,4,32,128]{3,2,1,0:T(8,128)S(1)}, u32[]{:S(2)}, u32[]{:S(2)}) collective-permute-start(f32[4,4,32,128]{3,2,1,0:T(8,128)S(1)} %pad_maximum_fusion.refs_0_), channel_id=1, source_target_pairs={{0,128},{4,132},{8,136},{12,140},{16,144},{20,148},{24,152},{28,15... | collective-permute-start | bytes 786440 | tf_op jit(solution)/shard_map/ppermute | solution.py:364
  48.6 1.3 %collective-permute-start.10 = (f32[4,4,32,128]{3,2,1,0:T(8,128)S(1)}, f32[4,4,32,128]{3,2,1,0:T(8,128)S(1)}, u32[]{:S(2)}, u32[]{:S(2)}) collective-permute-start(f32[4,4,32,128]{3,2,1,0:T(8,128)S(1)} %pad_maximum_fusion.refs_0_), channel_id=1, source_target_pairs={{0,64},{4,68},{8,72},{12,76},{16,80},{20,84},{24,88},{28,92},{32,9... | collective-permute-start | bytes 786440 | tf_op jit(solution)/shard_map/ppermute | solution.py:364
  49.9 0.0 copy-done
  49.9 0.0 copy-done.1
  49.9 0.0 copy-done.6
  49.9 0.0 copy-done.7
  49.9 8.0 %own_final_state.1 = f32[64,4096]{1,0:T(8,128)} custom-call(s32[1]{0:T(128)} %copy.14.point_ref, s32[32,32]{1,0:T(8,128)S(1)} %copy-done.2, bf16[272,96]{1,0:T(8,128)(2,1)S(1)} %copy-done.3, f32[2,32,32]{2,1,0:T(8,128)S(1)} %copy-done.7, f32[2,32,128]{2,1,0:T(8,128)S(1)} %copy-done.6, f32[64,4096]{1,0:T(8,128)S(1)} %copy-done, f32[64,4096]{1,0:T(8,128)S(1)} %copy-done.1, ...), custom_call_target="tpu_custom_call" | custom-call | flops 2000000000 | bytes 3500000 | tf_op jit(solution)/shard_map/own_final_state/pallas_call | solution.py:347
  57.9 0.6 %collective-permute-done.12.refs_3_ = f32[4,4,32,128]{3,2,1,0:T(8,128)S(1)} collective-permute-done((f32[4,4,32,128]{3,2,1,0:T(8,128)S(1)}, f32[4,4,32,128]{3,2,1,0:T(8,128)S(1)}, u32[]{:S(2)}, u32[]{:S(2)}) %collective-permute-start.12) | collective-permute-done | bytes 262176 | tf_op jit(solution)/shard_map/ppermute | solution.py:364
  58.5 0.0 collective-permute-done.11.refs_2_
  58.5 0.6 %collective-permute-done.10.refs_1_ = f32[4,4,32,128]{3,2,1,0:T(8,128)S(1)} collective-permute-done((f32[4,4,32,128]{3,2,1,0:T(8,128)S(1)}, f32[4,4,32,128]{3,2,1,0:T(8,128)S(1)}, u32[]{:S(2)}, u32[]{:S(2)}) %collective-permute-start.10) | collective-permute-done | bytes 262176 | tf_op jit(solution)/shard_map/ppermute | solution.py:364
  59.1 1.3 %assemble.1 = f32[64,4096]{1,0:T(8,128)} custom-call(f32[4,4,32,128]{3,2,1,0:T(8,128)S(1)} %pad_maximum_fusion.refs_0_, f32[4,4,32,128]{3,2,1,0:T(8,128)S(1)} %collective-permute-done.10.refs_1_, f32[4,4,32,128]{3,2,1,0:T(8,128)S(1)} %collective-permute-done.11.refs_2_, f32[4,4,32,128]{3,2,1,0:T(8,128)S(1)} %collective-permute-done.12.refs_3_), custom_call_target="tpu_custom_call" | custom-call | tf_op jit(solution)/shard_map/assemble/pallas_call | solution.py:254
  (2 shorter events, 0.0 us)
Async XLA Ops:
  1.9 21.0 %all-to-all-start = ((s32[64,1,128]{2,1,0:T(1,128)}), s32[64,1,128]{2,1,0:T(1,128)S(1)}, u32[]{:S(2)}, u32[]{:S(2)}) async-start(s32[64,1,128]{2,1,0:T(1,128)} %broadcast_in_dim.12), calls=%async_computation | async-start | bytes 65536 | tf_op jit(solution)/shard_map/all_to_all | solution.py:378
  16.5 5.9 %collective-permute-start = (f32[3,8,128]{2,1,0:T(8,128)}, f32[3,8,128]{2,1,0:T(8,128)S(1)}, u32[]{:S(2)}, u32[]{:S(2)}) collective-permute-start(f32[3,8,128]{2,1,0:T(8,128)} %get-tuple-element.12), channel_id=1, source_target_pairs={{0,1},{1,0},{2,3},{3,2},{4,5},{5,4},{6,7},{7,6},{8,9},{9,8},{10,11... | collective-permute-start | bytes 36872 | tf_op jit(solution)/shard_map/ppermute | solution.py:375
  16.6 6.2 %collective-permute-start.1 = (f32[3,8,128]{2,1,0:T(8,128)}, f32[3,8,128]{2,1,0:T(8,128)S(1)}, u32[]{:S(2)}, u32[]{:S(2)}) collective-permute-start(f32[3,8,128]{2,1,0:T(8,128)} %get-tuple-element.14), channel_id=1, source_target_pairs={{0,11},{1,10},{2,9},{3,8},{4,15},{5,14},{6,13},{7,12},{8,3},{9,2},... | collective-permute-start | bytes 36872 | tf_op jit(solution)/shard_map/ppermute | solution.py:375
  21.2 15.6 %collective-permute-start.5 = (f32[32,8,128]{2,1,0:T(8,128)}, f32[32,8,128]{2,1,0:T(8,128)S(1)}, u32[]{:S(2)}, u32[]{:S(2)}) collective-permute-start(f32[32,8,128]{2,1,0:T(8,128)} %get-tuple-element.15), channel_id=1, source_target_pairs={{0,1},{1,0},{2,3},{3,2},{4,5},{5,4},{6,7},{7,6},{8,9},{9,8},{10,11... | collective-permute-start | bytes 393224 | tf_op jit(solution)/shard_map/ppermute | solution.py:376
  21.3 15.6 %collective-permute-start.6 = (f32[32,8,128]{2,1,0:T(8,128)}, f32[32,8,128]{2,1,0:T(8,128)S(1)}, u32[]{:S(2)}, u32[]{:S(2)}) collective-permute-start(f32[32,8,128]{2,1,0:T(8,128)} %get-tuple-element.16), channel_id=1, source_target_pairs={{0,11},{1,10},{2,9},{3,8},{4,15},{5,14},{6,13},{7,12},{8,3},{9,2},... | collective-permute-start | bytes 393224 | tf_op jit(solution)/shard_map/ppermute | solution.py:376
  21.4 1.0 %copy-start.2 = (s32[32,32]{1,0:T(8,128)S(1)}, s32[32,32]{1,0:T(8,128)}, u32[]{:S(2)}) copy-start(s32[32,32]{1,0:T(8,128)} %gen_ref) | copy-start | bytes 12292
  21.4 1.4 %copy-start.3 = (bf16[272,96]{1,0:T(8,128)(2,1)S(1)}, bf16[272,96]{1,0:T(8,128)(2,1)}, u32[]{:S(2)}) copy-start(bf16[272,96]{1,0:T(8,128)(2,1)} %constant.14.clone.row_ref) | copy-start | bytes 156676
  21.4 1.4 %copy-start.4 = (f32[2,64,128]{2,1,0:T(8,128)S(1)}, f32[2,64,128]{2,1,0:T(8,128)}, u32[]{:S(2)}) copy-start(f32[2,64,128]{2,1,0:T(8,128)} %constant.12.clone.coarse_ref) | copy-start | bytes 196612
  21.4 1.4 %copy-start.5 = (f32[2,48,128]{2,1,0:T(8,128)S(1)}, f32[2,48,128]{2,1,0:T(8,128)}, u32[]{:S(2)}) copy-start(f32[2,48,128]{2,1,0:T(8,128)} %constant.13.clone.fine_ref) | copy-start | bytes 147460
  22.9 27.0 %copy-start = (f32[64,4096]{1,0:T(8,128)S(1)}, f32[64,4096]{1,0:T(8,128)}, u32[]{:S(2)}) copy-start(f32[64,4096]{1,0:T(8,128)} %init_ref.1) | copy-start | bytes 3145732
  22.9 27.0 %copy-start.1 = (f32[64,4096]{1,0:T(8,128)S(1)}, f32[64,4096]{1,0:T(8,128)}, u32[]{:S(2)}) copy-start(f32[64,4096]{1,0:T(8,128)} %control_ref.1) | copy-start | bytes 3145732
  29.6 5.8 %collective-permute-start.4 = (f32[32,128]{1,0:T(8,128)S(1)}, f32[32,128]{1,0:T(8,128)S(1)}, u32[]{:S(2)}, u32[]{:S(2)}) collective-permute-start(f32[32,128]{1,0:T(8,128)S(1)} %tile_gradient.1), channel_id=1, source_target_pairs={{0,12},{4,8},{8,4},{12,0},{16,28},{20,24},{24,20},{28,16},{32,44},... | collective-permute-start | bytes 49160 | tf_op jit(solution)/shard_map/ppermute | solution.py:364
  32.2 4.6 %collective-permute-start.3 = (f32[32,128]{1,0:T(8,128)S(1)}, f32[32,128]{1,0:T(8,128)S(1)}, u32[]{:S(2)}, u32[]{:S(2)}) collective-permute-start(f32[32,128]{1,0:T(8,128)S(1)} %tile_gradient.1), channel_id=1, source_target_pairs={{0,8},{4,12},{8,0},{12,4},{16,24},{20,28},{24,16},{28,20},{32,40},... | collective-permute-start | bytes 49160 | tf_op jit(solution)/shard_map/ppermute | solution.py:364
  32.7 4.2 %collective-permute-start.2 = (f32[32,128]{1,0:T(8,128)S(1)}, f32[32,128]{1,0:T(8,128)S(1)}, u32[]{:S(2)}, u32[]{:S(2)}) collective-permute-start(f32[32,128]{1,0:T(8,128)S(1)} %tile_gradient.1), channel_id=1, source_target_pairs={{0,4},{4,0},{8,12},{12,8},{16,20},{20,16},{24,28},{28,24},{32,36},... | collective-permute-start | bytes 49160 | tf_op jit(solution)/shard_map/ppermute | solution.py:364
  36.9 5.6 %collective-permute-start.9 = (f32[4,32,128]{2,1,0:T(8,128)S(1)}, f32[4,32,128]{2,1,0:T(8,128)S(1)}, u32[]{:S(2)}, u32[]{:S(2)}) collective-permute-start(f32[4,32,128]{2,1,0:T(8,128)S(1)} %pad_maximum_fusion.1), channel_id=1, source_target_pairs={{0,48},{4,52},{8,56},{12,60},{16,32},{20,36},{24,40},{28,44},{32,1... | collective-permute-start | bytes 196616 | tf_op jit(solution)/shard_map/ppermute | solution.py:364
  39.7 5.8 %collective-permute-start.8 = (f32[4,32,128]{2,1,0:T(8,128)S(1)}, f32[4,32,128]{2,1,0:T(8,128)S(1)}, u32[]{:S(2)}, u32[]{:S(2)}) collective-permute-start(f32[4,32,128]{2,1,0:T(8,128)S(1)} %pad_maximum_fusion.1), channel_id=1, source_target_pairs={{0,32},{4,36},{8,40},{12,44},{16,48},{20,52},{24,56},{28,60},{32,0... | collective-permute-start | bytes 196616 | tf_op jit(solution)/shard_map/ppermute | solution.py:364
  40.5 5.0 %collective-permute-start.7 = (f32[4,32,128]{2,1,0:T(8,128)S(1)}, f32[4,32,128]{2,1,0:T(8,128)S(1)}, u32[]{:S(2)}, u32[]{:S(2)}) collective-permute-start(f32[4,32,128]{2,1,0:T(8,128)S(1)} %pad_maximum_fusion.1), channel_id=1, source_target_pairs={{0,16},{4,20},{8,24},{12,28},{16,0},{20,4},{24,8},{28,12},{32,48},... | collective-permute-start | bytes 196616 | tf_op jit(solution)/shard_map/ppermute | solution.py:364
  45.5 4.4 %copy-start.6 = (f32[2,32,128]{2,1,0:T(8,128)S(1)}, f32[2,32,128]{2,1,0:T(8,128)}, u32[]{:S(2)}) copy-start(f32[2,32,128]{2,1,0:T(8,128)} %constant.16.clone.fine_ref) | copy-start | bytes 98308
  45.5 4.4 %copy-start.7 = (f32[2,32,32]{2,1,0:T(8,128)S(1)}, f32[2,32,32]{2,1,0:T(8,128)}, u32[]{:S(2)}) copy-start(f32[2,32,32]{2,1,0:T(8,128)} %constant.15.clone.coarse_ref) | copy-start | bytes 24580
  45.5 13.0 %collective-permute-start.12 = (f32[4,4,32,128]{3,2,1,0:T(8,128)S(1)}, f32[4,4,32,128]{3,2,1,0:T(8,128)S(1)}, u32[]{:S(2)}, u32[]{:S(2)}) collective-permute-start(f32[4,4,32,128]{3,2,1,0:T(8,128)S(1)} %pad_maximum_fusion.refs_0_), channel_id=1, source_target_pairs={{0,192},{4,196},{8,200},{12,204},{16,208},{20,212},{24,216},{28,22... | collective-permute-start | bytes 786440 | tf_op jit(solution)/shard_map/ppermute | solution.py:364
  46.1 12.4 %collective-permute-start.11 = (f32[4,4,32,128]{3,2,1,0:T(8,128)S(1)}, f32[4,4,32,128]{3,2,1,0:T(8,128)S(1)}, u32[]{:S(2)}, u32[]{:S(2)}) collective-permute-start(f32[4,4,32,128]{3,2,1,0:T(8,128)S(1)} %pad_maximum_fusion.refs_0_), channel_id=1, source_target_pairs={{0,128},{4,132},{8,136},{12,140},{16,144},{20,148},{24,152},{28,15... | collective-permute-start | bytes 786440 | tf_op jit(solution)/shard_map/ppermute | solution.py:364
  48.6 10.5 %collective-permute-start.10 = (f32[4,4,32,128]{3,2,1,0:T(8,128)S(1)}, f32[4,4,32,128]{3,2,1,0:T(8,128)S(1)}, u32[]{:S(2)}, u32[]{:S(2)}) collective-permute-start(f32[4,4,32,128]{3,2,1,0:T(8,128)S(1)} %pad_maximum_fusion.refs_0_), channel_id=1, source_target_pairs={{0,64},{4,68},{8,72},{12,76},{16,80},{20,84},{24,88},{28,92},{32,9... | collective-permute-start | bytes 786440 | tf_op jit(solution)/shard_map/ppermute | solution.py:364

commit v7 on v6

--- a/solution.py
+++ b/solution.py
@@ -240,12 +240,12 @@
     left = lax.broadcasted_iota(jnp.int32, (1, 128), 1) < TILE
     tile = lax.axis_index("samp")
     x, y, z = tile // 16, lax.rem(tile // 4, 4), lax.rem(tile, 4)
-    for kx in range(4):
+    for ky in range(4):
         for pair in range(8):
-            to_y, to_z = pair // 2, pair % 2 * 2
-            a = parts[kx][y ^ to_y, z ^ to_z]
-            b = parts[kx][y ^ to_y, z ^ (to_z + 1)]
-            first = pl.multiple_of(((x ^ kx) * 8 + pair) * 128, 128)
+            to_x, to_z = pair // 2, pair % 2 * 2
+            a = parts[ky][x ^ to_x, z ^ to_z]
+            b = parts[ky][x ^ to_x, z ^ (to_z + 1)]
+            first = pl.multiple_of((to_x * 8 + (y ^ ky) * 2 + to_z // 2) * 128, 128)
             out_ref[:HALF, pl.ds(first, 128)] = jnp.where(left, a, pltpu.roll(b, TILE, 1))
             out_ref[HALF:, pl.ds(first, 128)] = jnp.where(left, pltpu.roll(a, TILE, 1), b)
 
@@ -380,9 +380,9 @@
 
     tiles = jnp.stack(exchange(mine, 1))
     tiles, core_wide, far_wide = lax.optimization_barrier((tiles, core_wide, far_wide))
-    tiles = jnp.stack(exchange(tiles, 4))
+    tiles = jnp.stack(exchange(tiles, 16))
     tiles, generator = lax.optimization_barrier((tiles, generator))
-    new_control = assemble(exchange(tiles, 16))
+    new_control = assemble(exchange(tiles, 4))
 
     state = own_final_state(point_index, generator, row_table, initial_state, control, core_wide, far_wide)
     return (new_control, state[None])

time: 60.6 us -> 60.6 us (level)
  the two profiles are of different devices: /device:TPU:6 before, /device:TPU:8 now
where the time goes in v7:
time: 60.6 us; the launch traced here: 60.4 us
  starting transfers between devices  29.9 us (49%)
  Pallas kernels  18.3 us (30%)
  waiting for transfers between devices  9.09 us (15%)
  between operations  1.39 us (2%)
  other arithmetic  0.96 us (2%)
  local copies, waits for them, and re-layouts  0.72 us (1%)
    ppermute x9, starting transfers between devices, exchange(): lax.ppermute(block, 'samp', [(i, i ^ stride * k) for i in range(64)])  13 us
    all_to_all x1, starting transfers between devices, on_device(): lax.all_to_all(points, 'samp', 0, 0, tiled=True).reshape(SAMPLES, 128)  12 us
    ppermute x9, waiting for transfers between devices, exchange(): lax.ppermute(block, 'samp', [(i, i ^ stride * k) for i in range(64)])  8.57 us
    pallas_call x1, Pallas kernels, own_final_state(): pl.pallas_call(state_kernel, out_shape=jax.ShapeDtypeStruct((rows, width)...  7.95 us
    pallas_call x1, Pallas kernels, tile_gradient(): pl.pallas_call(tile_kernel, out_shape=jax.ShapeDtypeStruct((HALF, 128), j...  6.65 us
    ppermute x1, starting transfers between devices, on_device(): lax.ppermute(to_z, both, ACROSS)  4.61 us
    pallas_call x1, Pallas kernels, strip_edges(): pl.pallas_call(edges_kernel, out_shape=[jax.ShapeDtypeStruct(shape, jnp.f...  2.37 us
    pallas_call x1, Pallas kernels, assemble(): pl.pallas_call(assemble_kernel, out_shape=jax.ShapeDtypeStruct((TILE, SAM...  1.33 us
  transfers between devices with their start and end apart: 14, of which 7 were waited for; matrix products, arithmetic and copies ran while one was open for 2% of the time, Pallas kernels for 28%

profile of v7, /device:TPU:8, one launch (start us, length us, event | category | flops | bytes accessed | tf_op | source)
XLA Modules:
  0.0 60.4 jit_solution(3448027010209623918)
XLA Ops:
  1.3 0.6 %broadcast_in_dim.12 = s32[64,1,128]{2,1,0:T(1,128)} broadcast(s32[]{:T(128)} %bitcast.12), dimensions={} | broadcast | bytes 32772 | tf_op jit(solution)/shard_map/broadcast_in_dim | solution.py:377
  1.9 12.0 %all-to-all-start = ((s32[64,1,128]{2,1,0:T(1,128)}), s32[64,1,128]{2,1,0:T(1,128)S(1)}, u32[]{:S(2)}, u32[]{:S(2)}) async-start(s32[64,1,128]{2,1,0:T(1,128)} %broadcast_in_dim.12), calls=%async_computation | async-start | bytes 65536 | tf_op jit(solution)/shard_map/all_to_all | solution.py:378
  13.9 2.4 %strip_edges.1 = (f32[3,64,128]{2,1,0:T(8,128)}, f32[3,8,128]{2,1,0:T(8,128)}, f32[3,8,128]{2,1,0:T(8,128)}, f32[32,8,128]{2,1,0:T(8,128)}, f32[32,8,128]{2,1,0:T(8,128)}) custom-call(f32[64,4096]{1,0:T(8,128)} %init_ref.1, f32[64,4096]{1,0:T(8,128)} %control_ref.1, f32[64,4096]{1,0:T(8,128)} %refs_2_.1), custom_call_target="tpu_custom_call" | custom-call | tf_op jit(solution)/shard_map/strip_edges/pallas_call | solution.py:115
  16.3 0.1 collective-permute-start
  16.4 4.6 %collective-permute-start.1 = (f32[3,8,128]{2,1,0:T(8,128)}, f32[3,8,128]{2,1,0:T(8,128)S(1)}, u32[]{:S(2)}, u32[]{:S(2)}) collective-permute-start(f32[3,8,128]{2,1,0:T(8,128)} %get-tuple-element.14), channel_id=1, source_target_pairs={{0,11},{1,10},{2,9},{3,8},{4,15},{5,14},{6,13},{7,12},{8,3},{9,2},... | collective-permute-start | bytes 36872 | tf_op jit(solution)/shard_map/ppermute | solution.py:375
  21.0 0.1 collective-permute-start.5
  21.1 0.1 collective-permute-start.6
  21.2 0.0 copy-start.2
  21.2 0.0 copy-start.3
  21.2 0.0 copy-start.4
  21.2 0.0 copy-start.5
  21.2 0.9 %broadcast_maximum_fusion.own_ref = f32[3,64,128]{2,1,0:T(8,128)S(1)} fusion(f32[3,64,128]{2,1,0:T(8,128)} %get-tuple-element.13), kind=kLoop, calls=%fused_computation.2 | loop fusion | flops 24576 | bytes 196608 | tf_op jit(solution)/shard_map/max | solution.py:374
  22.1 0.0 copy-done.2
  22.1 0.1 copy.13
  22.2 0.0 collective-permute-done.core_ref
  22.2 0.4 collective-permute-done.1.z_ref
  22.6 0.1 all-to-all-done
  22.7 0.0 copy-done.3
  22.7 0.0 copy-done.4
  22.7 0.0 copy-done.5
  22.7 0.0 copy-start
  22.7 0.0 copy-start.1
  22.8 6.7 %tile_gradient.1 = f32[32,128]{1,0:T(8,128)S(1)} custom-call(s32[64,128]{1,0:T(8,128)S(1)} %bitcast.13, s32[32,32]{1,0:T(8,128)S(1)} %bitcast.14, f32[2,64,128]{2,1,0:T(8,128)S(1)} %copy-done.4, f32[2,48,128]{2,1,0:T(8,128)S(1)} %copy-done.5, bf16[272,96]{1,0:T(8,128)(2,1)S(1)} %copy-done.3, f32[3,8,128]{2,1,0:T(8,128)S(1)} %collective-permute-done.core_ref, ...), custom_call_target="tpu_custom_call" | custom-call | flops 4000000000 | bytes 20000000 | tf_op jit(solution)/shard_map/tile_gradient/pallas_call | solution.py:226
  29.4 2.5 %collective-permute-start.4 = (f32[32,128]{1,0:T(8,128)S(1)}, f32[32,128]{1,0:T(8,128)S(1)}, u32[]{:S(2)}, u32[]{:S(2)}) collective-permute-start(f32[32,128]{1,0:T(8,128)S(1)} %tile_gradient.1), channel_id=1, source_target_pairs={{0,12},{4,8},{8,4},{12,0},{16,28},{20,24},{24,20},{28,16},{32,44},... | collective-permute-start | bytes 49160 | tf_op jit(solution)/shard_map/ppermute | solution.py:364
  32.0 0.5 collective-permute-start.3
  32.4 1.5 %collective-permute-start.2 = (f32[32,128]{1,0:T(8,128)S(1)}, f32[32,128]{1,0:T(8,128)S(1)}, u32[]{:S(2)}, u32[]{:S(2)}) collective-permute-start(f32[32,128]{1,0:T(8,128)S(1)} %tile_gradient.1), channel_id=1, source_target_pairs={{0,4},{4,0},{8,12},{12,8},{16,20},{20,16},{24,28},{28,24},{32,36},... | collective-permute-start | bytes 49160 | tf_op jit(solution)/shard_map/ppermute | solution.py:364
  33.9 1.2 %collective-permute-done.4 = f32[32,128]{1,0:T(8,128)S(1)} collective-permute-done((f32[32,128]{1,0:T(8,128)S(1)}, f32[32,128]{1,0:T(8,128)S(1)}, u32[]{:S(2)}, u32[]{:S(2)}) %collective-permute-start.4) | collective-permute-done | bytes 16416 | tf_op jit(solution)/shard_map/ppermute | solution.py:364
  35.1 1.5 %collective-permute-done.3 = f32[32,128]{1,0:T(8,128)S(1)} collective-permute-done((f32[32,128]{1,0:T(8,128)S(1)}, f32[32,128]{1,0:T(8,128)S(1)}, u32[]{:S(2)}, u32[]{:S(2)}) %collective-permute-start.3) | collective-permute-done | bytes 16416 | tf_op jit(solution)/shard_map/ppermute | solution.py:364
  36.6 0.0 collective-permute-done.2
  36.6 0.0 collective-permute-done.5.core_ref
  36.6 0.0 collective-permute-done.6.z_ref
  36.6 3.0 %collective-permute-start.9 = (f32[4,32,128]{2,1,0:T(8,128)S(1)}, f32[4,32,128]{2,1,0:T(8,128)S(1)}, u32[]{:S(2)}, u32[]{:S(2)}) collective-permute-start(f32[4,32,128]{2,1,0:T(8,128)S(1)} %pad_maximum_fusion.1), channel_id=1, source_target_pairs={{0,192},{4,196},{8,200},{12,204},{16,208},{20,212},{24,216},{28,22... | collective-permute-start | bytes 196616 | tf_op jit(solution)/shard_map/ppermute | solution.py:364
  39.6 0.6 %collective-permute-start.8 = (f32[4,32,128]{2,1,0:T(8,128)S(1)}, f32[4,32,128]{2,1,0:T(8,128)S(1)}, u32[]{:S(2)}, u32[]{:S(2)}) collective-permute-start(f32[4,32,128]{2,1,0:T(8,128)S(1)} %pad_maximum_fusion.1), channel_id=1, source_target_pairs={{0,128},{4,132},{8,136},{12,140},{16,144},{20,148},{24,152},{28,15... | collective-permute-start | bytes 196616 | tf_op jit(solution)/shard_map/ppermute | solution.py:364
  40.3 0.5 collective-permute-start.7
  40.8 1.4 %collective-permute-done.9 = f32[4,32,128]{2,1,0:T(8,128)S(1)} collective-permute-done((f32[4,32,128]{2,1,0:T(8,128)S(1)}, f32[4,32,128]{2,1,0:T(8,128)S(1)}, u32[]{:S(2)}, u32[]{:S(2)}) %collective-permute-start.9) | collective-permute-done | bytes 65568 | tf_op jit(solution)/shard_map/ppermute | solution.py:364
  42.2 3.2 %collective-permute-done.8 = f32[4,32,128]{2,1,0:T(8,128)S(1)} collective-permute-done((f32[4,32,128]{2,1,0:T(8,128)S(1)}, f32[4,32,128]{2,1,0:T(8,128)S(1)}, u32[]{:S(2)}, u32[]{:S(2)}) %collective-permute-start.8) | collective-permute-done | bytes 65568 | tf_op jit(solution)/shard_map/ppermute | solution.py:364
  45.4 0.0 collective-permute-done.7
  45.4 0.0 copy-start.6
  45.4 0.0 copy-start.7
  45.4 1.8 %collective-permute-start.12 = (f32[4,4,32,128]{3,2,1,0:T(8,128)S(1)}, f32[4,4,32,128]{3,2,1,0:T(8,128)S(1)}, u32[]{:S(2)}, u32[]{:S(2)}) collective-permute-start(f32[4,4,32,128]{3,2,1,0:T(8,128)S(1)} %pad_maximum_fusion.refs_0_), channel_id=1, source_target_pairs={{0,48},{4,52},{8,56},{12,60},{16,32},{20,36},{24,40},{28,44},{32,1... | collective-permute-start | bytes 786440 | tf_op jit(solution)/shard_map/ppermute | solution.py:364
  47.2 1.1 %collective-permute-start.11 = (f32[4,4,32,128]{3,2,1,0:T(8,128)S(1)}, f32[4,4,32,128]{3,2,1,0:T(8,128)S(1)}, u32[]{:S(2)}, u32[]{:S(2)}) collective-permute-start(f32[4,4,32,128]{3,2,1,0:T(8,128)S(1)} %pad_maximum_fusion.refs_0_), channel_id=1, source_target_pairs={{0,32},{4,36},{8,40},{12,44},{16,48},{20,52},{24,56},{28,60},{32,0... | collective-permute-start | bytes 786440 | tf_op jit(solution)/shard_map/ppermute | solution.py:364
  48.3 1.5 %collective-permute-start.10 = (f32[4,4,32,128]{3,2,1,0:T(8,128)S(1)}, f32[4,4,32,128]{3,2,1,0:T(8,128)S(1)}, u32[]{:S(2)}, u32[]{:S(2)}) collective-permute-start(f32[4,4,32,128]{3,2,1,0:T(8,128)S(1)} %pad_maximum_fusion.refs_0_), channel_id=1, source_target_pairs={{0,16},{4,20},{8,24},{12,28},{16,0},{20,4},{24,8},{28,12},{32,48},... | collective-permute-start | bytes 786440 | tf_op jit(solution)/shard_map/ppermute | solution.py:364
  49.8 0.0 copy-done
  49.8 0.0 copy-done.1
  49.8 0.0 copy-done.6
  49.8 0.0 copy-done.7
  49.8 8.0 %own_final_state.1 = f32[64,4096]{1,0:T(8,128)} custom-call(s32[1]{0:T(128)} %copy.14.point_ref, s32[32,32]{1,0:T(8,128)S(1)} %copy-done.2, bf16[272,96]{1,0:T(8,128)(2,1)S(1)} %copy-done.3, f32[2,32,32]{2,1,0:T(8,128)S(1)} %copy-done.7, f32[2,32,128]{2,1,0:T(8,128)S(1)} %copy-done.6, f32[64,4096]{1,0:T(8,128)S(1)} %copy-done, f32[64,4096]{1,0:T(8,128)S(1)} %copy-done.1, ...), custom_call_target="tpu_custom_call" | custom-call | flops 2000000000 | bytes 3500000 | tf_op jit(solution)/shard_map/own_final_state/pallas_call | solution.py:347
  57.8 0.0 collective-permute-done.12.refs_3_
  57.8 0.0 collective-permute-done.11.refs_2_
  57.8 1.3 %collective-permute-done.10.refs_1_ = f32[4,4,32,128]{3,2,1,0:T(8,128)S(1)} collective-permute-done((f32[4,4,32,128]{3,2,1,0:T(8,128)S(1)}, f32[4,4,32,128]{3,2,1,0:T(8,128)S(1)}, u32[]{:S(2)}, u32[]{:S(2)}) %collective-permute-start.10) | collective-permute-done | bytes 262176 | tf_op jit(solution)/shard_map/ppermute | solution.py:364
  59.0 1.3 %assemble.1 = f32[64,4096]{1,0:T(8,128)} custom-call(f32[4,4,32,128]{3,2,1,0:T(8,128)S(1)} %pad_maximum_fusion.refs_0_, f32[4,4,32,128]{3,2,1,0:T(8,128)S(1)} %collective-permute-done.10.refs_1_, f32[4,4,32,128]{3,2,1,0:T(8,128)S(1)} %collective-permute-done.11.refs_2_, f32[4,4,32,128]{3,2,1,0:T(8,128)S(1)} %collective-permute-done.12.refs_3_), custom_call_target="tpu_custom_call" | custom-call | tf_op jit(solution)/shard_map/assemble/pallas_call | solution.py:254
  (2 shorter events, 0.0 us)
Async XLA Ops:
  1.9 20.8 %all-to-all-start = ((s32[64,1,128]{2,1,0:T(1,128)}), s32[64,1,128]{2,1,0:T(1,128)S(1)}, u32[]{:S(2)}, u32[]{:S(2)}) async-start(s32[64,1,128]{2,1,0:T(1,128)} %broadcast_in_dim.12), calls=%async_computation | async-start | bytes 65536 | tf_op jit(solution)/shard_map/all_to_all | solution.py:378
  16.3 5.9 %collective-permute-start = (f32[3,8,128]{2,1,0:T(8,128)}, f32[3,8,128]{2,1,0:T(8,128)S(1)}, u32[]{:S(2)}, u32[]{:S(2)}) collective-permute-start(f32[3,8,128]{2,1,0:T(8,128)} %get-tuple-element.12), channel_id=1, source_target_pairs={{0,1},{1,0},{2,3},{3,2},{4,5},{5,4},{6,7},{7,6},{8,9},{9,8},{10,11... | collective-permute-start | bytes 36872 | tf_op jit(solution)/shard_map/ppermute | solution.py:375
  16.4 6.2 %collective-permute-start.1 = (f32[3,8,128]{2,1,0:T(8,128)}, f32[3,8,128]{2,1,0:T(8,128)S(1)}, u32[]{:S(2)}, u32[]{:S(2)}) collective-permute-start(f32[3,8,128]{2,1,0:T(8,128)} %get-tuple-element.14), channel_id=1, source_target_pairs={{0,11},{1,10},{2,9},{3,8},{4,15},{5,14},{6,13},{7,12},{8,3},{9,2},... | collective-permute-start | bytes 36872 | tf_op jit(solution)/shard_map/ppermute | solution.py:375
  21.0 15.6 %collective-permute-start.5 = (f32[32,8,128]{2,1,0:T(8,128)}, f32[32,8,128]{2,1,0:T(8,128)S(1)}, u32[]{:S(2)}, u32[]{:S(2)}) collective-permute-start(f32[32,8,128]{2,1,0:T(8,128)} %get-tuple-element.15), channel_id=1, source_target_pairs={{0,1},{1,0},{2,3},{3,2},{4,5},{5,4},{6,7},{7,6},{8,9},{9,8},{10,11... | collective-permute-start | bytes 393224 | tf_op jit(solution)/shard_map/ppermute | solution.py:376
  21.1 15.5 %collective-permute-start.6 = (f32[32,8,128]{2,1,0:T(8,128)}, f32[32,8,128]{2,1,0:T(8,128)S(1)}, u32[]{:S(2)}, u32[]{:S(2)}) collective-permute-start(f32[32,8,128]{2,1,0:T(8,128)} %get-tuple-element.16), channel_id=1, source_target_pairs={{0,11},{1,10},{2,9},{3,8},{4,15},{5,14},{6,13},{7,12},{8,3},{9,2},... | collective-permute-start | bytes 393224 | tf_op jit(solution)/shard_map/ppermute | solution.py:376
  21.2 1.0 %copy-start.2 = (s32[32,32]{1,0:T(8,128)S(1)}, s32[32,32]{1,0:T(8,128)}, u32[]{:S(2)}) copy-start(s32[32,32]{1,0:T(8,128)} %gen_ref) | copy-start | bytes 12292
  21.2 1.6 %copy-start.3 = (bf16[272,96]{1,0:T(8,128)(2,1)S(1)}, bf16[272,96]{1,0:T(8,128)(2,1)}, u32[]{:S(2)}) copy-start(bf16[272,96]{1,0:T(8,128)(2,1)} %constant.14.clone.row_ref) | copy-start | bytes 156676
  21.2 1.6 %copy-start.4 = (f32[2,64,128]{2,1,0:T(8,128)S(1)}, f32[2,64,128]{2,1,0:T(8,128)}, u32[]{:S(2)}) copy-start(f32[2,64,128]{2,1,0:T(8,128)} %constant.12.clone.coarse_ref) | copy-start | bytes 196612
  21.2 1.6 %copy-start.5 = (f32[2,48,128]{2,1,0:T(8,128)S(1)}, f32[2,48,128]{2,1,0:T(8,128)}, u32[]{:S(2)}) copy-start(f32[2,48,128]{2,1,0:T(8,128)} %constant.13.clone.fine_ref) | copy-start | bytes 147460
  22.7 27.1 %copy-start = (f32[64,4096]{1,0:T(8,128)S(1)}, f32[64,4096]{1,0:T(8,128)}, u32[]{:S(2)}) copy-start(f32[64,4096]{1,0:T(8,128)} %init_ref.1) | copy-start | bytes 3145732
  22.7 27.1 %copy-start.1 = (f32[64,4096]{1,0:T(8,128)S(1)}, f32[64,4096]{1,0:T(8,128)}, u32[]{:S(2)}) copy-start(f32[64,4096]{1,0:T(8,128)} %control_ref.1) | copy-start | bytes 3145732
  29.4 5.6 %collective-permute-start.4 = (f32[32,128]{1,0:T(8,128)S(1)}, f32[32,128]{1,0:T(8,128)S(1)}, u32[]{:S(2)}, u32[]{:S(2)}) collective-permute-start(f32[32,128]{1,0:T(8,128)S(1)} %tile_gradient.1), channel_id=1, source_target_pairs={{0,12},{4,8},{8,4},{12,0},{16,28},{20,24},{24,20},{28,16},{32,44},... | collective-permute-start | bytes 49160 | tf_op jit(solution)/shard_map/ppermute | solution.py:364
  32.0 4.6 %collective-permute-start.3 = (f32[32,128]{1,0:T(8,128)S(1)}, f32[32,128]{1,0:T(8,128)S(1)}, u32[]{:S(2)}, u32[]{:S(2)}) collective-permute-start(f32[32,128]{1,0:T(8,128)S(1)} %tile_gradient.1), channel_id=1, source_target_pairs={{0,8},{4,12},{8,0},{12,4},{16,24},{20,28},{24,16},{28,20},{32,40},... | collective-permute-start | bytes 49160 | tf_op jit(solution)/shard_map/ppermute | solution.py:364
  32.4 4.2 %collective-permute-start.2 = (f32[32,128]{1,0:T(8,128)S(1)}, f32[32,128]{1,0:T(8,128)S(1)}, u32[]{:S(2)}, u32[]{:S(2)}) collective-permute-start(f32[32,128]{1,0:T(8,128)S(1)} %tile_gradient.1), channel_id=1, source_target_pairs={{0,4},{4,0},{8,12},{12,8},{16,20},{20,16},{24,28},{28,24},{32,36},... | collective-permute-start | bytes 49160 | tf_op jit(solution)/shard_map/ppermute | solution.py:364
  36.6 5.6 %collective-permute-start.9 = (f32[4,32,128]{2,1,0:T(8,128)S(1)}, f32[4,32,128]{2,1,0:T(8,128)S(1)}, u32[]{:S(2)}, u32[]{:S(2)}) collective-permute-start(f32[4,32,128]{2,1,0:T(8,128)S(1)} %pad_maximum_fusion.1), channel_id=1, source_target_pairs={{0,192},{4,196},{8,200},{12,204},{16,208},{20,212},{24,216},{28,22... | collective-permute-start | bytes 196616 | tf_op jit(solution)/shard_map/ppermute | solution.py:364
  39.6 5.8 %collective-permute-start.8 = (f32[4,32,128]{2,1,0:T(8,128)S(1)}, f32[4,32,128]{2,1,0:T(8,128)S(1)}, u32[]{:S(2)}, u32[]{:S(2)}) collective-permute-start(f32[4,32,128]{2,1,0:T(8,128)S(1)} %pad_maximum_fusion.1), channel_id=1, source_target_pairs={{0,128},{4,132},{8,136},{12,140},{16,144},{20,148},{24,152},{28,15... | collective-permute-start | bytes 196616 | tf_op jit(solution)/shard_map/ppermute | solution.py:364
  40.3 5.1 %collective-permute-start.7 = (f32[4,32,128]{2,1,0:T(8,128)S(1)}, f32[4,32,128]{2,1,0:T(8,128)S(1)}, u32[]{:S(2)}, u32[]{:S(2)}) collective-permute-start(f32[4,32,128]{2,1,0:T(8,128)S(1)} %pad_maximum_fusion.1), channel_id=1, source_target_pairs={{0,64},{4,68},{8,72},{12,76},{16,80},{20,84},{24,88},{28,92},{32,9... | collective-permute-start | bytes 196616 | tf_op jit(solution)/shard_map/ppermute | solution.py:364
  45.4 4.4 %copy-start.6 = (f32[2,32,128]{2,1,0:T(8,128)S(1)}, f32[2,32,128]{2,1,0:T(8,128)}, u32[]{:S(2)}) copy-start(f32[2,32,128]{2,1,0:T(8,128)} %constant.16.clone.fine_ref) | copy-start | bytes 98308
  45.4 4.4 %copy-start.7 = (f32[2,32,32]{2,1,0:T(8,128)S(1)}, f32[2,32,32]{2,1,0:T(8,128)}, u32[]{:S(2)}) copy-start(f32[2,32,32]{2,1,0:T(8,128)} %constant.15.clone.coarse_ref) | copy-start | bytes 24580
  45.4 12.3 %collective-permute-start.12 = (f32[4,4,32,128]{3,2,1,0:T(8,128)S(1)}, f32[4,4,32,128]{3,2,1,0:T(8,128)S(1)}, u32[]{:S(2)}, u32[]{:S(2)}) collective-permute-start(f32[4,4,32,128]{3,2,1,0:T(8,128)S(1)} %pad_maximum_fusion.refs_0_), channel_id=1, source_target_pairs={{0,48},{4,52},{8,56},{12,60},{16,32},{20,36},{24,40},{28,44},{32,1... | collective-permute-start | bytes 786440 | tf_op jit(solution)/shard_map/ppermute | solution.py:364
  47.2 10.6 %collective-permute-start.11 = (f32[4,4,32,128]{3,2,1,0:T(8,128)S(1)}, f32[4,4,32,128]{3,2,1,0:T(8,128)S(1)}, u32[]{:S(2)}, u32[]{:S(2)}) collective-permute-start(f32[4,4,32,128]{3,2,1,0:T(8,128)S(1)} %pad_maximum_fusion.refs_0_), channel_id=1, source_target_pairs={{0,32},{4,36},{8,40},{12,44},{16,48},{20,52},{24,56},{28,60},{32,0... | collective-permute-start | bytes 786440 | tf_op jit(solution)/shard_map/ppermute | solution.py:364
  48.3 10.7 %collective-permute-start.10 = (f32[4,4,32,128]{3,2,1,0:T(8,128)S(1)}, f32[4,4,32,128]{3,2,1,0:T(8,128)S(1)}, u32[]{:S(2)}, u32[]{:S(2)}) collective-permute-start(f32[4,4,32,128]{3,2,1,0:T(8,128)S(1)} %pad_maximum_fusion.refs_0_), channel_id=1, source_target_pairs={{0,16},{4,20},{8,24},{12,28},{16,0},{20,4},{24,8},{28,12},{32,48},... | collective-permute-start | bytes 786440 | tf_op jit(solution)/shard_map/ppermute | solution.py:364
